TPU v7x, 1024 devices: a whole 8x8x8 slice. The times are simulated.
1024 devices in a mesh: seq: 16 (over x_hi, z), exp: 4 (over x_lo), ffn: 16 (over y, core).
Axes of the slice: x: 8 (x_hi: 2, x_lo: 4; x = x_hi * 4 + x_lo), y: 8, z: 8, core: 2. Of those that a mesh axis runs over, the one named last changes fastest.
Arguments:
- tokens: bfloat16 [4096, 3072], P(('seq', 'exp')), may hold values from -6 to 6
- cotangent: bfloat16 [4096, 3072], P(('seq', 'exp')), may hold values from -1.5 to 1.5
- routes: int32 [4096, 2], P(('seq', 'exp')), may hold values from 0 to 3, all different within a row; in each aligned block of 64 rows (0 to 63, 64 to 127, ...) at most 36 rows name the same one
- router_gates: float32 [4096, 2], P(('seq', 'exp')), may hold values from 0.1 to 1
- gate_weight: bfloat16 [4, 3072, 5376], P('exp', None, 'ffn'), may hold values from -0.109375 to 0.109375
- up_weight: bfloat16 [4, 3072, 5376], P('exp', None, 'ffn'), may hold values from -0.109375 to 0.109375
- down_weight: bfloat16 [4, 5376, 3072], P('exp', 'ffn'), may hold values from -0.078125 to 0.078125
Outputs:
- layer_out: bfloat16 [4096, 3072], P(('seq', 'exp'), 'ffn')
- token_grad: bfloat16 [4096, 3072], P(('seq', 'exp'), 'ffn')
- gate_weight_grad: float32 [4, 3072, 5376], P('exp', 'seq', 'ffn')
- up_weight_grad: float32 [4, 3072, 5376], P('exp', 'seq', 'ffn')
- down_weight_grad: float32 [4, 5376, 3072], P('exp', 'ffn', 'seq')
Inputs may be any that keep to these rules, and one draw needn't show every extreme that they name: `routes`: among the 64 rows of one device no expert is named by more than 36 rows, and some device has an expert named by exactly 36 of its rows.
All inputs are finite; a program needn't handle non-finite values.
Results may differ from a plain program's by a relative error of at most 0.024.
Values may be sent and summed in bfloat16 or wider, within the bound.
No kernel may reach another device: no remote copies, remote signals or barrier semaphores. Data moves between devices by JAX's collectives and lax.ppermute only.
A program may use at most 64 MiB of HBM per device.

v0:
```python
import jax
import jax.numpy as jnp
from jax import lax
from jax.sharding import PartitionSpec as P

CAP = 36


def on_device(tokens, cotangent, routes, router_gates, gate_weight, up_weight, down_weight):
    tok_count = tokens.shape[0]
    width = tokens.shape[1]
    top_count = routes.shape[1]
    local_experts = gate_weight.shape[0]
    exp_devices = lax.axis_size("exp")
    all_experts = local_experts * exp_devices
    capacity = CAP
    pairs = tok_count * top_count
    flat_ids = routes.reshape(pairs)
    expert_range = jnp.arange(all_experts, dtype=jnp.int32)
    onehot = (flat_ids[:, None] == expert_range[None, :]).astype(jnp.int32)
    earlier = jnp.cumsum(onehot, axis=0) - onehot
    slot_index = jnp.sum(earlier * onehot, axis=1)
    slot_range = jnp.arange(capacity, dtype=jnp.int32)
    chosen = (onehot[:, :, None] == 1) & (slot_index[:, None, None] == slot_range[None, None, :])
    chosen = chosen.reshape(tok_count, top_count, all_experts * capacity).astype(jnp.float32)
    token_pick = jnp.sum(chosen, axis=1)
    combine = jnp.sum(router_gates[:, :, None] * chosen, axis=1)
    scaled = (router_gates[:, :, None] * cotangent.astype(jnp.float32)[:, None, :]).astype(
        jnp.bfloat16
    )
    scaled = scaled.reshape(pairs, width)
    send_x = jnp.dot(token_pick.T.astype(jnp.bfloat16), tokens, preferred_element_type=jnp.float32)
    send_dy = jnp.dot(
        chosen.reshape(pairs, -1).T.astype(jnp.bfloat16), scaled, preferred_element_type=jnp.float32
    )
    shaped = (exp_devices, local_experts, capacity, width)
    rows_x, rows_dy = (
        lax.all_to_all(
            send_x.astype(jnp.bfloat16).reshape(shaped),
            "exp",
            split_axis=0,
            concat_axis=0,
            tiled=True,
        ),
        lax.all_to_all(
            send_dy.astype(jnp.bfloat16).reshape(shaped),
            "exp",
            split_axis=0,
            concat_axis=0,
            tiled=True,
        ),
    )
    gate_act = jnp.einsum("secd,edf->secf", rows_x, gate_weight, preferred_element_type=jnp.float32)
    up_act = jnp.einsum("secd,edf->secf", rows_x, up_weight, preferred_element_type=jnp.float32)
    sigmoid_gate = jax.nn.sigmoid(gate_act)
    hidden = (gate_act * sigmoid_gate * up_act).astype(jnp.bfloat16)
    part_out = jnp.einsum("secf,efd->secd", hidden, down_weight, preferred_element_type=jnp.float32)
    hidden_grad = jnp.einsum(
        "secd,efd->secf", rows_dy, down_weight, preferred_element_type=jnp.float32
    )
    gate_grad = (
        hidden_grad * up_act * sigmoid_gate * (1.0 + gate_act * (1.0 - sigmoid_gate))
    ).astype(jnp.bfloat16)
    up_grad = (hidden_grad * gate_act * sigmoid_gate).astype(jnp.bfloat16)
    part_back = jnp.einsum(
        "secf,edf->secd", gate_grad, gate_weight, preferred_element_type=jnp.float32
    )
    part_back = part_back + jnp.einsum(
        "secf,edf->secd", up_grad, up_weight, preferred_element_type=jnp.float32
    )
    own_out, own_back = (
        lax.psum_scatter(
            part_out.astype(jnp.bfloat16), "ffn", scatter_dimension=3, tiled=True
        ).astype(jnp.float32),
        lax.psum_scatter(
            part_back.astype(jnp.bfloat16), "ffn", scatter_dimension=3, tiled=True
        ).astype(jnp.float32),
    )
    back_out, back_grad = (
        lax.all_to_all(
            own_out.astype(jnp.bfloat16), "exp", split_axis=0, concat_axis=0, tiled=True
        ),
        lax.all_to_all(
            own_back.astype(jnp.bfloat16), "exp", split_axis=0, concat_axis=0, tiled=True
        ),
    )
    local_width = back_out.shape[3]
    layer_out = jnp.dot(
        combine,
        back_out.reshape(-1, local_width).astype(jnp.float32),
        precision=lax.Precision.HIGHEST,
    )
    token_grad = jnp.dot(
        token_pick.astype(jnp.bfloat16),
        back_grad.reshape(-1, local_width),
        preferred_element_type=jnp.float32,
    )
    cols_x, cols_dy = (
        lax.all_to_all(rows_x, "seq", split_axis=3, concat_axis=0, tiled=True),
        lax.all_to_all(rows_dy, "seq", split_axis=3, concat_axis=0, tiled=True),
    )
    narrow = cols_x.shape[3]
    ff_local = gate_weight.shape[2]
    pieces = (
        lax.all_gather(gate_grad, "seq", axis=0, tiled=True),
        lax.all_gather(up_grad, "seq", axis=0, tiled=True),
        lax.all_gather(hidden, "seq", axis=0, tiled=True),
    )
    count = pieces[0].shape[0]
    shards = count // exp_devices
    piece_x = cols_x
    piece_dy = cols_dy
    piece_x = piece_x.reshape(shards, exp_devices, local_experts, capacity, narrow)
    piece_dy = piece_dy.reshape(shards, exp_devices, local_experts, capacity, narrow)
    split_shape = (shards, exp_devices, local_experts, capacity, ff_local)
    part_gate = jnp.einsum(
        "snecd,snecf->sedf",
        piece_x,
        pieces[0].reshape(split_shape),
        preferred_element_type=jnp.float32,
    )
    part_up = jnp.einsum(
        "snecd,snecf->sedf",
        piece_x,
        pieces[1].reshape(split_shape),
        preferred_element_type=jnp.float32,
    )
    part_down = jnp.einsum(
        "snecd,snecf->sedf",
        piece_dy,
        pieces[2].reshape(split_shape),
        preferred_element_type=jnp.float32,
    )
    parts = lax.optimization_barrier(
        (
            part_gate.astype(jnp.bfloat16),
            part_up.astype(jnp.bfloat16),
            part_down.astype(jnp.bfloat16),
        )
    )
    grad_gate = jnp.sum(parts[0].astype(jnp.float32), axis=0)
    grad_up = jnp.sum(parts[1].astype(jnp.float32), axis=0)
    down_turned = jnp.sum(parts[2].astype(jnp.float32), axis=0)
    grad_down = jnp.swapaxes(down_turned, 1, 2)
    return (
        layer_out.astype(jnp.bfloat16),
        token_grad.astype(jnp.bfloat16),
        grad_gate,
        grad_up,
        grad_down,
    )


def solution(mesh):
    placed = (
        P(("seq", "exp"), None),
        P(("seq", "exp"), None),
        P(("seq", "exp"), None),
        P(("seq", "exp"), None),
        P("exp", None, "ffn"),
        P("exp", None, "ffn"),
        P("exp", "ffn", None),
    )
    return jax.shard_map(
        on_device,
        mesh=mesh,
        in_specs=placed,
        out_specs=(
            P(("seq", "exp"), "ffn"),
            P(("seq", "exp"), "ffn"),
            P("exp", "seq", "ffn"),
            P("exp", "seq", "ffn"),
            P("exp", "ffn", "seq"),
        ),
        check_vma=False,
    )
```

profile of v0, /device:TPU:14, one launch (start us, length us, event | category | flops | bytes accessed | tf_op | source)
XLA Modules:
  0.0 474.6 jit_solution(15323432545933071212)
XLA Ops:
  8.0 0.9 copy.26
  8.9 0.1 eq.48
  9.2 0.2 reduce_window_sum.11
  9.3 0.2 select_reduce_fusion.1
  9.7 0.2 copy.28
  9.8 0.2 and.22
  10.0 0.8 copy.29
  10.8 0.9 convert_reduce_fusion.3
  11.7 0.6 copy-done.9
  12.3 1.4 convolution_convert_fusion.2
  13.8 1.2 reshape.157
  14.9 6.7 %all-to-all-start = ((bf16[4,1,36,3072]{3,2,1,0:T(8,128)(2,1)}), bf16[4,1,36,3072]{3,2,1,0:T(8,128)(2,1)S(1)}, u32[]{:S(2)}, u32[]{:S(2)}) async-start(bf16[4,1,36,3072]{3,2,1,0:T(8,128)(2,1)} %bitcast.162), calls=%async_computation | async-start | bytes 1966080 | tf_op jit(solution)/shard_map/all_to_all | solution.py:38
  21.6 0.1 mul.58
  21.7 1.5 mul.60
  23.3 3.2 mul.61
  26.5 2.8 convolution_convert_fusion.1
  29.2 2.3 reshape.164
  31.5 12.3 %all-to-all-done = bf16[4,1,36,3072]{3,2,1,0:T(8,128)(2,1)S(1)} async-done(((bf16[4,1,36,3072]{3,2,1,0:T(8,128)(2,1)}), bf16[4,1,36,3072]{3,2,1,0:T(8,128)(2,1)S(1)}, u32[]{:S(2)}, u32[]{:S(2)}) %all-to-all-start) | async-done | bytes 884768 | tf_op jit(solution)/shard_map/all_to_all | solution.py:38
  43.8 6.6 %all-to-all-start.2 = ((bf16[4,1,36,3072]{3,2,1,0:T(8,128)(2,1)}), bf16[4,1,36,3072]{3,2,1,0:T(8,128)(2,1)}, u32[]{:S(2)}, u32[]{:S(2)}) async-start(bf16[4,1,36,3072]{3,2,1,0:T(8,128)(2,1)} %bitcast.163), calls=%async_computation.2 | async-start | bytes 1966080 | tf_op jit(solution)/shard_map/all_to_all | solution.py:45
  50.4 3.3 fusion.22
  53.7 1.6 fusion.25
  55.3 16.7 %all-to-all-done.2 = bf16[4,1,36,3072]{3,2,1,0:T(8,128)(2,1)} async-done(((bf16[4,1,36,3072]{3,2,1,0:T(8,128)(2,1)}), bf16[4,1,36,3072]{3,2,1,0:T(8,128)(2,1)}, u32[]{:S(2)}, u32[]{:S(2)}) %all-to-all-start.2) | async-done | bytes 884768 | tf_op jit(solution)/shard_map/all_to_all | solution.py:45
  72.0 2.3 multiply_convert_fusion.2
  74.3 1.7 fusion.1
  76.0 5.1 %copy.51 = bf16[4,1,36,3072]{2,0,1,3:T(4,128)(2,1)} copy(bf16[4,1,36,3072]{3,2,0,1:T(8,128)(2,1)} %fusion.1) | data formatting | bytes 1769472
  81.1 5.5 %reshape.180 = bf16[3072,144]{1,0:T(8,128)(2,1)} reshape(bf16[3072,1,4,36]{3,2,1,0:T(4,128)(2,1)} %bitcast.156) | data formatting | bytes 1769472
  86.6 2.4 fusion.12
  89.1 1.7 fusion.2
  90.7 5.1 %copy.53 = bf16[4,1,36,3072]{2,0,1,3:T(4,128)(2,1)} copy(bf16[4,1,36,3072]{3,2,0,1:T(8,128)(2,1)} %fusion.2) | data formatting | bytes 1769472
  95.8 5.5 %reshape.182 = bf16[3072,144]{1,0:T(8,128)(2,1)} reshape(bf16[3072,1,4,36]{3,2,1,0:T(4,128)(2,1)} %bitcast.157) | data formatting | bytes 1769472
  101.4 0.5 all-gather.4.cloned.1.call-update
  101.9 0.2 all-gather.6.cloned.1.call-start
  102.1 0.4 all-gather.6.cloned.1.call-update
  102.5 3.7 copy.35
  106.2 10.0 %reshape.184 = bf16[16,2,13824]{2,1,0:T(2,128)(2,1)} reshape(bf16[3072,1,4,36]{3,2,1,0:T(4,128)(2,1)} %bitcast.158) | data formatting | bytes 1769472
  116.2 22.1 %all-to-all-start.4 = ((bf16[16,2,13824]{2,1,0:T(2,128)(2,1)}), bf16[16,2,13824]{2,1,0:T(2,128)(2,1)S(1)}, u32[]{:S(2)}, u32[]{:S(2)}) async-start(bf16[16,2,13824]{2,1,0:T(2,128)(2,1)} %reshape.184), calls=%async_computation.4 | async-start | bytes 1769472 | tf_op jit(solution)/shard_map/all_to_all | solution.py:99
  138.3 5.1 %copy.40 = bf16[4,1,36,3072]{2,0,1,3:T(4,128)(2,1)} copy(bf16[4,1,36,3072]{3,2,1,0:T(8,128)(2,1)} %all-to-all-done.2) | data formatting | bytes 1769472 | tf_op jit(solution)/shard_map/all_to_all | solution.py:45
  143.4 10.0 %reshape.186 = bf16[16,2,13824]{2,1,0:T(2,128)(2,1)} reshape(bf16[3072,1,4,36]{3,2,1,0:T(4,128)(2,1)} %bitcast.159) | data formatting | bytes 1769472
  153.4 9.7 %all-to-all-done.4 = bf16[16,2,13824]{2,1,0:T(2,128)(2,1)S(1)} async-done(((bf16[16,2,13824]{2,1,0:T(2,128)(2,1)}), bf16[16,2,13824]{2,1,0:T(2,128)(2,1)S(1)}, u32[]{:S(2)}, u32[]{:S(2)}) %all-to-all-start.4) | async-done | bytes 884768 | tf_op jit(solution)/shard_map/all_to_all | solution.py:99
  163.1 9.7 %all-to-all-start.5 = ((bf16[16,2,13824]{2,1,0:T(2,128)(2,1)}), bf16[16,2,13824]{2,1,0:T(2,128)(2,1)}, u32[]{:S(2)}, u32[]{:S(2)}) async-start(bf16[16,2,13824]{2,1,0:T(2,128)(2,1)} %reshape.186), calls=%async_computation.5 | async-start | bytes 1769472 | tf_op jit(solution)/shard_map/all_to_all | solution.py:100
  172.8 0.5 all-gather.8.cloned.1.call-update
  173.3 1.0 reshape.181
  174.4 0.8 copy.52
  175.2 18.7 %all-to-all-done.5 = bf16[16,2,13824]{2,1,0:T(2,128)(2,1)} async-done(((bf16[16,2,13824]{2,1,0:T(2,128)(2,1)}), bf16[16,2,13824]{2,1,0:T(2,128)(2,1)}, u32[]{:S(2)}, u32[]{:S(2)}) %all-to-all-start.5) | async-done | bytes 884768 | tf_op jit(solution)/shard_map/all_to_all | solution.py:100
  193.9 8.2 %all-to-all-start.1 = ((bf16[4,1,36,192]{3,2,1,0:T(8,128)(2,1)}), bf16[4,1,36,192]{3,2,1,0:T(8,128)(2,1)S(1)}, u32[]{:S(2)}, u32[]{:S(2)}) async-start(bf16[4,1,36,192]{3,2,1,0:T(8,128)(2,1)} %bitcast.20), calls=%async_computation.1 | async-start | bytes 163840 | tf_op jit(solution)/shard_map/all_to_all | solution.py:80
  202.1 27.6 %reduce-scatter.9.cloned.1.call-done = bf16[192,144]{1,0:T(8,128)(2,1)} async-done(((bf16[3072,144]{1,0:T(8,128)(2,1)}), bf16[192,144]{1,0:T(8,128)(2,1)}) %reduce-scatter.9.cloned.1.call-update) | async-done | bytes 55312
  229.7 1.0 reshape.183
  230.7 0.8 copy.54
  231.5 6.6 %all-to-all-start.3 = ((bf16[4,1,36,192]{3,2,1,0:T(8,128)(2,1)}), bf16[4,1,36,192]{3,2,1,0:T(8,128)(2,1)S(1)}, u32[]{:S(2)}, u32[]{:S(2)}) async-start(bf16[4,1,36,192]{3,2,1,0:T(8,128)(2,1)} %bitcast.35), calls=%async_computation.3 | async-start | bytes 163840 | tf_op jit(solution)/shard_map/all_to_all | solution.py:83
  238.2 10.1 %reshape.185 = bf16[3072,1,4,36]{3,2,1,0:T(4,128)(2,1)} reshape(bf16[16,2,13824]{2,1,0:T(2,128)(2,1)S(1)} %all-to-all-done.4) | data formatting | bytes 1769472
  248.3 6.2 %copy.37 = bf16[4,1,36,16,192]{4,2,0,3,1:T(8,128)(2,1)} copy(bf16[4,1,36,16,192]{2,0,4,3,1:T(4,128)(2,1)} %bitcast.160) | data formatting | bytes 1769472 | tf_op jit(solution)/shard_map/all_to_all | solution.py:99
  254.4 11.6 %reshape.187 = bf16[3072,1,4,36]{3,2,1,0:T(4,128)(2,1)} reshape(bf16[16,2,13824]{2,1,0:T(2,128)(2,1)} %all-to-all-done.5) | data formatting | bytes 1769472
  266.1 5.6 %copy.42 = bf16[4,1,36,16,192]{4,2,0,3,1:T(8,128)(2,1)S(1)} copy(bf16[4,1,36,16,192]{2,0,4,3,1:T(4,128)(2,1)} %bitcast.161) | data formatting | bytes 1769472 | tf_op jit(solution)/shard_map/all_to_all | solution.py:100
  271.6 0.7 reshape.163
  272.3 1.5 convolution_convert_fusion.3
  273.8 1.7 convolution_convert_fusion.4
  275.6 4.4 fusion.3
  280.0 71.6 %all-gather.6.cloned.1.call-done = bf16[64,1,36,336]{3,2,1,0:T(8,128)(2,1)} async-done(((bf16[4,1,36,336]{3,2,1,0:T(8,128)(2,1)}), bf16[64,1,36,336]{3,2,1,0:T(8,128)(2,1)}) %all-gather.6.cloned.1.call-update) | async-done | bytes 1548304 | tf_op jit(solution)/shard_map/all_gather | solution.py:106
  351.6 4.4 fusion.4
  356.0 105.0 %all-gather.8.cloned.1.call-done = bf16[64,1,36,336]{3,2,1,0:T(8,128)(2,1)} async-done(((bf16[4,1,36,336]{3,2,1,0:T(8,128)(2,1)}), bf16[64,1,36,336]{3,2,1,0:T(8,128)(2,1)}) %all-gather.8.cloned.1.call-update) | async-done | bytes 1548304 | tf_op jit(solution)/shard_map/all_gather | solution.py:107
  461.0 2.7 fusion.5
  463.7 1.1 convert_reduce_fusion.2
  464.8 0.7 copy-done.4
  465.5 1.5 convert_reduce_fusion
  (34 shorter events, 0.5 us)
Async XLA Ops:
  8.0 64.0 %copy-start = (bf16[1,336,3072]{2,1,0:T(8,128)(2,1)S(1)}, bf16[1,336,3072]{2,1,0:T(8,128)(2,1)}, u32[]{:S(2)}) copy-start(bf16[1,336,3072]{2,1,0:T(8,128)(2,1)} %param.13) | copy-start | bytes 6193156
  11.7 0.6 copy-start.9
  13.7 8.0 %copy-start.8 = (bf16[64,3072]{1,0:T(8,128)(2,1)S(1)}, bf16[64,3072]{1,0:T(8,128)(2,1)}, u32[]{:S(2)}) copy-start(bf16[64,3072]{1,0:T(8,128)(2,1)} %param.8) | copy-start | bytes 1179652
  14.9 28.9 %all-to-all-start = ((bf16[4,1,36,3072]{3,2,1,0:T(8,128)(2,1)}), bf16[4,1,36,3072]{3,2,1,0:T(8,128)(2,1)S(1)}, u32[]{:S(2)}, u32[]{:S(2)}) async-start(bf16[4,1,36,3072]{3,2,1,0:T(8,128)(2,1)} %bitcast.162), calls=%async_computation | async-start | bytes 1966080 | tf_op jit(solution)/shard_map/all_to_all | solution.py:38
  43.8 28.2 %all-to-all-start.2 = ((bf16[4,1,36,3072]{3,2,1,0:T(8,128)(2,1)}), bf16[4,1,36,3072]{3,2,1,0:T(8,128)(2,1)}, u32[]{:S(2)}, u32[]{:S(2)}) async-start(bf16[4,1,36,3072]{3,2,1,0:T(8,128)(2,1)} %bitcast.163), calls=%async_computation.2 | async-start | bytes 1966080 | tf_op jit(solution)/shard_map/all_to_all | solution.py:45
  50.4 123.0 %reduce-scatter.7.cloned.1.call-start = ((), (), s32[]{:S(2)}) async-start(), calls=%async_computation.11 | async-start | bytes 1671168
  50.4 3.3 copy-start.1
  74.3 6.8 %copy-start.6 = (bf16[4,1,36,336]{3,2,0,1:T(8,128)(2,1)}, bf16[4,1,36,336]{3,2,0,1:T(8,128)(2,1)S(1)}, u32[]{:S(2)}) copy-start(bf16[4,1,36,336]{3,2,0,1:T(8,128)(2,1)S(1)} %get-tuple-element.15) | copy-start | bytes 290308
  74.3 12.3 %copy-start.5 = (bf16[4,1,36,336]{3,2,0,1:T(8,128)(2,1)}, bf16[4,1,36,336]{3,2,0,1:T(8,128)(2,1)S(1)}, u32[]{:S(2)}) copy-start(bf16[4,1,36,336]{3,2,0,1:T(8,128)(2,1)S(1)} %get-tuple-element.14) | copy-start | bytes 290308
  74.3 14.8 %copy-start.7 = (bf16[4,1,36,336]{3,2,0,1:T(8,128)(2,1)}, bf16[4,1,36,336]{3,2,0,1:T(8,128)(2,1)S(1)}, u32[]{:S(2)}) copy-start(bf16[4,1,36,336]{3,2,0,1:T(8,128)(2,1)S(1)} %get-tuple-element.13) | copy-start | bytes 290308
  86.6 143.1 %reduce-scatter.9.cloned.1.call-start = ((), (), s32[]{:S(2)}) async-start(), calls=%async_computation.12 | async-start | bytes 1671168
  86.6 2.4 copy-start.2
  101.3 174.2 %all-gather.4.cloned.1.call-start = ((), (), s32[]{:S(2)}) async-start(), calls=%async_computation.8 | async-start | bytes 2088960 | tf_op jit(solution)/shard_map/all_gather | solution.py:105
  101.9 249.7 %all-gather.6.cloned.1.call-start = ((), (), s32[]{:S(2)}) async-start(), calls=%async_computation.9 | async-start | bytes 2088960 | tf_op jit(solution)/shard_map/all_gather | solution.py:106
  116.2 46.9 %all-to-all-start.4 = ((bf16[16,2,13824]{2,1,0:T(2,128)(2,1)}), bf16[16,2,13824]{2,1,0:T(2,128)(2,1)S(1)}, u32[]{:S(2)}, u32[]{:S(2)}) async-start(bf16[16,2,13824]{2,1,0:T(2,128)(2,1)} %reshape.184), calls=%async_computation.4 | async-start | bytes 1769472 | tf_op jit(solution)/shard_map/all_to_all | solution.py:99
  163.1 30.8 %all-to-all-start.5 = ((bf16[16,2,13824]{2,1,0:T(2,128)(2,1)}), bf16[16,2,13824]{2,1,0:T(2,128)(2,1)}, u32[]{:S(2)}, u32[]{:S(2)}) async-start(bf16[16,2,13824]{2,1,0:T(2,128)(2,1)} %reshape.186), calls=%async_computation.5 | async-start | bytes 1769472 | tf_op jit(solution)/shard_map/all_to_all | solution.py:100
  172.7 288.2 %all-gather.8.cloned.1.call-start = ((), (), s32[]{:S(2)}) async-start(), calls=%async_computation.10 | async-start | bytes 2088960 | tf_op jit(solution)/shard_map/all_gather | solution.py:107
  193.9 37.6 %all-to-all-start.1 = ((bf16[4,1,36,192]{3,2,1,0:T(8,128)(2,1)}), bf16[4,1,36,192]{3,2,1,0:T(8,128)(2,1)S(1)}, u32[]{:S(2)}, u32[]{:S(2)}) async-start(bf16[4,1,36,192]{3,2,1,0:T(8,128)(2,1)} %bitcast.20), calls=%async_computation.1 | async-start | bytes 163840 | tf_op jit(solution)/shard_map/all_to_all | solution.py:80
  231.5 40.8 %all-to-all-start.3 = ((bf16[4,1,36,192]{3,2,1,0:T(8,128)(2,1)}), bf16[4,1,36,192]{3,2,1,0:T(8,128)(2,1)S(1)}, u32[]{:S(2)}, u32[]{:S(2)}) async-start(bf16[4,1,36,192]{3,2,1,0:T(8,128)(2,1)} %bitcast.35), calls=%async_computation.3 | async-start | bytes 163840 | tf_op jit(solution)/shard_map/all_to_all | solution.py:83
  461.0 2.8 copy-start.3
  463.7 1.8 copy-start.4
Sparse Core Ops, SparseCore 0:
  86.7 74.5 reduce-scatter.6
  165.0 64.6 reduce-scatter.8
Sparse Core Ops, SparseCore 1:
  106.7 136.8 all-gather.3
  248.3 103.2 all-gather.5
  356.4 104.5 all-gather.7
where the time goes:
time: 482 us; the launch traced here: 475 us
  waiting for transfers between devices  263 us (55%)
  local copies, waits for them, and re-layouts  99.7 us (21%)
  starting transfers between devices  60.2 us (12%)
  matrix products  31.9 us (7%)
  between operations  15.9 us (3%)
    all_gather x1, waiting for transfers between devices, on_device(): lax.all_gather(hidden, 'seq', axis=0, tiled=True)  105 us
    all_gather x1, waiting for transfers between devices, on_device(): lax.all_gather(up_grad, 'seq', axis=0, tiled=True)  71.6 us
    unnamed x34, local copies, waits for them, and re-layouts  69.5 us
    unnamed x7, waiting for transfers between devices  29 us
    all_to_all x1, starting transfers between devices, on_device(): lax.all_to_all(rows_x, 'seq', split_axis=3, concat_axis=0, tiled=True)  22.1 us
    all_to_all x1, waiting for transfers between devices, on_device(): lax.all_to_all(rows_dy, 'seq', split_axis=3, concat_axis=0, tiled=True)  18.7 us
    all_to_all x1, waiting for transfers between devices, on_device(): lax.all_to_all(send_dy.astype(jnp.bfloat16).reshape(shaped), 'exp', split...  16.7 us
    all_to_all x1, waiting for transfers between devices, on_device(): lax.all_to_all(send_x.astype(jnp.bfloat16).reshape(shaped), 'exp', split_...  12.3 us
  transfers between devices with their start and end apart: 11, of which 7 were waited for; matrix products, arithmetic and copies ran while one was open for 23% of the time, Pallas kernels for 0%

commit v1 on v0

v1 whole, which is shorter than its diff:
```python
import functools

import jax
import jax.numpy as jnp
from jax import lax
from jax.experimental import pallas as pl
from jax.experimental.pallas import tpu as pltpu
from jax.sharding import Mesh, PartitionSpec as P

CAP = 36
SLOT = 40
N_Z = 8
N_Y = 8
N_XL = 4
BF16 = jnp.bfloat16
F32 = jnp.float32
HIGHEST = lax.Precision.HIGHEST


def dot(a, b, dims=((1,), (0,)), precision=None):
    return lax.dot_general(a, b, (dims, ((), ())), precision=precision, preferred_element_type=F32)


def picks(routes, gates):
    tok_count = routes.shape[1]
    shape = (N_XL * SLOT, tok_count)
    row = lax.broadcasted_iota(jnp.int32, shape, 0)
    expert = sum((row >= SLOT * i).astype(jnp.int32) for i in range(1, N_XL))
    slot = (row - SLOT * expert).astype(F32)
    first = routes[0:1, :] == expert
    second = routes[1:2, :] == expert
    member = jnp.where(first | second, 1.0, 0.0).astype(F32)
    at = lax.broadcasted_iota(jnp.int32, (tok_count, tok_count), 0)
    to = lax.broadcasted_iota(jnp.int32, (tok_count, tok_count), 1)
    earlier = jnp.where(at < to, 1.0, 0.0).astype(BF16)
    rank = dot(member.astype(BF16), earlier)
    pick = jnp.where(rank == slot, member, 0.0)
    gate = jnp.where(first, gates[0:1, :], gates[1:2, :]) * pick
    return pick, gate


def squeeze_matrix(rows, slots):
    row = lax.broadcasted_iota(jnp.int32, (rows, slots), 0)
    col = lax.broadcasted_iota(jnp.int32, (rows, slots), 1)
    expert = sum((row >= CAP * i).astype(jnp.int32) for i in range(1, N_XL))
    return jnp.where(col == row + (SLOT - CAP) * expert, 1.0, 0.0).astype(BF16)


def dispatch(flags, routes, gates, tokens, cotangent, rows_out):
    pick, gate = picks(routes[...], gates[...])
    pick = pick.astype(BF16)

    @pl.when(flags[0] == 0)
    def _():
        rows_out[...] = dot(pick, tokens[...]).astype(BF16)

    @pl.when(flags[0] != 0)
    def _():
        scale = jnp.sum(gate, axis=1, keepdims=True)
        rows_out[...] = (dot(pick, cotangent[...]) * scale).astype(BF16)


def squeeze(flags, rows, full_out, cols_out):
    count = full_out.shape[0]
    full = dot(squeeze_matrix(count, rows.shape[0]), rows[...]).astype(BF16)
    full_out[...] = full
    width = full.shape[1]
    half = width // 2
    part = half // N_Z

    def write(swap):
        for i in range(N_Z):
            low = full[:, part * i : part * (i + 1)]
            high = full[:, half + part * i : half + part * (i + 1)]
            pair = [high, low] if swap else [low, high]
            cols_out[i] = jnp.concatenate(pair, axis=1)

    @pl.when(flags[1] == 0)
    def _():
        write(False)

    @pl.when(flags[1] != 0)
    def _():
        write(True)


def expert_front(flags, mine, other, gate_w, up_w, down_w, pieces_out):
    is_x = flags[0] == 0
    a, b = mine[...], other[...]
    x = jnp.where(is_x, a, b)
    dy = jnp.where(is_x, b, a)
    gate_act = dot(x, gate_w[0])
    up_act = dot(x, up_w[0])
    hidden_grad = dot(dy, down_w[0], ((1,), (1,)))
    s = 1.0 / (1.0 + jnp.exp(-gate_act))
    silu = gate_act * s
    hidden = (silu * up_act).astype(BF16)
    gate_grad = (hidden_grad * up_act * s * (1.0 + gate_act * (1.0 - s))).astype(BF16)
    up_grad = (hidden_grad * silu).astype(BF16)
    pieces_out[...] = jnp.concatenate([hidden, gate_grad, up_grad], axis=1)


def expert_back(flags, pieces, gate_w, up_w, down_w, keep_out, send_out):
    ff = pieces.shape[1] // 3
    hidden = pieces[:, :ff]
    gate_grad = pieces[:, ff : 2 * ff]
    up_grad = pieces[:, 2 * ff :]
    out = dot(hidden, down_w[0]).astype(BF16)
    back = dot(gate_grad, gate_w[0], ((1,), (1,))) + dot(up_grad, up_w[0], ((1,), (1,)))
    back = back.astype(BF16)
    part = out.shape[1] // (2 * N_Y)

    def write(even, odd):
        for i in range(N_Y):
            for j, ref in ((2 * i, even), (2 * i + 1, odd)):
                at = slice(part * j, part * (j + 1))
                ref[i] = jnp.concatenate([out[:, at], back[:, at]], axis=1)

    @pl.when(flags[0] == 0)
    def _():
        write(keep_out, send_out)

    @pl.when(flags[0] != 0)
    def _():
        write(send_out, keep_out)


def add_up(blocks, rows_out):
    total = blocks[0].astype(F32)
    for i in range(1, N_Y):
        total = total + blocks[i].astype(F32)
    count = total.shape[0]
    spread = squeeze_matrix(count, rows_out.shape[0])
    rows_out[...] = dot(spread, total.astype(BF16), ((0,), (0,))).astype(BF16)


def combine(routes, gates, rows, layer_out, grad_out):
    pick, gate = picks(routes[...], gates[...])
    part = layer_out.shape[1]
    both = rows[...]
    layer_out[...] = dot(gate, both[:, :part].astype(F32), ((0,), (0,)), HIGHEST).astype(BF16)
    grad_out[...] = dot(pick.astype(BF16), both[:, part:], ((0,), (0,))).astype(BF16)


def weight_grads(flags, pieces, mine, other, keep_out, send_out):
    is_x = flags[0] == 0
    a, b = mine[...], other[...]
    x = jnp.where(is_x, a, b)
    dy = jnp.where(is_x, b, a)
    ff = pieces.shape[1] // 3
    down = dot(dy, pieces[:, :ff], ((0,), (0,)))
    gate_up = dot(x, pieces[:, ff:], ((0,), (0,)))
    part = keep_out.shape[0]
    both = jnp.concatenate([down, gate_up], axis=1)
    keep_out[...] = both[:part]
    send_out[...] = both[part:].astype(BF16)


def finish(keep, got, gate_out, up_out, down_out):
    total = keep[...] + got[...].astype(F32)
    ff = total.shape[1] // 3
    down_out[0] = total[:, :ff].T
    gate_out[0] = total[:, ff : 2 * ff]
    up_out[0] = total[:, 2 * ff :]


def call(body, outs, scalars, *operands):
    vmem = pl.BlockSpec(memory_space=pltpu.VMEM)
    specs = [pl.BlockSpec(memory_space=pltpu.SMEM)] * len(scalars) + [vmem] * len(operands)
    return pl.pallas_call(
        body,
        out_shape=[jax.ShapeDtypeStruct(s, t) for s, t in outs],
        in_specs=specs,
        out_specs=[vmem] * len(outs),
        compiler_params=pltpu.CompilerParams(vmem_limit_bytes=40 * 1024 * 1024),
        name=body.__name__,
    )(*scalars, *operands)


def swap(value, axis):
    return lax.ppermute(value, axis, [(0, 1), (1, 0)])


def on_device(tokens, cotangent, routes, router_gates, gate_weight, up_weight, down_weight):
    width = tokens.shape[1]
    tok_count = tokens.shape[0]
    ff = gate_weight.shape[2]
    part = width // 16
    slots = N_XL * SLOT
    rows = N_XL * CAP
    flags = jnp.stack([lax.axis_index("c"), lax.axis_index("xh")]).astype(jnp.int32)
    routes = routes.T
    gates = router_gates.T

    (sent,) = call(dispatch, [((slots, width), BF16)], [flags], routes, gates, tokens, cotangent)
    got = lax.all_to_all(
        sent.reshape(N_XL, SLOT, width), "xl", split_axis=0, concat_axis=0, tiled=True
    ).reshape(slots, width)
    mine, cols = call(
        squeeze, [((rows, width), BF16), ((N_Z, rows, 2 * part), BF16)], [flags], got
    )
    other = swap(mine, "c")
    (pieces,) = call(
        expert_front,
        [((rows, 3 * ff), BF16)],
        [flags],
        mine,
        other,
        gate_weight,
        up_weight,
        down_weight,
    )
    cols = lax.all_to_all(cols, "z", split_axis=0, concat_axis=0, tiled=True)
    cols = cols.reshape(N_Z * rows, 2 * part)
    cols_other = swap(cols, "c")
    pieces_all = lax.all_gather(pieces, "z", axis=0, tiled=True)

    keep, send = call(
        expert_back,
        [((N_Y, rows, 2 * part), BF16)] * 2,
        [flags],
        pieces,
        gate_weight,
        up_weight,
        down_weight,
    )
    summed = (keep.astype(F32) + swap(send, "c").astype(F32)).astype(BF16)
    blocks = lax.all_to_all(summed, "y", split_axis=0, concat_axis=0, tiled=True)
    (back,) = call(add_up, [((slots, 2 * part), BF16)], [], blocks)
    back = lax.all_to_all(
        back.reshape(N_XL, SLOT, 2 * part), "xl", split_axis=0, concat_axis=0, tiled=True
    ).reshape(slots, 2 * part)
    layer_out, token_grad = call(
        combine, [((tok_count, part), BF16)] * 2, [], routes, gates, back
    )

    kept, given = call(
        weight_grads,
        [((part, 3 * ff), F32), ((part, 3 * ff), BF16)],
        [flags],
        pieces_all,
        cols,
        cols_other,
    )
    grad_gate, grad_up, grad_down = call(
        finish,
        [((1, part, ff), F32), ((1, part, ff), F32), ((1, ff, part), F32)],
        [],
        kept,
        swap(given, "xh"),
    )
    return layer_out, token_grad, grad_gate, grad_up, grad_down


def solution(mesh):
    fine = Mesh(
        mesh.devices.reshape(2, N_Z, N_XL, N_Y, 2), ("xh", "z", "xl", "y", "c")
    )
    seq, ffn = ("xh", "z"), ("y", "c")
    rows = P(("xh", "z", "xl"), None)
    return jax.shard_map(
        on_device,
        mesh=fine,
        in_specs=(
            rows,
            rows,
            rows,
            rows,
            P("xl", None, ffn),
            P("xl", None, ffn),
            P("xl", ffn, None),
        ),
        out_specs=(
            P(("xh", "z", "xl"), ffn),
            P(("xh", "z", "xl"), ffn),
            P("xl", seq, ffn),
            P("xl", seq, ffn),
            P("xl", ffn, seq),
        ),
        check_vma=False,
    )
```

time: 482 us -> 167 us (0.35)
  the two profiles are of different devices: /device:TPU:14 before, /device:TPU:1 now
where the time goes in v1:
time: 167 us; the launch traced here: 166 us
  starting transfers between devices  48.3 us (29%)
  blocking collectives  33.4 us (20%)
  waiting for transfers between devices  32.2 us (19%)
  local copies, waits for them, and re-layouts  22.4 us (13%)
  between operations  14.1 us (8%)
  Pallas kernels  14 us (8%)
    ppermute x4, starting transfers between devices, swap(): return lax.ppermute(value, axis, [(0, 1), (1, 0)])  25.5 us
    unnamed x31, local copies, waits for them, and re-layouts  22.4 us
    all_to_all x1, blocking collectives, on_device(): lax.all_to_all(sent.reshape(N_XL, SLOT, width), 'xl', split_axis=0, conca...  19 us
    all_to_all x1, waiting for transfers between devices, on_device(): cols = lax.all_to_all(cols, 'z', split_axis=0, concat_axis=0, tiled=True)  17.8 us
    all_to_all x1, starting transfers between devices, on_device(): cols = lax.all_to_all(cols, 'z', split_axis=0, concat_axis=0, tiled=True)  14.9 us
    all_to_all x1, blocking collectives, on_device(): lax.all_to_all(back.reshape(N_XL, SLOT, 2 * part), 'xl', split_axis=0, co...  14.4 us
    pallas_call x8, Pallas kernels, call(): pl.pallas_call(body, out_shape=[jax.ShapeDtypeStruct(s, t) for s, t in ou...  14 us
    all_to_all x1, starting transfers between devices, on_device(): lax.all_to_all(summed, 'y', split_axis=0, concat_axis=0, tiled=True)  7.82 us
  transfers between devices with their start and end apart: 7, of which 5 were waited for; matrix products, arithmetic and copies ran while one was open for 5% of the time, Pallas kernels for 4%

profile of v1, /device:TPU:1, one launch (start us, length us, event | category | flops | bytes accessed | tf_op | source)
XLA Modules:
  0.0 165.7 jit_solution(8969055903637324181)
XLA Ops:
  7.2 0.0 all-gather.2.cloned.1.call-start
  7.2 0.1 pad_add_fusion.flags
  7.3 0.0 copy-start.8
  7.3 1.0 copy-done.8
  8.3 0.0 copy-start.9
  8.3 1.0 copy-done.9
  9.3 0.0 copy-start.10
  9.3 0.7 copy-done.10
  10.0 0.0 copy-start.12
  10.0 0.7 copy-done.12
  10.6 1.1 dispatch.1
  11.7 19.0 %all_to_all.20 = bf16[4,40,3072]{2,1,0:T(8,128)(2,1)S(1)} all-to-all(bf16[4,40,3072]{2,1,0:T(8,128)(2,1)S(1)} %bitcast.9), channel_id=1, replica_groups=mesh['xh'=2,'z'=8,'xl'=4,'y'=8,'c'=2] {'xl'}, dimensions={0} | all-to-all | bytes 1966080 | tf_op jit(solution)/shard_map/all_to_all | solution.py:196
  30.7 1.1 squeeze.1
  31.9 0.0 copy-start.5
  31.9 0.9 copy-done.5
  32.8 14.6 %collective-permute-start = (bf16[144,3072]{1,0:T(8,128)(2,1)S(1)}, bf16[144,3072]{1,0:T(8,128)(2,1)}, u32[]{:S(2)}, u32[]{:S(2)}) collective-permute-start(bf16[144,3072]{1,0:T(8,128)(2,1)S(1)} %get-tuple-element.16.mine), channel_id=1, source_target_pairs={{0,1},{1,0},{2,3},{3,2},{4,5},{5,4},{6,7},{7,6},{8,9},{9,8},{10,11... | collective-permute-start | bytes 2654216 | tf_op jit(solution)/shard_map/ppermute | solution.py:181
  47.5 2.9 %copy.12.gate_w = bf16[1,3072,336]{2,1,0:T(8,128)(2,1)S(1)} copy(bf16[1,3072,336]{1,2,0:T(8,128)(2,1)} %param.11) | data formatting | bytes 4128768 | tf_op args[4]
  50.4 4.1 %copy.13.up_w = bf16[1,3072,336]{2,1,0:T(8,128)(2,1)} copy(bf16[1,3072,336]{1,2,0:T(8,128)(2,1)} %param.12) | data formatting | bytes 4128768 | tf_op args[5]
  54.6 0.0 collective-permute-done.other
  54.6 0.0 copy-start
  54.6 1.7 %copy-done = bf16[1,3072,336]{2,1,0:T(8,128)(2,1)S(1)} copy-done((bf16[1,3072,336]{2,1,0:T(8,128)(2,1)S(1)}, bf16[1,3072,336]{2,1,0:T(8,128)(2,1)}, u32[]{:S(2)}) %copy-start) | copy-done | bytes 2064408
  56.2 0.0 copy-start.2
  56.2 1.6 copy-done.2
  57.8 3.7 %expert_front.1.pieces = bf16[144,1008]{1,0:T(8,128)(2,1)} custom-call(s32[2]{0:T(128)S(1)} %pad_add_fusion.flags, bf16[144,3072]{1,0:T(8,128)(2,1)S(1)} %get-tuple-element.16.mine, bf16[144,3072]{1,0:T(8,128)(2,1)} %collective-permute-done.other, bf16[1,3072,336]{2,1,0:T(8,128)(2,1)S(1)} %copy.12.gate_w, bf16[1,3072,336]{2,1,0:T(8,128)(2,1)S(1)} %copy-done, ...), custom_call_target="tpu_custom_call" | custom-call | tf_op jit(solution)/shard_map/expert_front/pallas_call | solution.py:170
  61.6 0.0 all-gather.2.cloned.1.call-update
  61.6 14.9 %all-to-all-start.3 = ((bf16[8,144,384]{2,1,0:T(8,128)(2,1)}), bf16[8,144,384]{2,1,0:T(8,128)(2,1)S(1)}, u32[]{:S(2)}, u32[]{:S(2)}) async-start(bf16[8,144,384]{2,1,0:T(8,128)(2,1)} %copy-done.5), calls=%async_computation.3 | async-start | bytes 1769472 | tf_op jit(solution)/shard_map/all_to_all | solution.py:213
  76.5 0.0 copy-start.1
  76.5 1.7 %copy-done.1 = bf16[1,3072,336]{2,1,0:T(8,128)(2,1)S(1)} copy-done((bf16[1,3072,336]{2,1,0:T(8,128)(2,1)S(1)}, bf16[1,3072,336]{2,1,0:T(8,128)(2,1)}, u32[]{:S(2)}) %copy-start.1) | copy-done | bytes 2064408
  78.1 0.0 copy-start.3
  78.1 1.6 copy-done.3
  79.7 3.5 %expert_back.1 = (bf16[8,144,384]{2,1,0:T(8,128)(2,1)S(1)}, bf16[8,144,384]{2,1,0:T(8,128)(2,1)S(1)}) custom-call(s32[2]{0:T(128)S(1)} %pad_add_fusion.flags, bf16[144,1008]{1,0:T(8,128)(2,1)} %expert_front.1.pieces, bf16[1,3072,336]{2,1,0:T(8,128)(2,1)S(1)} %copy.12.gate_w, bf16[1,3072,336]{2,1,0:T(8,128)(2,1)S(1)} %copy-done.1, ...), custom_call_target="tpu_custom_call" | custom-call | tf_op jit(solution)/shard_map/expert_back/pallas_call | solution.py:170
  83.2 2.2 %collective-permute-start.1 = (bf16[8,144,384]{2,1,0:T(8,128)(2,1)S(1)}, bf16[8,144,384]{2,1,0:T(8,128)(2,1)S(1)}, u32[]{:S(2)}, u32[]{:S(2)}) collective-permute-start(bf16[8,144,384]{2,1,0:T(8,128)(2,1)S(1)} %get-tuple-element.18), channel_id=1, source_target_pairs={{0,1},{1,0},{2,3},{3,2},{4,5},{5,4},{6,7},{7,6},{8,9},{9,8},{10,11... | collective-permute-start | bytes 2654216 | tf_op jit(solution)/shard_map/ppermute | solution.py:181
  85.4 2.1 %collective-permute-done.1 = bf16[8,144,384]{2,1,0:T(8,128)(2,1)S(1)} collective-permute-done((bf16[8,144,384]{2,1,0:T(8,128)(2,1)S(1)}, bf16[8,144,384]{2,1,0:T(8,128)(2,1)S(1)}, u32[]{:S(2)}, u32[]{:S(2)}) %collective-permute-start.1) | collective-permute-done | bytes 884768 | tf_op jit(solution)/shard_map/ppermute | solution.py:181
  87.5 1.1 add_convert_fusion
  88.7 17.8 %all-to-all-done.3 = bf16[8,144,384]{2,1,0:T(8,128)(2,1)S(1)} async-done(((bf16[8,144,384]{2,1,0:T(8,128)(2,1)}), bf16[8,144,384]{2,1,0:T(8,128)(2,1)S(1)}, u32[]{:S(2)}, u32[]{:S(2)}) %all-to-all-start.3) | async-done | bytes 884768 | tf_op jit(solution)/shard_map/all_to_all | solution.py:213
  106.5 0.0 copy-start.13
  106.5 7.8 %all-to-all-start.1 = ((bf16[8,144,384]{2,1,0:T(8,128)(2,1)}), bf16[8,144,384]{2,1,0:T(8,128)(2,1)S(1)}, u32[]{:S(2)}, u32[]{:S(2)}) async-start(bf16[8,144,384]{2,1,0:T(8,128)(2,1)} %add_convert_fusion), calls=%async_computation.1 | async-start | bytes 1769472 | tf_op jit(solution)/shard_map/all_to_all | solution.py:228
  114.3 0.0 copy-start.11
  114.3 3.0 %collective-permute-start.2 = (bf16[1152,384]{1,0:T(8,128)(2,1)S(1)}, bf16[1152,384]{1,0:T(8,128)(2,1)S(1)}, u32[]{:S(2)}, u32[]{:S(2)}) collective-permute-start(bf16[1152,384]{1,0:T(8,128)(2,1)S(1)} %bitcast.11), channel_id=1, source_target_pairs={{0,1},{1,0},{2,3},{3,2},{4,5},{5,4},{6,7},{7,6},{8,9},{9,8},{10,11... | collective-permute-start | bytes 2654216 | tf_op jit(solution)/shard_map/ppermute | solution.py:181
  117.3 2.0 %collective-permute-done.2.other = bf16[1152,384]{1,0:T(8,128)(2,1)S(1)} collective-permute-done((bf16[1152,384]{1,0:T(8,128)(2,1)S(1)}, bf16[1152,384]{1,0:T(8,128)(2,1)S(1)}, u32[]{:S(2)}, u32[]{:S(2)}) %collective-permute-start.2) | collective-permute-done | bytes 884768 | tf_op jit(solution)/shard_map/ppermute | solution.py:181
  119.3 3.3 %all-gather.2.cloned.1.call-done.pieces = bf16[1152,1008]{1,0:T(8,128)(2,1)} async-done(((bf16[144,1008]{1,0:T(8,128)(2,1)}), bf16[1152,1008]{1,0:T(8,128)(2,1)}) %all-gather.2.cloned.1.call-update) | async-done | bytes 2322448 | tf_op jit(solution)/shard_map/all_gather | solution.py:216
  122.7 0.0 copy-start.4
  122.7 1.7 %copy-done.4 = bf16[1152,1008]{1,0:T(8,128)(2,1)S(1)} copy-done((bf16[1152,1008]{1,0:T(8,128)(2,1)S(1)}, bf16[1152,1008]{1,0:T(8,128)(2,1)}, u32[]{:S(2)}) %copy-start.4) | copy-done | bytes 2322456
  124.3 2.2 %weight_grads.1 = (f32[192,1008]{1,0:T(8,128)S(1)}, bf16[192,1008]{1,0:T(8,128)(2,1)S(1)}) custom-call(s32[2]{0:T(128)S(1)} %pad_add_fusion.flags, bf16[1152,1008]{1,0:T(8,128)(2,1)S(1)} %copy-done.4, bf16[1152,384]{1,0:T(8,128)(2,1)S(1)} %bitcast.12, bf16[1152,384]{1,0:T(8,128)(2,1)S(1)} %collective-permute-done.2.other), custom_call_target="tpu_custom_call" | custom-call | tf_op jit(solution)/shard_map/weight_grads/pallas_call | solution.py:170
  126.6 0.0 copy-start.6
  126.6 0.9 copy-done.6
  127.5 5.7 %collective-permute-start.3 = (bf16[192,1008]{1,0:T(8,128)(2,1)S(1)}, bf16[192,1008]{1,0:T(8,128)(2,1)S(1)}, u32[]{:S(2)}, u32[]{:S(2)}) collective-permute-start(bf16[192,1008]{1,0:T(8,128)(2,1)S(1)} %get-tuple-element.23), channel_id=1, source_target_pairs={{0,512},{512,0},{1,513},{513,1},{2,514},{514,2},{3,515},{515,3},{4... | collective-permute-start | bytes 1161224 | tf_op jit(solution)/shard_map/ppermute | solution.py:181
  133.1 6.8 %all-to-all-done.1.blocks = bf16[8,144,384]{2,1,0:T(8,128)(2,1)S(1)} async-done(((bf16[8,144,384]{2,1,0:T(8,128)(2,1)}), bf16[8,144,384]{2,1,0:T(8,128)(2,1)S(1)}, u32[]{:S(2)}, u32[]{:S(2)}) %all-to-all-start.1) | async-done | bytes 884768 | tf_op jit(solution)/shard_map/all_to_all | solution.py:228
  140.0 0.3 add_up.1
  140.3 14.4 %all_to_all.21 = bf16[4,40,384]{2,1,0:T(8,128)(2,1)S(1)} all-to-all(bf16[4,40,384]{2,1,0:T(8,128)(2,1)S(1)} %bitcast.14), channel_id=1, replica_groups=mesh['xh'=2,'z'=8,'xl'=4,'y'=8,'c'=2] {'xl'}, dimensions={0} | all-to-all | bytes 245760 | tf_op jit(solution)/shard_map/all_to_all | solution.py:230
  154.7 0.0 copy-done.13
  154.7 0.0 copy-done.11
  154.7 1.1 combine.1
  155.7 0.0 collective-permute-done.3.got
  155.7 0.0 copy-start.7
  155.7 1.1 copy-done.7
  156.9 1.1 finish.1
  158.0 0.9 copy.16
Async XLA Ops:
  7.2 115.5 %all-gather.2.cloned.1.call-start = ((), (), s32[]{:S(2)}) async-start(), calls=%async_computation.4 | async-start | bytes 2654208 | tf_op jit(solution)/shard_map/all_gather | solution.py:216
  7.3 1.0 copy-start.8
  8.3 1.0 copy-start.9
  9.3 0.7 copy-start.10
  10.0 0.7 copy-start.12
  31.9 1.0 copy-start.5
  32.8 21.7 %collective-permute-start = (bf16[144,3072]{1,0:T(8,128)(2,1)S(1)}, bf16[144,3072]{1,0:T(8,128)(2,1)}, u32[]{:S(2)}, u32[]{:S(2)}) collective-permute-start(bf16[144,3072]{1,0:T(8,128)(2,1)S(1)} %get-tuple-element.16.mine), channel_id=1, source_target_pairs={{0,1},{1,0},{2,3},{3,2},{4,5},{5,4},{6,7},{7,6},{8,9},{9,8},{10,11... | collective-permute-start | bytes 2654216 | tf_op jit(solution)/shard_map/ppermute | solution.py:181
  54.6 1.7 %copy-start = (bf16[1,3072,336]{2,1,0:T(8,128)(2,1)S(1)}, bf16[1,3072,336]{2,1,0:T(8,128)(2,1)}, u32[]{:S(2)}) copy-start(bf16[1,3072,336]{2,1,0:T(8,128)(2,1)} %copy.13.up_w) | copy-start | bytes 6193156
  56.2 1.6 copy-start.2
  61.6 44.9 %all-to-all-start.3 = ((bf16[8,144,384]{2,1,0:T(8,128)(2,1)}), bf16[8,144,384]{2,1,0:T(8,128)(2,1)S(1)}, u32[]{:S(2)}, u32[]{:S(2)}) async-start(bf16[8,144,384]{2,1,0:T(8,128)(2,1)} %copy-done.5), calls=%async_computation.3 | async-start | bytes 1769472 | tf_op jit(solution)/shard_map/all_to_all | solution.py:213
  76.5 1.7 %copy-start.1 = (bf16[1,3072,336]{2,1,0:T(8,128)(2,1)S(1)}, bf16[1,3072,336]{2,1,0:T(8,128)(2,1)}, u32[]{:S(2)}) copy-start(bf16[1,3072,336]{2,1,0:T(8,128)(2,1)} %copy.13.up_w) | copy-start | bytes 6193156
  78.1 1.6 copy-start.3
  83.2 4.3 %collective-permute-start.1 = (bf16[8,144,384]{2,1,0:T(8,128)(2,1)S(1)}, bf16[8,144,384]{2,1,0:T(8,128)(2,1)S(1)}, u32[]{:S(2)}, u32[]{:S(2)}) collective-permute-start(bf16[8,144,384]{2,1,0:T(8,128)(2,1)S(1)} %get-tuple-element.18), channel_id=1, source_target_pairs={{0,1},{1,0},{2,3},{3,2},{4,5},{5,4},{6,7},{7,6},{8,9},{9,8},{10,11... | collective-permute-start | bytes 2654216 | tf_op jit(solution)/shard_map/ppermute | solution.py:181
  106.5 48.2 %copy-start.13 = (f32[64,2]{0,1:T(2,128)S(1)}, f32[64,2]{0,1:T(2,128)}, u32[]{:S(2)}) copy-start(f32[64,2]{0,1:T(2,128)} %param.10) | copy-start | bytes 1540
  106.5 33.5 %all-to-all-start.1 = ((bf16[8,144,384]{2,1,0:T(8,128)(2,1)}), bf16[8,144,384]{2,1,0:T(8,128)(2,1)S(1)}, u32[]{:S(2)}, u32[]{:S(2)}) async-start(bf16[8,144,384]{2,1,0:T(8,128)(2,1)} %add_convert_fusion), calls=%async_computation.1 | async-start | bytes 1769472 | tf_op jit(solution)/shard_map/all_to_all | solution.py:228
  114.3 40.4 %copy-start.11 = (s32[64,2]{0,1:T(2,128)S(1)}, s32[64,2]{0,1:T(2,128)}, u32[]{:S(2)}) copy-start(s32[64,2]{0,1:T(2,128)} %param.9) | copy-start | bytes 1540
  114.3 5.0 %collective-permute-start.2 = (bf16[1152,384]{1,0:T(8,128)(2,1)S(1)}, bf16[1152,384]{1,0:T(8,128)(2,1)S(1)}, u32[]{:S(2)}, u32[]{:S(2)}) collective-permute-start(bf16[1152,384]{1,0:T(8,128)(2,1)S(1)} %bitcast.11), channel_id=1, source_target_pairs={{0,1},{1,0},{2,3},{3,2},{4,5},{5,4},{6,7},{7,6},{8,9},{9,8},{10,11... | collective-permute-start | bytes 2654216 | tf_op jit(solution)/shard_map/ppermute | solution.py:181
  122.7 1.7 %copy-start.4 = (bf16[1152,1008]{1,0:T(8,128)(2,1)S(1)}, bf16[1152,1008]{1,0:T(8,128)(2,1)}, u32[]{:S(2)}) copy-start(bf16[1152,1008]{1,0:T(8,128)(2,1)} %all-gather.2.cloned.1.call-done.pieces) | copy-start | bytes 6967300
  126.6 0.9 copy-start.6
  127.5 28.3 %collective-permute-start.3 = (bf16[192,1008]{1,0:T(8,128)(2,1)S(1)}, bf16[192,1008]{1,0:T(8,128)(2,1)S(1)}, u32[]{:S(2)}, u32[]{:S(2)}) collective-permute-start(bf16[192,1008]{1,0:T(8,128)(2,1)S(1)} %get-tuple-element.23), channel_id=1, source_target_pairs={{0,512},{512,0},{1,513},{513,1},{2,514},{514,2},{3,515},{515,3},{4... | collective-permute-start | bytes 1161224 | tf_op jit(solution)/shard_map/ppermute | solution.py:181
  155.7 1.1 copy-start.7
Sparse Core Ops, SparseCore 0:
  61.7 60.9 all-gather.1

commit v2 on v1

v2 whole, which is shorter than its diff:
```python
import jax
import jax.numpy as jnp
from jax import lax
from jax.experimental import pallas as pl
from jax.experimental.pallas import tpu as pltpu
from jax.sharding import Mesh, PartitionSpec as P

CAP = 36
SLOT = 40
SOON = (0, 1, 7, 2, 6, 3, 5)
CUTS = 3
N_Z = 8
N_Y = 8
N_XL = 4
VMEM_BYTES = 20 * 1024 * 1024
BF16 = jnp.bfloat16
F32 = jnp.float32
HIGHEST = lax.Precision.HIGHEST


def dot(a, b, dims=((1,), (0,)), precision=None):
    return lax.dot_general(a, b, (dims, ((), ())), precision=precision, preferred_element_type=F32)


def picks(routes, gates, base=0):
    tok_count = routes.shape[1]
    shape = (N_XL * SLOT, tok_count)
    row = lax.broadcasted_iota(jnp.int32, shape, 0)
    expert = sum((row >= SLOT * i).astype(jnp.int32) for i in range(1, N_XL))
    slot = (row - SLOT * expert).astype(F32)
    expert = expert + base
    expert = jnp.where(expert >= N_XL, expert - N_XL, expert)
    first = routes[0:1, :] == expert
    second = routes[1:2, :] == expert
    member = jnp.where(first | second, 1.0, 0.0).astype(F32)
    at = lax.broadcasted_iota(jnp.int32, (tok_count, tok_count), 0)
    to = lax.broadcasted_iota(jnp.int32, (tok_count, tok_count), 1)
    earlier = jnp.where(at < to, 1.0, 0.0).astype(BF16)
    rank = dot(member.astype(BF16), earlier)
    pick = jnp.where(rank == slot, member, 0.0)
    gate = jnp.where(first, gates[0:1, :], gates[1:2, :]) * pick
    return pick, gate


def squeeze_matrix(rows, slots):
    row = lax.broadcasted_iota(jnp.int32, (rows, slots), 0)
    col = lax.broadcasted_iota(jnp.int32, (rows, slots), 1)
    expert = sum((row >= CAP * i).astype(jnp.int32) for i in range(1, N_XL))
    return jnp.where(col == row + (SLOT - CAP) * expert, 1.0, 0.0).astype(BF16)


def fetch_rows(pairs, sems):
    cuts = []
    for i, (a, b) in enumerate(pairs):
        step = a.shape[1] // CUTS
        at = [pl.ds(step * k, step) for k in range(CUTS)]
        cuts.append([pltpu.make_async_copy(a.at[:, r], b.at[:, r], sems.at[CUTS * i + k]) for k, r in enumerate(at)])
    for group in cuts:
        for copy in group:
            copy.start()
    return cuts


def fetch(pairs, sems):
    copies = [pltpu.make_async_copy(a, b, sems.at[i]) for i, (a, b) in enumerate(pairs)]
    for copy in copies:
        copy.start()
    return copies


def wait_all(copies):
    for copy in copies:
        copy.wait()


def dispatch(flags, routes_at, gates_at, tokens, cotangent, *refs):
    rows_out, (routes, gates, source, sem, sems) = refs[:N_XL], refs[N_XL:]
    is_x = flags[0] == 0
    copies = fetch(((routes_at, routes), (gates_at, gates)), sems)

    @pl.when(is_x)
    def _():
        pltpu.make_async_copy(tokens, source, sem).start()

    @pl.when(jnp.logical_not(is_x))
    def _():
        pltpu.make_async_copy(cotangent, source, sem).start()

    for copy in copies:
        copy.wait()
    pick, gate = picks(routes[...], gates[...], flags[3])
    scale = jnp.where(is_x, 1.0, jnp.sum(gate, axis=1, keepdims=True))
    pltpu.make_async_copy(tokens, source, sem).wait()
    rows = (dot(pick.astype(BF16), source[...]) * scale).astype(BF16)
    for k in range(N_XL):
        rows_out[k][...] = rows[SLOT * k : SLOT * (k + 1)]


def squeeze(flags, *refs):
    parts, (full_out, cols_out, cols, sems) = refs[:N_XL], refs[N_XL:]
    rows = jnp.concatenate([part[...] for part in parts], axis=0)
    matrix = squeeze_matrix(full_out.shape[0], rows.shape[0])
    full = dot(matrix, rows).astype(BF16)
    full_out[...] = full
    half = full.shape[1] // 2
    part = half // N_Z

    def write(swapped):
        for i in range(N_Z):
            low = full[:, part * i : part * (i + 1)]
            high = full[:, half + part * i : half + part * (i + 1)]
            cols[i] = jnp.concatenate([high, low] if swapped else [low, high], axis=1)

    @pl.when(flags[1] == 0)
    def _():
        write(False)

    @pl.when(flags[1] != 0)
    def _():
        write(True)

    wait_all(fetch([(cols.at[i], cols_out.at[i]) for i in range(N_Z)], sems))


def expert_front(flags, mine, other, gate_w, up_w, down_w, pieces_out, gate_v, up_v, down_v, sems):
    copies = fetch_rows(((gate_w, gate_v), (up_w, up_v), (down_w, down_v)), sems)
    is_x = flags[0] == 0
    a, b = mine[...], other[...]
    x = jnp.where(is_x, a, b)
    dy = jnp.where(is_x, b, a)
    wait_all(copies[0])
    gate_act = dot(x, gate_v[0], ((1,), (1,)))
    wait_all(copies[1])
    up_act = dot(x, up_v[0], ((1,), (1,)))
    wait_all(copies[2])
    hidden_grad = dot(dy, down_v[0], ((1,), (1,)))
    s = 1.0 / (1.0 + jnp.exp(-gate_act))
    silu = gate_act * s
    hidden = (silu * up_act).astype(BF16)
    gate_grad = (hidden_grad * up_act * s * (1.0 + gate_act * (1.0 - s))).astype(BF16)
    up_grad = (hidden_grad * silu).astype(BF16)
    pieces_out[...] = jnp.concatenate([hidden, gate_grad, up_grad], axis=1)


def expert_back(
    flags, pieces, gate_w, up_w, down_w, keep_out, send_out, gate_v, up_v, down_v, sems
):
    copies = fetch_rows(((down_w, down_v), (gate_w, gate_v), (up_w, up_v)), sems)
    ff = pieces.shape[1] // 3
    hidden = pieces[:, :ff]
    gate_grad = pieces[:, ff : 2 * ff]
    up_grad = pieces[:, 2 * ff :]
    wait_all(copies[0])
    out = dot(hidden, down_v[0]).astype(BF16)
    wait_all(copies[1])
    wait_all(copies[2])
    back = (dot(gate_grad, gate_v[0]) + dot(up_grad, up_v[0])).astype(BF16)
    part = out.shape[1] // (2 * N_Y)

    def write(even, odd):
        for i in range(N_Y):
            for j, ref in ((2 * i, even), (2 * i + 1, odd)):
                at = slice(part * j, part * (j + 1))
                ref[i] = jnp.concatenate([out[:, at], back[:, at]], axis=1)

    @pl.when(flags[0] == 0)
    def _():
        write(keep_out, send_out)

    @pl.when(flags[0] != 0)
    def _():
        write(send_out, keep_out)


def add_up(flags, blocks, rows_out):
    total = blocks[0].astype(F32)
    for i in range(1, N_Y):
        total = total + blocks[i].astype(F32)
    spread_out = squeeze_matrix(total.shape[0], N_XL * SLOT)
    rows = dot(spread_out, total.astype(BF16), ((0,), (0,))).astype(BF16)
    for k in range(N_XL):
        rows_out[lax.rem(flags[3] + (N_XL - k), N_XL)] = rows[SLOT * k : SLOT * (k + 1)]


def combine(routes, gates, rows, layer_out, grad_out):
    pick, gate = picks(routes[...], gates[...])
    part = layer_out.shape[1]
    both = rows[...]
    layer_out[...] = dot(gate, both[:, :part].astype(F32), ((0,), (0,)), HIGHEST).astype(BF16)
    grad_out[...] = dot(pick.astype(BF16), both[:, part:], ((0,), (0,))).astype(BF16)


def grads_of(flags, mine, other, distances, rows):
    is_x = flags[0] == 0
    order = [lax.rem(flags[2] + (N_Z - k), N_Z) for k in distances]
    a = jnp.concatenate([mine[k] for k in order], axis=0)
    b = jnp.concatenate([other[k] for k in order], axis=0)
    x = jnp.where(is_x, a, b)
    dy = jnp.where(is_x, b, a)
    ff = rows.shape[1] // 3
    down = dot(dy, rows[:, :ff], ((0,), (0,)))
    gate_up = dot(x, rows[:, ff:], ((0,), (0,)))
    return jnp.concatenate([down, gate_up], axis=1)


def weight_grads(flags, mine, other, *refs):
    *pieces, total_out, held, sems = refs
    count = pieces[0].shape[0]
    places = [held.at[pl.ds(count * i, count)] for i in range(len(SOON))]
    wait_all(fetch(list(zip(pieces, places)), sems))
    total_out[...] = grads_of(flags, mine, other, SOON, held[...])


def weight_grads_last(flags, mine, other, piece, total, keep_out, send_out):
    both = total[...] + grads_of(flags, mine, other, (N_Z // 2,), piece[...])
    part = keep_out.shape[0]
    keep_out[...] = both[:part]
    send_out[...] = both[part:].astype(BF16)


def finish(keep, got, gate_out, up_out, down_out):
    total = keep[...] + got[...].astype(F32)
    ff = total.shape[1] // 3
    down_out[0] = total[:, :ff]
    gate_out[0] = total[:, ff : 2 * ff]
    up_out[0] = total[:, 2 * ff :]


def call(body, outs, scalars, *operands, far=(), scratch=(), flops=0, far_outs=0):
    vmem = pl.BlockSpec(memory_space=pltpu.VMEM)
    smem = pl.BlockSpec(memory_space=pltpu.SMEM)
    hbm = pl.BlockSpec(memory_space=pltpu.HBM)
    moved = sum(v.size * v.dtype.itemsize for v in (*operands, *far))
    cost = pl.CostEstimate(flops=flops, transcendentals=0, bytes_accessed=moved)
    return pl.pallas_call(
        body,
        out_shape=[
            jax.ShapeDtypeStruct(s, t) if i < len(outs) - far_outs else pltpu.HBM(s, t)
            for i, (s, t) in enumerate(outs)
        ],
        in_specs=[smem] * len(scalars)
        + [vmem] * len(operands)
        + [hbm] * len(far),
        out_specs=[vmem] * (len(outs) - far_outs) + [hbm] * far_outs,
        scratch_shapes=list(scratch),
        compiler_params=pltpu.CompilerParams(vmem_limit_bytes=VMEM_BYTES),
        cost_estimate=cost if flops else None,
        name=body.__name__,
    )(*scalars, *operands, *[pltpu.with_memory_space_constraint(v, pltpu.HBM) for v in far])


def shift(value, by):
    return lax.ppermute(value, "z", [(i, (i + by) % N_Z) for i in range(N_Z)])


def spread(parts, axis, forward=1):
    count = len(parts)
    return [parts[0]] + [
        lax.ppermute(parts[k], axis, [(i, (i + forward * k) % count) for i in range(count)])
        for k in range(1, count)
    ]


def swap(value, axis):
    return lax.ppermute(value, axis, [(0, 1), (1, 0)])


def on_device(tokens, cotangent, routes, router_gates, gate_weight, up_weight, down_weight):
    width = tokens.shape[1]
    tok_count = tokens.shape[0]
    ff = gate_weight.shape[2]
    part = width // 16
    slots = N_XL * SLOT
    rows = N_XL * CAP
    work = 3 * 2 * rows * width * ff
    flags = jnp.stack([lax.axis_index(a) for a in ("c", "xh", "z", "xl", "y")]).astype(jnp.int32)
    routes = routes.T
    gates = router_gates.T
    weights = (jnp.swapaxes(gate_weight, 1, 2), jnp.swapaxes(up_weight, 1, 2), down_weight)
    held = [pltpu.VMEM(w.shape, BF16) for w in weights]
    held.append(pltpu.SemaphoreType.DMA((3 * CUTS,)))

    sent = call(
        dispatch,
        [((SLOT, width), BF16)] * N_XL,
        [flags],
        far=(routes, gates, tokens, cotangent),
        scratch=(
            pltpu.VMEM(routes.shape, routes.dtype),
            pltpu.VMEM(gates.shape, gates.dtype),
            pltpu.VMEM(tokens.shape, BF16),
            pltpu.SemaphoreType.DMA,
            pltpu.SemaphoreType.DMA((2,)),
        ),
    )
    got = spread(sent, "xl")
    mine, cols = call(
        squeeze,
        [((rows, width), BF16), ((N_Z, rows, 2 * part), BF16)],
        [flags],
        *got,
        scratch=(pltpu.VMEM((N_Z, rows, 2 * part), BF16), pltpu.SemaphoreType.DMA((N_Z,))),
        far_outs=1,
    )
    other = swap(mine, "c")
    cols = lax.all_to_all(cols, "z", split_axis=0, concat_axis=0, tiled=True)
    (pieces,) = call(
        expert_front, [((rows, 3 * ff), BF16)], [flags], mine, other, far=weights, scratch=held
    )
    keep, send = call(
        expert_back,
        [((N_Y, rows, 2 * part), BF16)] * 2,
        [flags],
        pieces,
        far=weights,
        scratch=held,
        flops=work,
    )
    summed = (keep.astype(F32) + swap(send, "c").astype(F32)).astype(BF16)

    found = [pieces] + [None] * (N_Z - 1)
    for k in range(1, N_Z // 2):
        found[k] = shift(found[k - 1], 1)
        found[N_Z - k] = shift(found[(N_Z - k + 1) % N_Z], -1)
    found[N_Z // 2] = shift(found[N_Z // 2 - 1], 1)
    cols_other = swap(cols, "c")

    blocks = lax.all_to_all(summed, "y", split_axis=0, concat_axis=0, tiled=True)
    (back,) = call(add_up, [((N_XL, SLOT, 2 * part), BF16)], [flags], blocks)
    back = lax.all_to_all(back, "xl", split_axis=0, concat_axis=0, tiled=True)
    layer_out, token_grad = call(
        combine,
        [((tok_count, part), BF16)] * 2,
        [],
        routes,
        gates,
        back.reshape(slots, 2 * part),
    )

    (total,) = call(
        weight_grads,
        [((2 * part, 3 * ff), F32)],
        [flags],
        cols,
        cols_other,
        far=[found[k] for k in SOON],
        scratch=(
            pltpu.VMEM((len(SOON) * rows, 3 * ff), BF16),
            pltpu.SemaphoreType.DMA((len(SOON),)),
        ),
        flops=2 * len(SOON) * rows * 2 * part * 3 * ff,
    )
    kept, given = call(
        weight_grads_last,
        [((part, 3 * ff), F32), ((part, 3 * ff), BF16)],
        [flags],
        cols,
        cols_other,
        found[N_Z // 2],
        total,
    )
    grad_gate, grad_up, grad_down = call(
        finish, [((1, part, ff), F32)] * 3, [], kept, swap(given, "xh")
    )
    return layer_out, token_grad, grad_gate, grad_up, jnp.swapaxes(grad_down, 1, 2)


def solution(mesh):
    fine = Mesh(
        mesh.devices.reshape(2, N_Z, N_XL, N_Y, 2), ("xh", "z", "xl", "y", "c")
    )
    seq, ffn = ("xh", "z"), ("y", "c")
    rows = P(("xh", "z", "xl"), None)
    return jax.shard_map(
        on_device,
        mesh=fine,
        in_specs=(
            rows,
            rows,
            rows,
            rows,
            P("xl", None, ffn),
            P("xl", None, ffn),
            P("xl", ffn, None),
        ),
        out_specs=(
            P(("xh", "z", "xl"), ffn),
            P(("xh", "z", "xl"), ffn),
            P("xl", seq, ffn),
            P("xl", seq, ffn),
            P("xl", ffn, seq),
        ),
        check_vma=False,
    )
```

time: 167 us -> 156 us (0.934)
  the two profiles are of different devices: /device:TPU:1 before, /device:TPU:16 now
where the time goes in v2:
time: 156 us; the launch traced here: 155 us
  starting transfers between devices  79.6 us (51%)
  waiting for transfers between devices  50.2 us (32%)
  Pallas kernels  22.7 us (15%)
    ppermute x7, starting transfers between devices, shift(): return lax.ppermute(value, 'z', [(i, (i + by) % N_Z) for i in range(N_Z)])  24 us
    pallas_call x9, Pallas kernels, call(): pl.pallas_call(body, out_shape=[jax.ShapeDtypeStruct(s, t) if i < len(out...  22.7 us
    all_to_all x1, starting transfers between devices, on_device(): cols = lax.all_to_all(cols, 'z', split_axis=0, concat_axis=0, tiled=True)  16.7 us
    ppermute x7, waiting for transfers between devices, shift(): return lax.ppermute(value, 'z', [(i, (i + by) % N_Z) for i in range(N_Z)])  13.4 us
    ppermute x4, starting transfers between devices, swap(): return lax.ppermute(value, axis, [(0, 1), (1, 0)])  13 us
    all_to_all x1, waiting for transfers between devices, on_device(): back = lax.all_to_all(back, 'xl', split_axis=0, concat_axis=0, tiled=True)  12.9 us
    ppermute x3, waiting for transfers between devices, spread(): lax.ppermute(parts[k], axis, [(i, (i + forward * k) % count) for i in ran...  11.4 us
    ppermute x3, starting transfers between devices, spread(): lax.ppermute(parts[k], axis, [(i, (i + forward * k) % count) for i in ran...  11.1 us
  transfers between devices with their start and end apart: 17, of which 12 were waited for; matrix products, arithmetic and copies ran while one was open for 1% of the time, Pallas kernels for 11%

profile of v2, /device:TPU:16, one launch (start us, length us, event | category | flops | bytes accessed | tf_op | source)
XLA Modules:
  0.0 155.4 jit_solution(14102651959217399606)
XLA Ops:
  0.6 0.1 stack.23.flags
  0.7 2.0 %dispatch.1 = (bf16[40,3072]{1,0:T(8,128)(2,1)S(1)}, bf16[40,3072]{1,0:T(8,128)(2,1)S(1)}, bf16[40,3072]{1,0:T(8,128)(2,1)S(1)}, bf16[40,3072]{1,0:T(8,128)(2,1)S(1)}) custom-call(s32[5]{0:T(128)S(1)} %stack.23.flags, s32[2,64]{1,0:T(2,128)} %bitcast.12, f32[2,64]{1,0:T(2,128)} %bitcast.14, bf16[64,3072]{1,0:T(8,128)(2,1)} %tokens.1, bf16[64,3072]{1,0:T(8,128)(2,1)} %cotangent.1), custom_call_target="tpu_custom_call" | custom-call | tf_op jit(solution)/shard_map/dispatch/pallas_call | solution.py:235
  2.7 3.4 %collective-permute-start = (bf16[40,3072]{1,0:T(8,128)(2,1)S(1)}, bf16[40,3072]{1,0:T(8,128)(2,1)S(1)}, u32[]{:S(2)}, u32[]{:S(2)}) collective-permute-start(bf16[40,3072]{1,0:T(8,128)(2,1)S(1)} %get-tuple-element.21), channel_id=1, source_target_pairs={{0,16},{16,32},{32,48},{48,0},{1,17},{17,33},{33,49},{49,1},{2,18}... | collective-permute-start | bytes 737288 | tf_op jit(solution)/shard_map/ppermute | solution.py:259
  6.1 4.3 %collective-permute-start.1 = (bf16[40,3072]{1,0:T(8,128)(2,1)S(1)}, bf16[40,3072]{1,0:T(8,128)(2,1)S(1)}, u32[]{:S(2)}, u32[]{:S(2)}) collective-permute-start(bf16[40,3072]{1,0:T(8,128)(2,1)S(1)} %get-tuple-element.22), channel_id=1, source_target_pairs={{0,32},{16,48},{32,0},{48,16},{1,33},{17,49},{33,1},{49,17},{2,34}... | collective-permute-start | bytes 737288 | tf_op jit(solution)/shard_map/ppermute | solution.py:259
  10.5 3.3 %collective-permute-start.2 = (bf16[40,3072]{1,0:T(8,128)(2,1)S(1)}, bf16[40,3072]{1,0:T(8,128)(2,1)S(1)}, u32[]{:S(2)}, u32[]{:S(2)}) collective-permute-start(bf16[40,3072]{1,0:T(8,128)(2,1)S(1)} %get-tuple-element.23), channel_id=1, source_target_pairs={{0,48},{16,0},{32,16},{48,32},{1,49},{17,1},{33,17},{49,33},{2,50}... | collective-permute-start | bytes 737288 | tf_op jit(solution)/shard_map/ppermute | solution.py:259
  13.8 1.6 collective-permute-done.refs_1_
  15.4 9.4 %collective-permute-done.1.refs_2_ = bf16[40,3072]{1,0:T(8,128)(2,1)S(1)} collective-permute-done((bf16[40,3072]{1,0:T(8,128)(2,1)S(1)}, bf16[40,3072]{1,0:T(8,128)(2,1)S(1)}, u32[]{:S(2)}, u32[]{:S(2)}) %collective-permute-start.1) | collective-permute-done | bytes 245792 | tf_op jit(solution)/shard_map/ppermute | solution.py:259
  24.8 0.4 collective-permute-done.2.refs_3_
  25.2 2.1 %squeeze.1 = (bf16[144,3072]{1,0:T(8,128)(2,1)S(1)}, bf16[8,144,384]{2,1,0:T(8,128)(2,1)}) custom-call(s32[5]{0:T(128)S(1)} %stack.23.flags, bf16[40,3072]{1,0:T(8,128)(2,1)S(1)} %get-tuple-element.20.refs_0_, bf16[40,3072]{1,0:T(8,128)(2,1)S(1)} %collective-permute-done.refs_1_, bf16[40,3072]{1,0:T(8,128)(2,1)S(1)} %collective-permute-done.1.refs_2_, ...), custom_call_target="tpu_custom_call" | custom-call | tf_op jit(solution)/shard_map/squeeze/pallas_call | solution.py:235
  27.3 1.9 %collective-permute-start.3 = (bf16[144,3072]{1,0:T(8,128)(2,1)S(1)}, bf16[144,3072]{1,0:T(8,128)(2,1)S(1)}, u32[]{:S(2)}, u32[]{:S(2)}) collective-permute-start(bf16[144,3072]{1,0:T(8,128)(2,1)S(1)} %get-tuple-element.24.mine), channel_id=1, source_target_pairs={{0,1},{1,0},{2,3},{3,2},{4,5},{5,4},{6,7},{7,6},{8,9},{9,8},{10,11... | collective-permute-start | bytes 2654216 | tf_op jit(solution)/shard_map/ppermute | solution.py:265
  29.3 16.7 %all-to-all-start.2 = ((bf16[8,144,384]{2,1,0:T(8,128)(2,1)}), bf16[8,144,384]{2,1,0:T(8,128)(2,1)S(1)}, u32[]{:S(2)}, u32[]{:S(2)}) async-start(bf16[8,144,384]{2,1,0:T(8,128)(2,1)} %get-tuple-element.29), calls=%async_computation.2 | async-start | bytes 1769472 | tf_op jit(solution)/shard_map/all_to_all | solution.py:306
  46.0 0.0 collective-permute-done.3.other
  46.0 5.1 %expert_front.1.pieces.refs_0_ = bf16[144,1008]{1,0:T(8,128)(2,1)S(1)} custom-call(s32[5]{0:T(128)S(1)} %stack.23.flags, bf16[144,3072]{1,0:T(8,128)(2,1)S(1)} %get-tuple-element.24.mine, bf16[144,3072]{1,0:T(8,128)(2,1)S(1)} %collective-permute-done.3.other, bf16[1,336,3072]{2,1,0:T(8,128)(2,1)} %bitcast.16, bf16[1,336,3072]{2,1,0:T(8,128)(2,1)} %bitcast.18, ...), custom_call_target="tpu_custom_call" | custom-call | tf_op jit(solution)/shard_map/expert_front/pallas_call | solution.py:235
  51.2 0.0 copy-start
  51.2 4.9 %expert_back.1 = (bf16[8,144,384]{2,1,0:T(8,128)(2,1)S(1)}, bf16[8,144,384]{2,1,0:T(8,128)(2,1)S(1)}) custom-call(s32[5]{0:T(128)S(1)} %stack.23.flags, bf16[144,1008]{1,0:T(8,128)(2,1)S(1)} %expert_front.1.pieces.refs_0_, bf16[1,336,3072]{2,1,0:T(8,128)(2,1)} %bitcast.17, bf16[1,336,3072]{2,1,0:T(8,128)(2,1)} %bitcast.19, bf16[1,336,3072]{2,1,0:T(8,128)(2,1)} %down_w.3), custom_call_target="tpu_custom_call" | custom-call | flops 891813888 | bytes 6483456 | tf_op jit(solution)/shard_map/expert_back/pallas_call | solution.py:235
  56.0 2.1 %collective-permute-start.4 = (bf16[8,144,384]{2,1,0:T(8,128)(2,1)S(1)}, bf16[8,144,384]{2,1,0:T(8,128)(2,1)S(1)}, u32[]{:S(2)}, u32[]{:S(2)}) collective-permute-start(bf16[8,144,384]{2,1,0:T(8,128)(2,1)S(1)} %get-tuple-element.26), channel_id=1, source_target_pairs={{0,1},{1,0},{2,3},{3,2},{4,5},{5,4},{6,7},{7,6},{8,9},{9,8},{10,11... | collective-permute-start | bytes 2654216 | tf_op jit(solution)/shard_map/ppermute | solution.py:265
  58.2 2.2 %collective-permute-done.4 = bf16[8,144,384]{2,1,0:T(8,128)(2,1)S(1)} collective-permute-done((bf16[8,144,384]{2,1,0:T(8,128)(2,1)S(1)}, bf16[8,144,384]{2,1,0:T(8,128)(2,1)S(1)}, u32[]{:S(2)}, u32[]{:S(2)}) %collective-permute-start.4) | collective-permute-done | bytes 884768 | tf_op jit(solution)/shard_map/ppermute | solution.py:265
  60.4 1.2 add_convert_fusion
  61.5 10.4 %all-to-all-done.2.mine = bf16[8,144,384]{2,1,0:T(8,128)(2,1)S(1)} async-done(((bf16[8,144,384]{2,1,0:T(8,128)(2,1)}), bf16[8,144,384]{2,1,0:T(8,128)(2,1)S(1)}, u32[]{:S(2)}, u32[]{:S(2)}) %all-to-all-start.2) | async-done | bytes 884768 | tf_op jit(solution)/shard_map/all_to_all | solution.py:306
  71.9 7.9 %all-to-all-start = ((bf16[8,144,384]{2,1,0:T(8,128)(2,1)}), bf16[8,144,384]{2,1,0:T(8,128)(2,1)S(1)}, u32[]{:S(2)}, u32[]{:S(2)}) async-start(bf16[8,144,384]{2,1,0:T(8,128)(2,1)} %add_convert_fusion), calls=%async_computation | async-start | bytes 1769472 | tf_op jit(solution)/shard_map/all_to_all | solution.py:328
  79.8 2.5 %collective-permute-start.6 = (bf16[144,1008]{1,0:T(8,128)(2,1)S(1)}, bf16[144,1008]{1,0:T(8,128)(2,1)S(1)}, u32[]{:S(2)}, u32[]{:S(2)}) collective-permute-start(bf16[144,1008]{1,0:T(8,128)(2,1)S(1)} %expert_front.1.pieces.refs_0_), channel_id=1, source_target_pairs={{0,64},{64,128},{128,192},{192,256},{256,320},{320,384},{384,448},... | collective-permute-start | bytes 870920 | tf_op jit(solution)/shard_map/ppermute | solution.py:253
  82.3 1.9 %collective-permute-start.5 = (bf16[8,144,384]{2,1,0:T(8,128)(2,1)S(1)}, bf16[8,144,384]{2,1,0:T(8,128)(2,1)S(1)}, u32[]{:S(2)}, u32[]{:S(2)}) collective-permute-start(bf16[8,144,384]{2,1,0:T(8,128)(2,1)S(1)} %all-to-all-done.2.mine), channel_id=1, source_target_pairs={{0,1},{1,0},{2,3},{3,2},{4,5},{5,4},{6,7},{7,6},{8,9},{9,8},{10,11... | collective-permute-start | bytes 2654216 | tf_op jit(solution)/shard_map/ppermute | solution.py:265
  84.2 0.0 copy-done
  84.2 4.6 %collective-permute-start.10 = (bf16[144,1008]{1,0:T(8,128)(2,1)S(1)}, bf16[144,1008]{1,0:T(8,128)(2,1)S(1)}, u32[]{:S(2)}, u32[]{:S(2)}) collective-permute-start(bf16[144,1008]{1,0:T(8,128)(2,1)S(1)} %expert_front.1.pieces.refs_0_), channel_id=1, source_target_pairs={{0,448},{64,0},{128,64},{192,128},{256,192},{320,256},{384,320},{4... | collective-permute-start | bytes 870920 | tf_op jit(solution)/shard_map/ppermute | solution.py:253
  88.8 2.5 %collective-permute-done.6.refs_1_ = bf16[144,1008]{1,0:T(8,128)(2,1)S(1)} collective-permute-done((bf16[144,1008]{1,0:T(8,128)(2,1)S(1)}, bf16[144,1008]{1,0:T(8,128)(2,1)S(1)}, u32[]{:S(2)}, u32[]{:S(2)}) %collective-permute-start.6) | collective-permute-done | bytes 290336 | tf_op jit(solution)/shard_map/ppermute | solution.py:253
  91.3 0.0 copy-start.3
  91.3 1.9 %collective-permute-start.7 = (bf16[144,1008]{1,0:T(8,128)(2,1)S(1)}, bf16[144,1008]{1,0:T(8,128)(2,1)S(1)}, u32[]{:S(2)}, u32[]{:S(2)}) collective-permute-start(bf16[144,1008]{1,0:T(8,128)(2,1)S(1)} %collective-permute-done.6.refs_1_), channel_id=1, source_target_pairs={{0,64},{64,128},{128,192},{192,256},{256,320},{320,384},{384,448},... | collective-permute-start | bytes 870920 | tf_op jit(solution)/shard_map/ppermute | solution.py:253
  93.2 2.5 %collective-permute-done.10.refs_2_ = bf16[144,1008]{1,0:T(8,128)(2,1)S(1)} collective-permute-done((bf16[144,1008]{1,0:T(8,128)(2,1)S(1)}, bf16[144,1008]{1,0:T(8,128)(2,1)S(1)}, u32[]{:S(2)}, u32[]{:S(2)}) %collective-permute-start.10) | collective-permute-done | bytes 290336 | tf_op jit(solution)/shard_map/ppermute | solution.py:253
  95.7 0.0 copy-start.4
  95.7 5.6 %collective-permute-start.11 = (bf16[144,1008]{1,0:T(8,128)(2,1)S(1)}, bf16[144,1008]{1,0:T(8,128)(2,1)S(1)}, u32[]{:S(2)}, u32[]{:S(2)}) collective-permute-start(bf16[144,1008]{1,0:T(8,128)(2,1)S(1)} %collective-permute-done.10.refs_2_), channel_id=1, source_target_pairs={{0,448},{64,0},{128,64},{192,128},{256,192},{320,256},{384,320},{4... | collective-permute-start | bytes 870920 | tf_op jit(solution)/shard_map/ppermute | solution.py:253
  101.3 0.6 collective-permute-done.7.refs_3_
  101.9 0.0 copy-start.5
  101.9 1.9 %collective-permute-start.8 = (bf16[144,1008]{1,0:T(8,128)(2,1)S(1)}, bf16[144,1008]{1,0:T(8,128)(2,1)S(1)}, u32[]{:S(2)}, u32[]{:S(2)}) collective-permute-start(bf16[144,1008]{1,0:T(8,128)(2,1)S(1)} %collective-permute-done.7.refs_3_), channel_id=1, source_target_pairs={{0,64},{64,128},{128,192},{192,256},{256,320},{320,384},{384,448},... | collective-permute-start | bytes 870920 | tf_op jit(solution)/shard_map/ppermute | solution.py:253
  103.8 3.6 %collective-permute-done.11.refs_4_ = bf16[144,1008]{1,0:T(8,128)(2,1)S(1)} collective-permute-done((bf16[144,1008]{1,0:T(8,128)(2,1)S(1)}, bf16[144,1008]{1,0:T(8,128)(2,1)S(1)}, u32[]{:S(2)}, u32[]{:S(2)}) %collective-permute-start.11) | collective-permute-done | bytes 290336 | tf_op jit(solution)/shard_map/ppermute | solution.py:253
  107.4 0.0 copy-start.6
  107.4 5.6 %collective-permute-start.12 = (bf16[144,1008]{1,0:T(8,128)(2,1)S(1)}, bf16[144,1008]{1,0:T(8,128)(2,1)S(1)}, u32[]{:S(2)}, u32[]{:S(2)}) collective-permute-start(bf16[144,1008]{1,0:T(8,128)(2,1)S(1)} %collective-permute-done.11.refs_4_), channel_id=1, source_target_pairs={{0,448},{64,0},{128,64},{192,128},{256,192},{320,256},{384,320},{4... | collective-permute-start | bytes 870920 | tf_op jit(solution)/shard_map/ppermute | solution.py:253
  113.0 0.0 collective-permute-done.8.refs_5_
  113.0 0.0 copy-start.7
  113.0 1.9 %collective-permute-start.9 = (bf16[144,1008]{1,0:T(8,128)(2,1)S(1)}, bf16[144,1008]{1,0:T(8,128)(2,1)S(1)}, u32[]{:S(2)}, u32[]{:S(2)}) collective-permute-start(bf16[144,1008]{1,0:T(8,128)(2,1)S(1)} %collective-permute-done.8.refs_5_), channel_id=1, source_target_pairs={{0,64},{64,128},{128,192},{192,256},{256,320},{320,384},{384,448},... | collective-permute-start | bytes 870920 | tf_op jit(solution)/shard_map/ppermute | solution.py:253
  115.0 3.3 %collective-permute-done.12.refs_6_ = bf16[144,1008]{1,0:T(8,128)(2,1)S(1)} collective-permute-done((bf16[144,1008]{1,0:T(8,128)(2,1)S(1)}, bf16[144,1008]{1,0:T(8,128)(2,1)S(1)}, u32[]{:S(2)}, u32[]{:S(2)}) %collective-permute-start.12) | collective-permute-done | bytes 290336 | tf_op jit(solution)/shard_map/ppermute | solution.py:253
  118.3 0.0 copy-start.8
  118.3 0.0 collective-permute-done.5.other
  118.3 0.0 copy-done.3
  118.3 0.0 copy-done.4
  118.3 0.0 copy-done.5
  118.3 0.0 copy-done.6
  118.3 0.0 copy-done.7
  118.3 0.7 copy-done.8
  119.0 3.7 %weight_grads.1.total = f32[384,1008]{1,0:T(8,128)S(1)} custom-call(s32[5]{0:T(128)S(1)} %stack.23.flags, bf16[8,144,384]{2,1,0:T(8,128)(2,1)S(1)} %all-to-all-done.2.mine, bf16[8,144,384]{2,1,0:T(8,128)(2,1)S(1)} %collective-permute-done.5.other, bf16[144,1008]{1,0:T(8,128)(2,1)} %copy-done, bf16[144,1008]{1,0:T(8,128)(2,1)} %copy-done.3, ...), custom_call_target="tpu_custom_call" | custom-call | flops 780337152 | bytes 3801600 | tf_op jit(solution)/shard_map/weight_grads/pallas_call | solution.py:235
  122.7 0.9 collective-permute-done.9.piece
  123.6 1.3 weight_grads_last.1
  124.9 0.0 copy-start.1
  124.9 0.0 copy-start.2
  124.9 7.0 %collective-permute-start.13 = (bf16[192,1008]{1,0:T(8,128)(2,1)S(1)}, bf16[192,1008]{1,0:T(8,128)(2,1)S(1)}, u32[]{:S(2)}, u32[]{:S(2)}) collective-permute-start(bf16[192,1008]{1,0:T(8,128)(2,1)S(1)} %get-tuple-element.31), channel_id=1, source_target_pairs={{0,512},{512,0},{1,513},{513,1},{2,514},{514,2},{3,515},{515,3},{4... | collective-permute-start | bytes 1161224 | tf_op jit(solution)/shard_map/ppermute | solution.py:265
  131.9 0.0 all-to-all-done.blocks
  131.9 1.5 add_up.1
  133.4 7.0 %all-to-all-start.1 = ((bf16[4,40,384]{2,1,0:T(8,128)(2,1)}), bf16[4,40,384]{2,1,0:T(8,128)(2,1)S(1)}, u32[]{:S(2)}, u32[]{:S(2)}) async-start(bf16[4,40,384]{2,1,0:T(8,128)(2,1)} %add_up.1), calls=%async_computation.1 | async-start | bytes 245760 | tf_op jit(solution)/shard_map/all_to_all | solution.py:330
  140.4 0.0 collective-permute-done.13.got
  140.4 1.1 finish.1
  141.4 12.9 %all-to-all-done.1 = bf16[4,40,384]{2,1,0:T(8,128)(2,1)S(1)} async-done(((bf16[4,40,384]{2,1,0:T(8,128)(2,1)}), bf16[4,40,384]{2,1,0:T(8,128)(2,1)S(1)}, u32[]{:S(2)}, u32[]{:S(2)}) %all-to-all-start.1) | async-done | bytes 122912 | tf_op jit(solution)/shard_map/all_to_all | solution.py:330
  154.4 0.0 copy-done.1
  154.4 0.0 copy-done.2
  154.4 1.1 combine.1
Async XLA Ops:
  2.7 12.6 %collective-permute-start = (bf16[40,3072]{1,0:T(8,128)(2,1)S(1)}, bf16[40,3072]{1,0:T(8,128)(2,1)S(1)}, u32[]{:S(2)}, u32[]{:S(2)}) collective-permute-start(bf16[40,3072]{1,0:T(8,128)(2,1)S(1)} %get-tuple-element.21), channel_id=1, source_target_pairs={{0,16},{16,32},{32,48},{48,0},{1,17},{17,33},{33,49},{49,1},{2,18}... | collective-permute-start | bytes 737288 | tf_op jit(solution)/shard_map/ppermute | solution.py:259
  6.1 18.7 %collective-permute-start.1 = (bf16[40,3072]{1,0:T(8,128)(2,1)S(1)}, bf16[40,3072]{1,0:T(8,128)(2,1)S(1)}, u32[]{:S(2)}, u32[]{:S(2)}) collective-permute-start(bf16[40,3072]{1,0:T(8,128)(2,1)S(1)} %get-tuple-element.22), channel_id=1, source_target_pairs={{0,32},{16,48},{32,0},{48,16},{1,33},{17,49},{33,1},{49,17},{2,34}... | collective-permute-start | bytes 737288 | tf_op jit(solution)/shard_map/ppermute | solution.py:259
  10.5 14.8 %collective-permute-start.2 = (bf16[40,3072]{1,0:T(8,128)(2,1)S(1)}, bf16[40,3072]{1,0:T(8,128)(2,1)S(1)}, u32[]{:S(2)}, u32[]{:S(2)}) collective-permute-start(bf16[40,3072]{1,0:T(8,128)(2,1)S(1)} %get-tuple-element.23), channel_id=1, source_target_pairs={{0,48},{16,0},{32,16},{48,32},{1,49},{17,1},{33,17},{49,33},{2,50}... | collective-permute-start | bytes 737288 | tf_op jit(solution)/shard_map/ppermute | solution.py:259
  27.3 18.7 %collective-permute-start.3 = (bf16[144,3072]{1,0:T(8,128)(2,1)S(1)}, bf16[144,3072]{1,0:T(8,128)(2,1)S(1)}, u32[]{:S(2)}, u32[]{:S(2)}) collective-permute-start(bf16[144,3072]{1,0:T(8,128)(2,1)S(1)} %get-tuple-element.24.mine), channel_id=1, source_target_pairs={{0,1},{1,0},{2,3},{3,2},{4,5},{5,4},{6,7},{7,6},{8,9},{9,8},{10,11... | collective-permute-start | bytes 2654216 | tf_op jit(solution)/shard_map/ppermute | solution.py:265
  29.3 42.6 %all-to-all-start.2 = ((bf16[8,144,384]{2,1,0:T(8,128)(2,1)}), bf16[8,144,384]{2,1,0:T(8,128)(2,1)S(1)}, u32[]{:S(2)}, u32[]{:S(2)}) async-start(bf16[8,144,384]{2,1,0:T(8,128)(2,1)} %get-tuple-element.29), calls=%async_computation.2 | async-start | bytes 1769472 | tf_op jit(solution)/shard_map/all_to_all | solution.py:306
  51.2 33.0 %copy-start = (bf16[144,1008]{1,0:T(8,128)(2,1)}, bf16[144,1008]{1,0:T(8,128)(2,1)S(1)}, u32[]{:S(2)}) copy-start(bf16[144,1008]{1,0:T(8,128)(2,1)S(1)} %expert_front.1.pieces.refs_0_) | copy-start | bytes 870916
  56.0 4.3 %collective-permute-start.4 = (bf16[8,144,384]{2,1,0:T(8,128)(2,1)S(1)}, bf16[8,144,384]{2,1,0:T(8,128)(2,1)S(1)}, u32[]{:S(2)}, u32[]{:S(2)}) collective-permute-start(bf16[8,144,384]{2,1,0:T(8,128)(2,1)S(1)} %get-tuple-element.26), channel_id=1, source_target_pairs={{0,1},{1,0},{2,3},{3,2},{4,5},{5,4},{6,7},{7,6},{8,9},{9,8},{10,11... | collective-permute-start | bytes 2654216 | tf_op jit(solution)/shard_map/ppermute | solution.py:265
  71.9 60.0 %all-to-all-start = ((bf16[8,144,384]{2,1,0:T(8,128)(2,1)}), bf16[8,144,384]{2,1,0:T(8,128)(2,1)S(1)}, u32[]{:S(2)}, u32[]{:S(2)}) async-start(bf16[8,144,384]{2,1,0:T(8,128)(2,1)} %add_convert_fusion), calls=%async_computation | async-start | bytes 1769472 | tf_op jit(solution)/shard_map/all_to_all | solution.py:328
  79.8 11.5 %collective-permute-start.6 = (bf16[144,1008]{1,0:T(8,128)(2,1)S(1)}, bf16[144,1008]{1,0:T(8,128)(2,1)S(1)}, u32[]{:S(2)}, u32[]{:S(2)}) collective-permute-start(bf16[144,1008]{1,0:T(8,128)(2,1)S(1)} %expert_front.1.pieces.refs_0_), channel_id=1, source_target_pairs={{0,64},{64,128},{128,192},{192,256},{256,320},{320,384},{384,448},... | collective-permute-start | bytes 870920 | tf_op jit(solution)/shard_map/ppermute | solution.py:253
  82.3 36.0 %collective-permute-start.5 = (bf16[8,144,384]{2,1,0:T(8,128)(2,1)S(1)}, bf16[8,144,384]{2,1,0:T(8,128)(2,1)S(1)}, u32[]{:S(2)}, u32[]{:S(2)}) collective-permute-start(bf16[8,144,384]{2,1,0:T(8,128)(2,1)S(1)} %all-to-all-done.2.mine), channel_id=1, source_target_pairs={{0,1},{1,0},{2,3},{3,2},{4,5},{5,4},{6,7},{7,6},{8,9},{9,8},{10,11... | collective-permute-start | bytes 2654216 | tf_op jit(solution)/shard_map/ppermute | solution.py:265
  84.2 11.5 %collective-permute-start.10 = (bf16[144,1008]{1,0:T(8,128)(2,1)S(1)}, bf16[144,1008]{1,0:T(8,128)(2,1)S(1)}, u32[]{:S(2)}, u32[]{:S(2)}) collective-permute-start(bf16[144,1008]{1,0:T(8,128)(2,1)S(1)} %expert_front.1.pieces.refs_0_), channel_id=1, source_target_pairs={{0,448},{64,0},{128,64},{192,128},{256,192},{320,256},{384,320},{4... | collective-permute-start | bytes 870920 | tf_op jit(solution)/shard_map/ppermute | solution.py:253
  91.3 27.0 %copy-start.3 = (bf16[144,1008]{1,0:T(8,128)(2,1)}, bf16[144,1008]{1,0:T(8,128)(2,1)S(1)}, u32[]{:S(2)}) copy-start(bf16[144,1008]{1,0:T(8,128)(2,1)S(1)} %collective-permute-done.6.refs_1_) | copy-start | bytes 870916
  91.3 10.6 %collective-permute-start.7 = (bf16[144,1008]{1,0:T(8,128)(2,1)S(1)}, bf16[144,1008]{1,0:T(8,128)(2,1)S(1)}, u32[]{:S(2)}, u32[]{:S(2)}) collective-permute-start(bf16[144,1008]{1,0:T(8,128)(2,1)S(1)} %collective-permute-done.6.refs_1_), channel_id=1, source_target_pairs={{0,64},{64,128},{128,192},{192,256},{256,320},{320,384},{384,448},... | collective-permute-start | bytes 870920 | tf_op jit(solution)/shard_map/ppermute | solution.py:253
  95.7 22.6 %copy-start.4 = (bf16[144,1008]{1,0:T(8,128)(2,1)}, bf16[144,1008]{1,0:T(8,128)(2,1)S(1)}, u32[]{:S(2)}) copy-start(bf16[144,1008]{1,0:T(8,128)(2,1)S(1)} %collective-permute-done.10.refs_2_) | copy-start | bytes 870916
  95.7 11.7 %collective-permute-start.11 = (bf16[144,1008]{1,0:T(8,128)(2,1)S(1)}, bf16[144,1008]{1,0:T(8,128)(2,1)S(1)}, u32[]{:S(2)}, u32[]{:S(2)}) collective-permute-start(bf16[144,1008]{1,0:T(8,128)(2,1)S(1)} %collective-permute-done.10.refs_2_), channel_id=1, source_target_pairs={{0,448},{64,0},{128,64},{192,128},{256,192},{320,256},{384,320},{4... | collective-permute-start | bytes 870920 | tf_op jit(solution)/shard_map/ppermute | solution.py:253
  101.9 16.4 %copy-start.5 = (bf16[144,1008]{1,0:T(8,128)(2,1)}, bf16[144,1008]{1,0:T(8,128)(2,1)S(1)}, u32[]{:S(2)}) copy-start(bf16[144,1008]{1,0:T(8,128)(2,1)S(1)} %collective-permute-done.7.refs_3_) | copy-start | bytes 870916
  101.9 11.2 %collective-permute-start.8 = (bf16[144,1008]{1,0:T(8,128)(2,1)S(1)}, bf16[144,1008]{1,0:T(8,128)(2,1)S(1)}, u32[]{:S(2)}, u32[]{:S(2)}) collective-permute-start(bf16[144,1008]{1,0:T(8,128)(2,1)S(1)} %collective-permute-done.7.refs_3_), channel_id=1, source_target_pairs={{0,64},{64,128},{128,192},{192,256},{256,320},{320,384},{384,448},... | collective-permute-start | bytes 870920 | tf_op jit(solution)/shard_map/ppermute | solution.py:253
  107.4 10.9 %copy-start.6 = (bf16[144,1008]{1,0:T(8,128)(2,1)}, bf16[144,1008]{1,0:T(8,128)(2,1)S(1)}, u32[]{:S(2)}) copy-start(bf16[144,1008]{1,0:T(8,128)(2,1)S(1)} %collective-permute-done.11.refs_4_) | copy-start | bytes 870916
  107.4 10.8 %collective-permute-start.12 = (bf16[144,1008]{1,0:T(8,128)(2,1)S(1)}, bf16[144,1008]{1,0:T(8,128)(2,1)S(1)}, u32[]{:S(2)}, u32[]{:S(2)}) collective-permute-start(bf16[144,1008]{1,0:T(8,128)(2,1)S(1)} %collective-permute-done.11.refs_4_), channel_id=1, source_target_pairs={{0,448},{64,0},{128,64},{192,128},{256,192},{320,256},{384,320},{4... | collective-permute-start | bytes 870920 | tf_op jit(solution)/shard_map/ppermute | solution.py:253
  113.0 5.3 %copy-start.7 = (bf16[144,1008]{1,0:T(8,128)(2,1)}, bf16[144,1008]{1,0:T(8,128)(2,1)S(1)}, u32[]{:S(2)}) copy-start(bf16[144,1008]{1,0:T(8,128)(2,1)S(1)} %collective-permute-done.8.refs_5_) | copy-start | bytes 870916
  113.0 10.6 %collective-permute-start.9 = (bf16[144,1008]{1,0:T(8,128)(2,1)S(1)}, bf16[144,1008]{1,0:T(8,128)(2,1)S(1)}, u32[]{:S(2)}, u32[]{:S(2)}) collective-permute-start(bf16[144,1008]{1,0:T(8,128)(2,1)S(1)} %collective-permute-done.8.refs_5_), channel_id=1, source_target_pairs={{0,64},{64,128},{128,192},{192,256},{256,320},{320,384},{384,448},... | collective-permute-start | bytes 870920 | tf_op jit(solution)/shard_map/ppermute | solution.py:253
  118.3 0.7 copy-start.8
  124.9 29.5 %copy-start.1 = (s32[64,2]{0,1:T(2,128)S(1)}, s32[64,2]{0,1:T(2,128)}, u32[]{:S(2)}) copy-start(s32[64,2]{0,1:T(2,128)} %param.9) | copy-start | bytes 1540
  124.9 29.5 %copy-start.2 = (f32[64,2]{0,1:T(2,128)S(1)}, f32[64,2]{0,1:T(2,128)}, u32[]{:S(2)}) copy-start(f32[64,2]{0,1:T(2,128)} %param.10) | copy-start | bytes 1540
  124.9 15.5 %collective-permute-start.13 = (bf16[192,1008]{1,0:T(8,128)(2,1)S(1)}, bf16[192,1008]{1,0:T(8,128)(2,1)S(1)}, u32[]{:S(2)}, u32[]{:S(2)}) collective-permute-start(bf16[192,1008]{1,0:T(8,128)(2,1)S(1)} %get-tuple-element.31), channel_id=1, source_target_pairs={{0,512},{512,0},{1,513},{513,1},{2,514},{514,2},{3,515},{515,3},{4... | collective-permute-start | bytes 1161224 | tf_op jit(solution)/shard_map/ppermute | solution.py:265
  133.4 21.0 %all-to-all-start.1 = ((bf16[4,40,384]{2,1,0:T(8,128)(2,1)}), bf16[4,40,384]{2,1,0:T(8,128)(2,1)S(1)}, u32[]{:S(2)}, u32[]{:S(2)}) async-start(bf16[4,40,384]{2,1,0:T(8,128)(2,1)} %add_up.1), calls=%async_computation.1 | async-start | bytes 245760 | tf_op jit(solution)/shard_map/all_to_all | solution.py:330

commit v3 on v2

--- a/solution.py
+++ b/solution.py
@@ -7,7 +7,8 @@
 
 CAP = 36
 SLOT = 40
-SOON = (0, 1, 7, 2, 6, 3, 5)
+SOON = (0, 1, 7, 2, 6, 3)
+LAST = (5, 4)
 CUTS = 3
 N_Z = 8
 N_Y = 8
@@ -147,9 +148,11 @@
 ):
     copies = fetch_rows(((down_w, down_v), (gate_w, gate_v), (up_w, up_v)), sems)
     ff = pieces.shape[1] // 3
-    hidden = pieces[:, :ff]
-    gate_grad = pieces[:, ff : 2 * ff]
-    up_grad = pieces[:, 2 * ff :]
+    matrix = squeeze_matrix(pieces.shape[0], N_XL * SLOT)
+    held = dot(matrix, pieces[...], ((0,), (0,))).astype(BF16)
+    hidden = held[:, :ff]
+    gate_grad = held[:, ff : 2 * ff]
+    up_grad = held[:, 2 * ff :]
     wait_all(copies[0])
     out = dot(hidden, down_v[0]).astype(BF16)
     wait_all(copies[1])
@@ -161,7 +164,10 @@
         for i in range(N_Y):
             for j, ref in ((2 * i, even), (2 * i + 1, odd)):
                 at = slice(part * j, part * (j + 1))
-                ref[i] = jnp.concatenate([out[:, at], back[:, at]], axis=1)
+                both = jnp.concatenate([out[:, at], back[:, at]], axis=1)
+                for k in range(N_XL):
+                    source = lax.rem(flags[3] + (N_XL - k), N_XL)
+                    ref[i, source] = both[SLOT * k : SLOT * (k + 1)]
 
     @pl.when(flags[0] == 0)
     def _():
@@ -172,20 +178,16 @@
         write(send_out, keep_out)
 
 
-def add_up(flags, blocks, rows_out):
-    total = blocks[0].astype(F32)
-    for i in range(1, N_Y):
-        total = total + blocks[i].astype(F32)
-    spread_out = squeeze_matrix(total.shape[0], N_XL * SLOT)
-    rows = dot(spread_out, total.astype(BF16), ((0,), (0,))).astype(BF16)
-    for k in range(N_XL):
-        rows_out[lax.rem(flags[3] + (N_XL - k), N_XL)] = rows[SLOT * k : SLOT * (k + 1)]
-
-
-def combine(routes, gates, rows, layer_out, grad_out):
+def combine(routes, gates, blocks, layer_out, grad_out):
     pick, gate = picks(routes[...], gates[...])
     part = layer_out.shape[1]
-    both = rows[...]
+    experts = []
+    for e in range(N_XL):
+        total = blocks[e].astype(F32)
+        for i in range(1, N_Y):
+            total = total + blocks[N_XL * i + e].astype(F32)
+        experts.append(total.astype(BF16))
+    both = jnp.concatenate(experts, axis=0)
     layer_out[...] = dot(gate, both[:, :part].astype(F32), ((0,), (0,)), HIGHEST).astype(BF16)
     grad_out[...] = dot(pick.astype(BF16), both[:, part:], ((0,), (0,))).astype(BF16)
 
@@ -211,8 +213,10 @@
     total_out[...] = grads_of(flags, mine, other, SOON, held[...])
 
 
-def weight_grads_last(flags, mine, other, piece, total, keep_out, send_out):
-    both = total[...] + grads_of(flags, mine, other, (N_Z // 2,), piece[...])
+def weight_grads_last(flags, mine, other, total, *refs):
+    *pieces, keep_out, send_out = refs
+    rows = jnp.concatenate([piece[...] for piece in pieces], axis=0)
+    both = total[...] + grads_of(flags, mine, other, LAST, rows)
     part = keep_out.shape[0]
     keep_out[...] = both[:part]
     send_out[...] = both[part:].astype(BF16)
@@ -309,7 +313,7 @@
     )
     keep, send = call(
         expert_back,
-        [((N_Y, rows, 2 * part), BF16)] * 2,
+        [((N_Y, N_XL, SLOT, 2 * part), BF16)] * 2,
         [flags],
         pieces,
         far=weights,
@@ -325,16 +329,16 @@
     found[N_Z // 2] = shift(found[N_Z // 2 - 1], 1)
     cols_other = swap(cols, "c")
 
-    blocks = lax.all_to_all(summed, "y", split_axis=0, concat_axis=0, tiled=True)
-    (back,) = call(add_up, [((N_XL, SLOT, 2 * part), BF16)], [flags], blocks)
-    back = lax.all_to_all(back, "xl", split_axis=0, concat_axis=0, tiled=True)
+    summed, _ = lax.optimization_barrier((summed, (found[1], found[7])))
+    blocks = lax.all_to_all(
+        summed.reshape(N_Y * N_XL, SLOT, 2 * part),
+        ("y", "xl"),
+        split_axis=0,
+        concat_axis=0,
+        tiled=True,
+    )
     layer_out, token_grad = call(
-        combine,
-        [((tok_count, part), BF16)] * 2,
-        [],
-        routes,
-        gates,
-        back.reshape(slots, 2 * part),
+        combine, [((tok_count, part), BF16)] * 2, [], routes, gates, blocks
     )
 
     (total,) = call(
@@ -356,8 +360,8 @@
         [flags],
         cols,
         cols_other,
-        found[N_Z // 2],
         total,
+        *[found[k] for k in LAST],
     )
     grad_gate, grad_up, grad_down = call(
         finish, [((1, part, ff), F32)] * 3, [], kept, swap(given, "xh")

time: 156 us -> 155 us (level)
  the two profiles are of different devices: /device:TPU:16 before, /device:TPU:14 now
where the time goes in v3:
time: 155 us; the launch traced here: 154 us
  starting transfers between devices  71 us (46%)
  waiting for transfers between devices  59.6 us (38%)
  Pallas kernels  21.5 us (14%)
    ppermute x7, waiting for transfers between devices, shift(): return lax.ppermute(value, 'z', [(i, (i + by) % N_Z) for i in range(N_Z)])  24.4 us
    ppermute x7, starting transfers between devices, shift(): return lax.ppermute(value, 'z', [(i, (i + by) % N_Z) for i in range(N_Z)])  23.1 us
    pallas_call x8, Pallas kernels, call(): pl.pallas_call(body, out_shape=[jax.ShapeDtypeStruct(s, t) if i < len(out...  21.5 us
    ppermute x4, waiting for transfers between devices, swap(): return lax.ppermute(value, axis, [(0, 1), (1, 0)])  19 us
    all_to_all x1, starting transfers between devices, on_device(): cols = lax.all_to_all(cols, 'z', split_axis=0, concat_axis=0, tiled=True)  16.7 us
    ppermute x3, waiting for transfers between devices, spread(): lax.ppermute(parts[k], axis, [(i, (i + forward * k) % count) for i in ran...  16.2 us
    all_to_all x1, starting transfers between devices, on_device(): lax.all_to_all(summed.reshape(N_Y * N_XL, SLOT, 2 * part), ('y', 'xl'), s...  11.9 us
    ppermute x3, starting transfers between devices, spread(): lax.ppermute(parts[k], axis, [(i, (i + forward * k) % count) for i in ran...  10.1 us
  transfers between devices with their start and end apart: 16, of which 7 were waited for; matrix products, arithmetic and copies ran while one was open for 1% of the time, Pallas kernels for 11%

profile of v3, /device:TPU:14, one launch (start us, length us, event | category | flops | bytes accessed | tf_op | source)
XLA Modules:
  0.0 154.3 jit_solution(2120026111587914946)
XLA Ops:
  0.6 0.1 stack.23.flags
  0.7 2.0 %dispatch.1 = (bf16[40,3072]{1,0:T(8,128)(2,1)S(1)}, bf16[40,3072]{1,0:T(8,128)(2,1)S(1)}, bf16[40,3072]{1,0:T(8,128)(2,1)S(1)}, bf16[40,3072]{1,0:T(8,128)(2,1)S(1)}) custom-call(s32[5]{0:T(128)S(1)} %stack.23.flags, s32[2,64]{1,0:T(2,128)} %bitcast.11, f32[2,64]{1,0:T(2,128)} %bitcast.13, bf16[64,3072]{1,0:T(8,128)(2,1)} %tokens.1, bf16[64,3072]{1,0:T(8,128)(2,1)} %cotangent.1), custom_call_target="tpu_custom_call" | custom-call | tf_op jit(solution)/shard_map/dispatch/pallas_call | solution.py:239
  2.7 5.1 %collective-permute-start = (bf16[40,3072]{1,0:T(8,128)(2,1)S(1)}, bf16[40,3072]{1,0:T(8,128)(2,1)S(1)}, u32[]{:S(2)}, u32[]{:S(2)}) collective-permute-start(bf16[40,3072]{1,0:T(8,128)(2,1)S(1)} %get-tuple-element.22), channel_id=1, source_target_pairs={{0,16},{16,32},{32,48},{48,0},{1,17},{17,33},{33,49},{49,1},{2,18}... | collective-permute-start | bytes 737288 | tf_op jit(solution)/shard_map/ppermute | solution.py:263
  7.8 1.9 %collective-permute-start.1 = (bf16[40,3072]{1,0:T(8,128)(2,1)S(1)}, bf16[40,3072]{1,0:T(8,128)(2,1)S(1)}, u32[]{:S(2)}, u32[]{:S(2)}) collective-permute-start(bf16[40,3072]{1,0:T(8,128)(2,1)S(1)} %get-tuple-element.23), channel_id=1, source_target_pairs={{0,32},{16,48},{32,0},{48,16},{1,33},{17,49},{33,1},{49,17},{2,34}... | collective-permute-start | bytes 737288 | tf_op jit(solution)/shard_map/ppermute | solution.py:263
  9.7 3.1 %collective-permute-start.2 = (bf16[40,3072]{1,0:T(8,128)(2,1)S(1)}, bf16[40,3072]{1,0:T(8,128)(2,1)S(1)}, u32[]{:S(2)}, u32[]{:S(2)}) collective-permute-start(bf16[40,3072]{1,0:T(8,128)(2,1)S(1)} %get-tuple-element.24), channel_id=1, source_target_pairs={{0,48},{16,0},{32,16},{48,32},{1,49},{17,1},{33,17},{49,33},{2,50}... | collective-permute-start | bytes 737288 | tf_op jit(solution)/shard_map/ppermute | solution.py:263
  12.8 1.7 %collective-permute-done.refs_1_ = bf16[40,3072]{1,0:T(8,128)(2,1)S(1)} collective-permute-done((bf16[40,3072]{1,0:T(8,128)(2,1)S(1)}, bf16[40,3072]{1,0:T(8,128)(2,1)S(1)}, u32[]{:S(2)}, u32[]{:S(2)}) %collective-permute-start) | collective-permute-done | bytes 245792 | tf_op jit(solution)/shard_map/ppermute | solution.py:263
  14.5 14.5 %collective-permute-done.1.refs_2_ = bf16[40,3072]{1,0:T(8,128)(2,1)S(1)} collective-permute-done((bf16[40,3072]{1,0:T(8,128)(2,1)S(1)}, bf16[40,3072]{1,0:T(8,128)(2,1)S(1)}, u32[]{:S(2)}, u32[]{:S(2)}) %collective-permute-start.1) | collective-permute-done | bytes 245792 | tf_op jit(solution)/shard_map/ppermute | solution.py:263
  29.0 0.0 collective-permute-done.2.refs_3_
  29.0 2.1 %squeeze.1 = (bf16[144,3072]{1,0:T(8,128)(2,1)S(1)}, bf16[8,144,384]{2,1,0:T(8,128)(2,1)}) custom-call(s32[5]{0:T(128)S(1)} %stack.23.flags, bf16[40,3072]{1,0:T(8,128)(2,1)S(1)} %get-tuple-element.21.refs_0_, bf16[40,3072]{1,0:T(8,128)(2,1)S(1)} %collective-permute-done.refs_1_, bf16[40,3072]{1,0:T(8,128)(2,1)S(1)} %collective-permute-done.1.refs_2_, ...), custom_call_target="tpu_custom_call" | custom-call | tf_op jit(solution)/shard_map/squeeze/pallas_call | solution.py:239
  31.1 1.9 %collective-permute-start.3 = (bf16[144,3072]{1,0:T(8,128)(2,1)S(1)}, bf16[144,3072]{1,0:T(8,128)(2,1)S(1)}, u32[]{:S(2)}, u32[]{:S(2)}) collective-permute-start(bf16[144,3072]{1,0:T(8,128)(2,1)S(1)} %get-tuple-element.25.mine), channel_id=1, source_target_pairs={{0,1},{1,0},{2,3},{3,2},{4,5},{5,4},{6,7},{7,6},{8,9},{9,8},{10,11... | collective-permute-start | bytes 2654216 | tf_op jit(solution)/shard_map/ppermute | solution.py:269
  33.1 16.7 %all-to-all-start.1 = ((bf16[8,144,384]{2,1,0:T(8,128)(2,1)}), bf16[8,144,384]{2,1,0:T(8,128)(2,1)S(1)}, u32[]{:S(2)}, u32[]{:S(2)}) async-start(bf16[8,144,384]{2,1,0:T(8,128)(2,1)} %get-tuple-element.31), calls=%async_computation.1 | async-start | bytes 1769472 | tf_op jit(solution)/shard_map/all_to_all | solution.py:310
  49.8 0.0 collective-permute-done.3.other
  49.8 5.1 %expert_front.1.pieces.refs_0_ = bf16[144,1008]{1,0:T(8,128)(2,1)S(1)} custom-call(s32[5]{0:T(128)S(1)} %stack.23.flags, bf16[144,3072]{1,0:T(8,128)(2,1)S(1)} %get-tuple-element.25.mine, bf16[144,3072]{1,0:T(8,128)(2,1)S(1)} %collective-permute-done.3.other, bf16[1,336,3072]{2,1,0:T(8,128)(2,1)} %bitcast.15, bf16[1,336,3072]{2,1,0:T(8,128)(2,1)} %bitcast.17, ...), custom_call_target="tpu_custom_call" | custom-call | tf_op jit(solution)/shard_map/expert_front/pallas_call | solution.py:239
  54.9 0.0 copy-start
  54.9 5.0 %expert_back.1 = (bf16[8,4,40,384]{3,2,1,0:T(8,128)(2,1)S(1)}, bf16[8,4,40,384]{3,2,1,0:T(8,128)(2,1)S(1)}) custom-call(s32[5]{0:T(128)S(1)} %stack.23.flags, bf16[144,1008]{1,0:T(8,128)(2,1)S(1)} %expert_front.1.pieces.refs_0_, bf16[1,336,3072]{2,1,0:T(8,128)(2,1)} %bitcast.16, bf16[1,336,3072]{2,1,0:T(8,128)(2,1)} %bitcast.18, bf16[1,336,3072]{2,1,0:T(8,128)(2,1)} %down_w.3), custom_call_target="tpu_custom_call" | custom-call | flops 891813888 | bytes 6483456 | tf_op jit(solution)/shard_map/expert_back/pallas_call | solution.py:239
  60.0 2.1 %collective-permute-start.4 = (bf16[8,4,40,384]{3,2,1,0:T(8,128)(2,1)S(1)}, bf16[8,4,40,384]{3,2,1,0:T(8,128)(2,1)S(1)}, u32[]{:S(2)}, u32[]{:S(2)}) collective-permute-start(bf16[8,4,40,384]{3,2,1,0:T(8,128)(2,1)S(1)} %get-tuple-element.27), channel_id=1, source_target_pairs={{0,1},{1,0},{2,3},{3,2},{4,5},{5,4},{6,7},{7,6},{8,9},{9,8},{10,11... | collective-permute-start | bytes 2949128 | tf_op jit(solution)/shard_map/ppermute | solution.py:269
  62.1 3.7 %collective-permute-start.5 = (bf16[144,1008]{1,0:T(8,128)(2,1)S(1)}, bf16[144,1008]{1,0:T(8,128)(2,1)S(1)}, u32[]{:S(2)}, u32[]{:S(2)}) collective-permute-start(bf16[144,1008]{1,0:T(8,128)(2,1)S(1)} %expert_front.1.pieces.refs_0_), channel_id=1, source_target_pairs={{0,64},{64,128},{128,192},{192,256},{256,320},{320,384},{384,448},... | collective-permute-start | bytes 870920 | tf_op jit(solution)/shard_map/ppermute | solution.py:257
  65.8 0.0 copy-done
  65.9 3.3 %collective-permute-start.6 = (bf16[144,1008]{1,0:T(8,128)(2,1)S(1)}, bf16[144,1008]{1,0:T(8,128)(2,1)S(1)}, u32[]{:S(2)}, u32[]{:S(2)}) collective-permute-start(bf16[144,1008]{1,0:T(8,128)(2,1)S(1)} %expert_front.1.pieces.refs_0_), channel_id=1, source_target_pairs={{0,448},{64,0},{128,64},{192,128},{256,192},{320,256},{384,320},{4... | collective-permute-start | bytes 870920 | tf_op jit(solution)/shard_map/ppermute | solution.py:257
  69.2 0.0 collective-permute-done.4
  69.2 1.2 add_convert_fusion
  70.4 9.0 %collective-permute-done.5.refs_1_ = bf16[144,1008]{1,0:T(8,128)(2,1)S(1)} collective-permute-done((bf16[144,1008]{1,0:T(8,128)(2,1)S(1)}, bf16[144,1008]{1,0:T(8,128)(2,1)S(1)}, u32[]{:S(2)}, u32[]{:S(2)}) %collective-permute-start.5) | collective-permute-done | bytes 290336 | tf_op jit(solution)/shard_map/ppermute | solution.py:257
  79.4 0.0 copy-start.3
  79.5 0.0 collective-permute-done.6.refs_2_
  79.5 0.0 copy-start.4
  79.5 0.0 all-to-all-done.1.mine
  79.5 11.9 %all-to-all-start = ((bf16[32,40,384]{2,1,0:T(8,128)(2,1)}), bf16[32,40,384]{2,1,0:T(8,128)(2,1)S(1)}, u32[]{:S(2)}, u32[]{:S(2)}) async-start(bf16[32,40,384]{2,1,0:T(8,128)(2,1)} %bitcast.9), calls=%async_computation | async-start | bytes 1966080 | tf_op jit(solution)/shard_map/all_to_all | solution.py:333
  91.4 1.9 %collective-permute-start.7 = (bf16[8,144,384]{2,1,0:T(8,128)(2,1)S(1)}, bf16[8,144,384]{2,1,0:T(8,128)(2,1)S(1)}, u32[]{:S(2)}, u32[]{:S(2)}) collective-permute-start(bf16[8,144,384]{2,1,0:T(8,128)(2,1)S(1)} %all-to-all-done.1.mine), channel_id=1, source_target_pairs={{0,1},{1,0},{2,3},{3,2},{4,5},{5,4},{6,7},{7,6},{8,9},{9,8},{10,11... | collective-permute-start | bytes 2654216 | tf_op jit(solution)/shard_map/ppermute | solution.py:269
  93.3 2.8 %collective-permute-start.8 = (bf16[144,1008]{1,0:T(8,128)(2,1)S(1)}, bf16[144,1008]{1,0:T(8,128)(2,1)S(1)}, u32[]{:S(2)}, u32[]{:S(2)}) collective-permute-start(bf16[144,1008]{1,0:T(8,128)(2,1)S(1)} %collective-permute-done.5.refs_1_), channel_id=1, source_target_pairs={{0,64},{64,128},{128,192},{192,256},{256,320},{320,384},{384,448},... | collective-permute-start | bytes 870920 | tf_op jit(solution)/shard_map/ppermute | solution.py:257
  96.1 4.3 %collective-permute-start.9 = (bf16[144,1008]{1,0:T(8,128)(2,1)S(1)}, bf16[144,1008]{1,0:T(8,128)(2,1)S(1)}, u32[]{:S(2)}, u32[]{:S(2)}) collective-permute-start(bf16[144,1008]{1,0:T(8,128)(2,1)S(1)} %collective-permute-done.6.refs_2_), channel_id=1, source_target_pairs={{0,448},{64,0},{128,64},{192,128},{256,192},{320,256},{384,320},{4... | collective-permute-start | bytes 870920 | tf_op jit(solution)/shard_map/ppermute | solution.py:257
  100.4 5.4 %collective-permute-done.8.refs_3_ = bf16[144,1008]{1,0:T(8,128)(2,1)S(1)} collective-permute-done((bf16[144,1008]{1,0:T(8,128)(2,1)S(1)}, bf16[144,1008]{1,0:T(8,128)(2,1)S(1)}, u32[]{:S(2)}, u32[]{:S(2)}) %collective-permute-start.8) | collective-permute-done | bytes 290336 | tf_op jit(solution)/shard_map/ppermute | solution.py:257
  105.8 0.0 copy-start.5
  105.8 1.9 %collective-permute-start.10 = (bf16[144,1008]{1,0:T(8,128)(2,1)S(1)}, bf16[144,1008]{1,0:T(8,128)(2,1)S(1)}, u32[]{:S(2)}, u32[]{:S(2)}) collective-permute-start(bf16[144,1008]{1,0:T(8,128)(2,1)S(1)} %collective-permute-done.8.refs_3_), channel_id=1, source_target_pairs={{0,64},{64,128},{128,192},{192,256},{256,320},{320,384},{384,448},... | collective-permute-start | bytes 870920 | tf_op jit(solution)/shard_map/ppermute | solution.py:257
  107.8 0.0 collective-permute-done.9.refs_4_
  107.8 0.0 copy-start.6
  107.8 5.1 %collective-permute-start.11 = (bf16[144,1008]{1,0:T(8,128)(2,1)S(1)}, bf16[144,1008]{1,0:T(8,128)(2,1)S(1)}, u32[]{:S(2)}, u32[]{:S(2)}) collective-permute-start(bf16[144,1008]{1,0:T(8,128)(2,1)S(1)} %collective-permute-done.9.refs_4_), channel_id=1, source_target_pairs={{0,448},{64,0},{128,64},{192,128},{256,192},{320,256},{384,320},{4... | collective-permute-start | bytes 870920 | tf_op jit(solution)/shard_map/ppermute | solution.py:257
  112.9 4.6 %collective-permute-done.10.refs_5_ = bf16[144,1008]{1,0:T(8,128)(2,1)S(1)} collective-permute-done((bf16[144,1008]{1,0:T(8,128)(2,1)S(1)}, bf16[144,1008]{1,0:T(8,128)(2,1)S(1)}, u32[]{:S(2)}, u32[]{:S(2)}) %collective-permute-start.10) | collective-permute-done | bytes 290336 | tf_op jit(solution)/shard_map/ppermute | solution.py:257
  117.6 0.0 copy-start.7
  117.6 1.9 %collective-permute-start.12 = (bf16[144,1008]{1,0:T(8,128)(2,1)S(1)}, bf16[144,1008]{1,0:T(8,128)(2,1)S(1)}, u32[]{:S(2)}, u32[]{:S(2)}) collective-permute-start(bf16[144,1008]{1,0:T(8,128)(2,1)S(1)} %collective-permute-done.10.refs_5_), channel_id=1, source_target_pairs={{0,64},{64,128},{128,192},{192,256},{256,320},{320,384},{384,448},... | collective-permute-start | bytes 870920 | tf_op jit(solution)/shard_map/ppermute | solution.py:257
  119.5 0.0 collective-permute-done.7.other
  119.5 0.0 copy-done.3
  119.5 0.0 copy-done.4
  119.5 0.0 copy-done.5
  119.5 0.0 copy-done.6
  119.5 0.0 copy-done.7
  119.5 3.5 %weight_grads.1.total = f32[384,1008]{1,0:T(8,128)S(1)} custom-call(s32[5]{0:T(128)S(1)} %stack.23.flags, bf16[8,144,384]{2,1,0:T(8,128)(2,1)S(1)} %all-to-all-done.1.mine, bf16[8,144,384]{2,1,0:T(8,128)(2,1)S(1)} %collective-permute-done.7.other, bf16[144,1008]{1,0:T(8,128)(2,1)} %copy-done, bf16[144,1008]{1,0:T(8,128)(2,1)} %copy-done.3, ...), custom_call_target="tpu_custom_call" | custom-call | flops 668860416 | bytes 3511296 | tf_op jit(solution)/shard_map/weight_grads/pallas_call | solution.py:239
  123.0 0.0 copy-start.1
  123.1 0.0 copy-start.2
  123.1 0.0 collective-permute-done.11.refs_0_
  123.1 5.3 %collective-permute-done.12.refs_1_ = bf16[144,1008]{1,0:T(8,128)(2,1)S(1)} collective-permute-done((bf16[144,1008]{1,0:T(8,128)(2,1)S(1)}, bf16[144,1008]{1,0:T(8,128)(2,1)S(1)}, u32[]{:S(2)}, u32[]{:S(2)}) %collective-permute-start.12) | collective-permute-done | bytes 290336 | tf_op jit(solution)/shard_map/ppermute | solution.py:257
  128.4 1.5 weight_grads_last.1
  129.9 3.3 %collective-permute-start.13 = (bf16[192,1008]{1,0:T(8,128)(2,1)S(1)}, bf16[192,1008]{1,0:T(8,128)(2,1)S(1)}, u32[]{:S(2)}, u32[]{:S(2)}) collective-permute-start(bf16[192,1008]{1,0:T(8,128)(2,1)S(1)} %get-tuple-element.33), channel_id=1, source_target_pairs={{0,512},{512,0},{1,513},{513,1},{2,514},{514,2},{3,515},{515,3},{4... | collective-permute-start | bytes 1161224 | tf_op jit(solution)/shard_map/ppermute | solution.py:269
  133.2 19.0 %collective-permute-done.13.got = bf16[192,1008]{1,0:T(8,128)(2,1)S(1)} collective-permute-done((bf16[192,1008]{1,0:T(8,128)(2,1)S(1)}, bf16[192,1008]{1,0:T(8,128)(2,1)S(1)}, u32[]{:S(2)}, u32[]{:S(2)}) %collective-permute-start.13) | collective-permute-done | bytes 387104 | tf_op jit(solution)/shard_map/ppermute | solution.py:269
  152.1 1.1 finish.1
  153.2 0.0 all-to-all-done.blocks
  153.2 0.0 copy-done.1
  153.2 0.0 copy-done.2
  153.2 1.1 combine.1
Async XLA Ops:
  2.7 11.7 %collective-permute-start = (bf16[40,3072]{1,0:T(8,128)(2,1)S(1)}, bf16[40,3072]{1,0:T(8,128)(2,1)S(1)}, u32[]{:S(2)}, u32[]{:S(2)}) collective-permute-start(bf16[40,3072]{1,0:T(8,128)(2,1)S(1)} %get-tuple-element.22), channel_id=1, source_target_pairs={{0,16},{16,32},{32,48},{48,0},{1,17},{17,33},{33,49},{49,1},{2,18}... | collective-permute-start | bytes 737288 | tf_op jit(solution)/shard_map/ppermute | solution.py:263
  7.8 21.2 %collective-permute-start.1 = (bf16[40,3072]{1,0:T(8,128)(2,1)S(1)}, bf16[40,3072]{1,0:T(8,128)(2,1)S(1)}, u32[]{:S(2)}, u32[]{:S(2)}) collective-permute-start(bf16[40,3072]{1,0:T(8,128)(2,1)S(1)} %get-tuple-element.23), channel_id=1, source_target_pairs={{0,32},{16,48},{32,0},{48,16},{1,33},{17,49},{33,1},{49,17},{2,34}... | collective-permute-start | bytes 737288 | tf_op jit(solution)/shard_map/ppermute | solution.py:263
  9.7 19.2 %collective-permute-start.2 = (bf16[40,3072]{1,0:T(8,128)(2,1)S(1)}, bf16[40,3072]{1,0:T(8,128)(2,1)S(1)}, u32[]{:S(2)}, u32[]{:S(2)}) collective-permute-start(bf16[40,3072]{1,0:T(8,128)(2,1)S(1)} %get-tuple-element.24), channel_id=1, source_target_pairs={{0,48},{16,0},{32,16},{48,32},{1,49},{17,1},{33,17},{49,33},{2,50}... | collective-permute-start | bytes 737288 | tf_op jit(solution)/shard_map/ppermute | solution.py:263
  31.1 18.6 %collective-permute-start.3 = (bf16[144,3072]{1,0:T(8,128)(2,1)S(1)}, bf16[144,3072]{1,0:T(8,128)(2,1)S(1)}, u32[]{:S(2)}, u32[]{:S(2)}) collective-permute-start(bf16[144,3072]{1,0:T(8,128)(2,1)S(1)} %get-tuple-element.25.mine), channel_id=1, source_target_pairs={{0,1},{1,0},{2,3},{3,2},{4,5},{5,4},{6,7},{7,6},{8,9},{9,8},{10,11... | collective-permute-start | bytes 2654216 | tf_op jit(solution)/shard_map/ppermute | solution.py:269
  33.1 46.4 %all-to-all-start.1 = ((bf16[8,144,384]{2,1,0:T(8,128)(2,1)}), bf16[8,144,384]{2,1,0:T(8,128)(2,1)S(1)}, u32[]{:S(2)}, u32[]{:S(2)}) async-start(bf16[8,144,384]{2,1,0:T(8,128)(2,1)} %get-tuple-element.31), calls=%async_computation.1 | async-start | bytes 1769472 | tf_op jit(solution)/shard_map/all_to_all | solution.py:310
  54.9 10.9 %copy-start = (bf16[144,1008]{1,0:T(8,128)(2,1)}, bf16[144,1008]{1,0:T(8,128)(2,1)S(1)}, u32[]{:S(2)}) copy-start(bf16[144,1008]{1,0:T(8,128)(2,1)S(1)} %expert_front.1.pieces.refs_0_) | copy-start | bytes 870916
  60.0 9.2 %collective-permute-start.4 = (bf16[8,4,40,384]{3,2,1,0:T(8,128)(2,1)S(1)}, bf16[8,4,40,384]{3,2,1,0:T(8,128)(2,1)S(1)}, u32[]{:S(2)}, u32[]{:S(2)}) collective-permute-start(bf16[8,4,40,384]{3,2,1,0:T(8,128)(2,1)S(1)} %get-tuple-element.27), channel_id=1, source_target_pairs={{0,1},{1,0},{2,3},{3,2},{4,5},{5,4},{6,7},{7,6},{8,9},{9,8},{10,11... | collective-permute-start | bytes 2949128 | tf_op jit(solution)/shard_map/ppermute | solution.py:269
  62.1 17.3 %collective-permute-start.5 = (bf16[144,1008]{1,0:T(8,128)(2,1)S(1)}, bf16[144,1008]{1,0:T(8,128)(2,1)S(1)}, u32[]{:S(2)}, u32[]{:S(2)}) collective-permute-start(bf16[144,1008]{1,0:T(8,128)(2,1)S(1)} %expert_front.1.pieces.refs_0_), channel_id=1, source_target_pairs={{0,64},{64,128},{128,192},{192,256},{256,320},{320,384},{384,448},... | collective-permute-start | bytes 870920 | tf_op jit(solution)/shard_map/ppermute | solution.py:257
  65.9 13.6 %collective-permute-start.6 = (bf16[144,1008]{1,0:T(8,128)(2,1)S(1)}, bf16[144,1008]{1,0:T(8,128)(2,1)S(1)}, u32[]{:S(2)}, u32[]{:S(2)}) collective-permute-start(bf16[144,1008]{1,0:T(8,128)(2,1)S(1)} %expert_front.1.pieces.refs_0_), channel_id=1, source_target_pairs={{0,448},{64,0},{128,64},{192,128},{256,192},{320,256},{384,320},{4... | collective-permute-start | bytes 870920 | tf_op jit(solution)/shard_map/ppermute | solution.py:257
  79.4 40.0 %copy-start.3 = (bf16[144,1008]{1,0:T(8,128)(2,1)}, bf16[144,1008]{1,0:T(8,128)(2,1)S(1)}, u32[]{:S(2)}) copy-start(bf16[144,1008]{1,0:T(8,128)(2,1)S(1)} %collective-permute-done.5.refs_1_) | copy-start | bytes 870916
  79.5 40.0 %copy-start.4 = (bf16[144,1008]{1,0:T(8,128)(2,1)}, bf16[144,1008]{1,0:T(8,128)(2,1)S(1)}, u32[]{:S(2)}) copy-start(bf16[144,1008]{1,0:T(8,128)(2,1)S(1)} %collective-permute-done.6.refs_2_) | copy-start | bytes 870916
  79.5 73.8 %all-to-all-start = ((bf16[32,40,384]{2,1,0:T(8,128)(2,1)}), bf16[32,40,384]{2,1,0:T(8,128)(2,1)S(1)}, u32[]{:S(2)}, u32[]{:S(2)}) async-start(bf16[32,40,384]{2,1,0:T(8,128)(2,1)} %bitcast.9), calls=%async_computation | async-start | bytes 1966080 | tf_op jit(solution)/shard_map/all_to_all | solution.py:333
  91.4 28.1 %collective-permute-start.7 = (bf16[8,144,384]{2,1,0:T(8,128)(2,1)S(1)}, bf16[8,144,384]{2,1,0:T(8,128)(2,1)S(1)}, u32[]{:S(2)}, u32[]{:S(2)}) collective-permute-start(bf16[8,144,384]{2,1,0:T(8,128)(2,1)S(1)} %all-to-all-done.1.mine), channel_id=1, source_target_pairs={{0,1},{1,0},{2,3},{3,2},{4,5},{5,4},{6,7},{7,6},{8,9},{9,8},{10,11... | collective-permute-start | bytes 2654216 | tf_op jit(solution)/shard_map/ppermute | solution.py:269
  93.3 12.5 %collective-permute-start.8 = (bf16[144,1008]{1,0:T(8,128)(2,1)S(1)}, bf16[144,1008]{1,0:T(8,128)(2,1)S(1)}, u32[]{:S(2)}, u32[]{:S(2)}) collective-permute-start(bf16[144,1008]{1,0:T(8,128)(2,1)S(1)} %collective-permute-done.5.refs_1_), channel_id=1, source_target_pairs={{0,64},{64,128},{128,192},{192,256},{256,320},{320,384},{384,448},... | collective-permute-start | bytes 870920 | tf_op jit(solution)/shard_map/ppermute | solution.py:257
  96.1 11.6 %collective-permute-start.9 = (bf16[144,1008]{1,0:T(8,128)(2,1)S(1)}, bf16[144,1008]{1,0:T(8,128)(2,1)S(1)}, u32[]{:S(2)}, u32[]{:S(2)}) collective-permute-start(bf16[144,1008]{1,0:T(8,128)(2,1)S(1)} %collective-permute-done.6.refs_2_), channel_id=1, source_target_pairs={{0,448},{64,0},{128,64},{192,128},{256,192},{320,256},{384,320},{4... | collective-permute-start | bytes 870920 | tf_op jit(solution)/shard_map/ppermute | solution.py:257
  105.8 13.7 %copy-start.5 = (bf16[144,1008]{1,0:T(8,128)(2,1)}, bf16[144,1008]{1,0:T(8,128)(2,1)S(1)}, u32[]{:S(2)}) copy-start(bf16[144,1008]{1,0:T(8,128)(2,1)S(1)} %collective-permute-done.8.refs_3_) | copy-start | bytes 870916
  105.8 11.7 %collective-permute-start.10 = (bf16[144,1008]{1,0:T(8,128)(2,1)S(1)}, bf16[144,1008]{1,0:T(8,128)(2,1)S(1)}, u32[]{:S(2)}, u32[]{:S(2)}) collective-permute-start(bf16[144,1008]{1,0:T(8,128)(2,1)S(1)} %collective-permute-done.8.refs_3_), channel_id=1, source_target_pairs={{0,64},{64,128},{128,192},{192,256},{256,320},{320,384},{384,448},... | collective-permute-start | bytes 870920 | tf_op jit(solution)/shard_map/ppermute | solution.py:257
  107.8 11.8 %copy-start.6 = (bf16[144,1008]{1,0:T(8,128)(2,1)}, bf16[144,1008]{1,0:T(8,128)(2,1)S(1)}, u32[]{:S(2)}) copy-start(bf16[144,1008]{1,0:T(8,128)(2,1)S(1)} %collective-permute-done.9.refs_4_) | copy-start | bytes 870916
  107.8 15.3 %collective-permute-start.11 = (bf16[144,1008]{1,0:T(8,128)(2,1)S(1)}, bf16[144,1008]{1,0:T(8,128)(2,1)S(1)}, u32[]{:S(2)}, u32[]{:S(2)}) collective-permute-start(bf16[144,1008]{1,0:T(8,128)(2,1)S(1)} %collective-permute-done.9.refs_4_), channel_id=1, source_target_pairs={{0,448},{64,0},{128,64},{192,128},{256,192},{320,256},{384,320},{4... | collective-permute-start | bytes 870920 | tf_op jit(solution)/shard_map/ppermute | solution.py:257
  117.6 2.0 %copy-start.7 = (bf16[144,1008]{1,0:T(8,128)(2,1)}, bf16[144,1008]{1,0:T(8,128)(2,1)S(1)}, u32[]{:S(2)}) copy-start(bf16[144,1008]{1,0:T(8,128)(2,1)S(1)} %collective-permute-done.10.refs_5_) | copy-start | bytes 870916
  117.6 10.8 %collective-permute-start.12 = (bf16[144,1008]{1,0:T(8,128)(2,1)S(1)}, bf16[144,1008]{1,0:T(8,128)(2,1)S(1)}, u32[]{:S(2)}, u32[]{:S(2)}) collective-permute-start(bf16[144,1008]{1,0:T(8,128)(2,1)S(1)} %collective-permute-done.10.refs_5_), channel_id=1, source_target_pairs={{0,64},{64,128},{128,192},{192,256},{256,320},{320,384},{384,448},... | collective-permute-start | bytes 870920 | tf_op jit(solution)/shard_map/ppermute | solution.py:257
  123.0 30.2 %copy-start.1 = (s32[64,2]{0,1:T(2,128)S(1)}, s32[64,2]{0,1:T(2,128)}, u32[]{:S(2)}) copy-start(s32[64,2]{0,1:T(2,128)} %param.9) | copy-start | bytes 1540
  123.1 30.2 %copy-start.2 = (f32[64,2]{0,1:T(2,128)S(1)}, f32[64,2]{0,1:T(2,128)}, u32[]{:S(2)}) copy-start(f32[64,2]{0,1:T(2,128)} %param.10) | copy-start | bytes 1540
  129.9 22.3 %collective-permute-start.13 = (bf16[192,1008]{1,0:T(8,128)(2,1)S(1)}, bf16[192,1008]{1,0:T(8,128)(2,1)S(1)}, u32[]{:S(2)}, u32[]{:S(2)}) collective-permute-start(bf16[192,1008]{1,0:T(8,128)(2,1)S(1)} %get-tuple-element.33), channel_id=1, source_target_pairs={{0,512},{512,0},{1,513},{513,1},{2,514},{514,2},{3,515},{515,3},{4... | collective-permute-start | bytes 1161224 | tf_op jit(solution)/shard_map/ppermute | solution.py:269

commit v4 on v3

--- a/solution.py
+++ b/solution.py
@@ -167,7 +167,7 @@
                 both = jnp.concatenate([out[:, at], back[:, at]], axis=1)
                 for k in range(N_XL):
                     source = lax.rem(flags[3] + (N_XL - k), N_XL)
-                    ref[i, source] = both[SLOT * k : SLOT * (k + 1)]
+                    ref[source, i] = both[SLOT * k : SLOT * (k + 1)]
 
     @pl.when(flags[0] == 0)
     def _():
@@ -183,9 +183,9 @@
     part = layer_out.shape[1]
     experts = []
     for e in range(N_XL):
-        total = blocks[e].astype(F32)
+        total = blocks[N_Y * e].astype(F32)
         for i in range(1, N_Y):
-            total = total + blocks[N_XL * i + e].astype(F32)
+            total = total + blocks[N_Y * e + i].astype(F32)
         experts.append(total.astype(BF16))
     both = jnp.concatenate(experts, axis=0)
     layer_out[...] = dot(gate, both[:, :part].astype(F32), ((0,), (0,)), HIGHEST).astype(BF16)
@@ -313,7 +313,7 @@
     )
     keep, send = call(
         expert_back,
-        [((N_Y, N_XL, SLOT, 2 * part), BF16)] * 2,
+        [((N_XL, N_Y, SLOT, 2 * part), BF16)] * 2,
         [flags],
         pieces,
         far=weights,
@@ -331,8 +331,8 @@
 
     summed, _ = lax.optimization_barrier((summed, (found[1], found[7])))
     blocks = lax.all_to_all(
-        summed.reshape(N_Y * N_XL, SLOT, 2 * part),
-        ("y", "xl"),
+        summed.reshape(N_XL * N_Y, SLOT, 2 * part),
+        ("xl", "y"),
         split_axis=0,
         concat_axis=0,
         tiled=True,
@@ -363,8 +363,11 @@
         total,
         *[found[k] for k in LAST],
     )
+    received, layer_out, token_grad = lax.optimization_barrier(
+        (swap(given, "xh"), layer_out, token_grad)
+    )
     grad_gate, grad_up, grad_down = call(
-        finish, [((1, part, ff), F32)] * 3, [], kept, swap(given, "xh")
+        finish, [((1, part, ff), F32)] * 3, [], kept, received
     )
     return layer_out, token_grad, grad_gate, grad_up, jnp.swapaxes(grad_down, 1, 2)
 

time: 155 us -> 154 us (level)
  no operation moved by 1% of the time
where the time goes in v4:
time: 154 us; the launch traced here: 153 us
  starting transfers between devices  71.1 us (46%)
  waiting for transfers between devices  58.4 us (38%)
  Pallas kernels  21.4 us (14%)
    ppermute x7, waiting for transfers between devices, shift(): return lax.ppermute(value, 'z', [(i, (i + by) % N_Z) for i in range(N_Z)])  24.4 us
    ppermute x7, starting transfers between devices, shift(): return lax.ppermute(value, 'z', [(i, (i + by) % N_Z) for i in range(N_Z)])  23.1 us
    pallas_call x8, Pallas kernels, call(): pl.pallas_call(body, out_shape=[jax.ShapeDtypeStruct(s, t) if i < len(out...  21.4 us
    ppermute x4, waiting for transfers between devices, swap(): return lax.ppermute(value, axis, [(0, 1), (1, 0)])  17.8 us
    all_to_all x1, starting transfers between devices, on_device(): cols = lax.all_to_all(cols, 'z', split_axis=0, concat_axis=0, tiled=True)  16.7 us
    ppermute x3, waiting for transfers between devices, spread(): lax.ppermute(parts[k], axis, [(i, (i + forward * k) % count) for i in ran...  16.2 us
    all_to_all x1, starting transfers between devices, on_device(): lax.all_to_all(summed.reshape(N_XL * N_Y, SLOT, 2 * part), ('xl', 'y'), s...  12 us
    ppermute x3, starting transfers between devices, spread(): lax.ppermute(parts[k], axis, [(i, (i + forward * k) % count) for i in ran...  10.1 us
  transfers between devices with their start and end apart: 16, of which 7 were waited for; matrix products, arithmetic and copies ran while one was open for 1% of the time, Pallas kernels for 11%

profile of v4, /device:TPU:14, one launch (start us, length us, event | category | flops | bytes accessed | tf_op | source)
XLA Modules:
  0.0 153.2 jit_solution(5255005263647123365)
XLA Ops:
  0.6 0.1 stack.23.flags
  0.7 2.0 %dispatch.1 = (bf16[40,3072]{1,0:T(8,128)(2,1)S(1)}, bf16[40,3072]{1,0:T(8,128)(2,1)S(1)}, bf16[40,3072]{1,0:T(8,128)(2,1)S(1)}, bf16[40,3072]{1,0:T(8,128)(2,1)S(1)}) custom-call(s32[5]{0:T(128)S(1)} %stack.23.flags, s32[2,64]{1,0:T(2,128)} %bitcast.11, f32[2,64]{1,0:T(2,128)} %bitcast.13, bf16[64,3072]{1,0:T(8,128)(2,1)} %tokens.1, bf16[64,3072]{1,0:T(8,128)(2,1)} %cotangent.1), custom_call_target="tpu_custom_call" | custom-call | tf_op jit(solution)/shard_map/dispatch/pallas_call | solution.py:239
  2.7 5.1 %collective-permute-start = (bf16[40,3072]{1,0:T(8,128)(2,1)S(1)}, bf16[40,3072]{1,0:T(8,128)(2,1)S(1)}, u32[]{:S(2)}, u32[]{:S(2)}) collective-permute-start(bf16[40,3072]{1,0:T(8,128)(2,1)S(1)} %get-tuple-element.25), channel_id=1, source_target_pairs={{0,16},{16,32},{32,48},{48,0},{1,17},{17,33},{33,49},{49,1},{2,18}... | collective-permute-start | bytes 737288 | tf_op jit(solution)/shard_map/ppermute | solution.py:263
  7.8 1.9 %collective-permute-start.1 = (bf16[40,3072]{1,0:T(8,128)(2,1)S(1)}, bf16[40,3072]{1,0:T(8,128)(2,1)S(1)}, u32[]{:S(2)}, u32[]{:S(2)}) collective-permute-start(bf16[40,3072]{1,0:T(8,128)(2,1)S(1)} %get-tuple-element.26), channel_id=1, source_target_pairs={{0,32},{16,48},{32,0},{48,16},{1,33},{17,49},{33,1},{49,17},{2,34}... | collective-permute-start | bytes 737288 | tf_op jit(solution)/shard_map/ppermute | solution.py:263
  9.7 3.1 %collective-permute-start.2 = (bf16[40,3072]{1,0:T(8,128)(2,1)S(1)}, bf16[40,3072]{1,0:T(8,128)(2,1)S(1)}, u32[]{:S(2)}, u32[]{:S(2)}) collective-permute-start(bf16[40,3072]{1,0:T(8,128)(2,1)S(1)} %get-tuple-element.27), channel_id=1, source_target_pairs={{0,48},{16,0},{32,16},{48,32},{1,49},{17,1},{33,17},{49,33},{2,50}... | collective-permute-start | bytes 737288 | tf_op jit(solution)/shard_map/ppermute | solution.py:263
  12.8 1.7 %collective-permute-done.refs_1_ = bf16[40,3072]{1,0:T(8,128)(2,1)S(1)} collective-permute-done((bf16[40,3072]{1,0:T(8,128)(2,1)S(1)}, bf16[40,3072]{1,0:T(8,128)(2,1)S(1)}, u32[]{:S(2)}, u32[]{:S(2)}) %collective-permute-start) | collective-permute-done | bytes 245792 | tf_op jit(solution)/shard_map/ppermute | solution.py:263
  14.5 14.5 %collective-permute-done.1.refs_2_ = bf16[40,3072]{1,0:T(8,128)(2,1)S(1)} collective-permute-done((bf16[40,3072]{1,0:T(8,128)(2,1)S(1)}, bf16[40,3072]{1,0:T(8,128)(2,1)S(1)}, u32[]{:S(2)}, u32[]{:S(2)}) %collective-permute-start.1) | collective-permute-done | bytes 245792 | tf_op jit(solution)/shard_map/ppermute | solution.py:263
  29.0 0.0 collective-permute-done.2.refs_3_
  29.0 2.1 %squeeze.1 = (bf16[144,3072]{1,0:T(8,128)(2,1)S(1)}, bf16[8,144,384]{2,1,0:T(8,128)(2,1)}) custom-call(s32[5]{0:T(128)S(1)} %stack.23.flags, bf16[40,3072]{1,0:T(8,128)(2,1)S(1)} %get-tuple-element.24.refs_0_, bf16[40,3072]{1,0:T(8,128)(2,1)S(1)} %collective-permute-done.refs_1_, bf16[40,3072]{1,0:T(8,128)(2,1)S(1)} %collective-permute-done.1.refs_2_, ...), custom_call_target="tpu_custom_call" | custom-call | tf_op jit(solution)/shard_map/squeeze/pallas_call | solution.py:239
  31.1 1.9 %collective-permute-start.4 = (bf16[144,3072]{1,0:T(8,128)(2,1)S(1)}, bf16[144,3072]{1,0:T(8,128)(2,1)S(1)}, u32[]{:S(2)}, u32[]{:S(2)}) collective-permute-start(bf16[144,3072]{1,0:T(8,128)(2,1)S(1)} %get-tuple-element.29.mine), channel_id=1, source_target_pairs={{0,1},{1,0},{2,3},{3,2},{4,5},{5,4},{6,7},{7,6},{8,9},{9,8},{10,11... | collective-permute-start | bytes 2654216 | tf_op jit(solution)/shard_map/ppermute | solution.py:269
  33.1 16.7 %all-to-all-start = ((bf16[8,144,384]{2,1,0:T(8,128)(2,1)}), bf16[8,144,384]{2,1,0:T(8,128)(2,1)S(1)}, u32[]{:S(2)}, u32[]{:S(2)}) async-start(bf16[8,144,384]{2,1,0:T(8,128)(2,1)} %get-tuple-element.28), calls=%async_computation | async-start | bytes 1769472 | tf_op jit(solution)/shard_map/all_to_all | solution.py:310
  49.8 0.0 collective-permute-done.4.other
  49.8 5.1 %expert_front.1.refs_0_.pieces = bf16[144,1008]{1,0:T(8,128)(2,1)S(1)} custom-call(s32[5]{0:T(128)S(1)} %stack.23.flags, bf16[144,3072]{1,0:T(8,128)(2,1)S(1)} %get-tuple-element.29.mine, bf16[144,3072]{1,0:T(8,128)(2,1)S(1)} %collective-permute-done.4.other, bf16[1,336,3072]{2,1,0:T(8,128)(2,1)} %bitcast.15, bf16[1,336,3072]{2,1,0:T(8,128)(2,1)} %bitcast.17, ...), custom_call_target="tpu_custom_call" | custom-call | tf_op jit(solution)/shard_map/expert_front/pallas_call | solution.py:239
  54.9 0.0 copy-start
  54.9 5.0 %expert_back.1 = (bf16[4,8,40,384]{3,2,1,0:T(8,128)(2,1)S(1)}, bf16[4,8,40,384]{3,2,1,0:T(8,128)(2,1)S(1)}) custom-call(s32[5]{0:T(128)S(1)} %stack.23.flags, bf16[144,1008]{1,0:T(8,128)(2,1)S(1)} %expert_front.1.refs_0_.pieces, bf16[1,336,3072]{2,1,0:T(8,128)(2,1)} %bitcast.16, bf16[1,336,3072]{2,1,0:T(8,128)(2,1)} %bitcast.18, bf16[1,336,3072]{2,1,0:T(8,128)(2,1)} %down_w.3), custom_call_target="tpu_custom_call" | custom-call | flops 891813888 | bytes 6483456 | tf_op jit(solution)/shard_map/expert_back/pallas_call | solution.py:239
  60.0 2.1 %collective-permute-start.13 = (bf16[4,8,40,384]{3,2,1,0:T(8,128)(2,1)S(1)}, bf16[4,8,40,384]{3,2,1,0:T(8,128)(2,1)S(1)}, u32[]{:S(2)}, u32[]{:S(2)}) collective-permute-start(bf16[4,8,40,384]{3,2,1,0:T(8,128)(2,1)S(1)} %get-tuple-element.32), channel_id=1, source_target_pairs={{0,1},{1,0},{2,3},{3,2},{4,5},{5,4},{6,7},{7,6},{8,9},{9,8},{10,11... | collective-permute-start | bytes 2949128 | tf_op jit(solution)/shard_map/ppermute | solution.py:269
  62.1 3.7 %collective-permute-start.5 = (bf16[144,1008]{1,0:T(8,128)(2,1)S(1)}, bf16[144,1008]{1,0:T(8,128)(2,1)S(1)}, u32[]{:S(2)}, u32[]{:S(2)}) collective-permute-start(bf16[144,1008]{1,0:T(8,128)(2,1)S(1)} %expert_front.1.refs_0_.pieces), channel_id=1, source_target_pairs={{0,64},{64,128},{128,192},{192,256},{256,320},{320,384},{384,448},... | collective-permute-start | bytes 870920 | tf_op jit(solution)/shard_map/ppermute | solution.py:257
  65.8 0.0 copy-done
  65.8 3.3 %collective-permute-start.6 = (bf16[144,1008]{1,0:T(8,128)(2,1)S(1)}, bf16[144,1008]{1,0:T(8,128)(2,1)S(1)}, u32[]{:S(2)}, u32[]{:S(2)}) collective-permute-start(bf16[144,1008]{1,0:T(8,128)(2,1)S(1)} %expert_front.1.refs_0_.pieces), channel_id=1, source_target_pairs={{0,448},{64,0},{128,64},{192,128},{256,192},{320,256},{384,320},{4... | collective-permute-start | bytes 870920 | tf_op jit(solution)/shard_map/ppermute | solution.py:257
  69.2 0.0 collective-permute-done.13
  69.2 1.2 add_convert_fusion
  70.4 9.0 %collective-permute-done.5.refs_1_ = bf16[144,1008]{1,0:T(8,128)(2,1)S(1)} collective-permute-done((bf16[144,1008]{1,0:T(8,128)(2,1)S(1)}, bf16[144,1008]{1,0:T(8,128)(2,1)S(1)}, u32[]{:S(2)}, u32[]{:S(2)}) %collective-permute-start.5) | collective-permute-done | bytes 290336 | tf_op jit(solution)/shard_map/ppermute | solution.py:257
  79.4 0.0 copy-start.3
  79.4 0.0 collective-permute-done.6.refs_2_
  79.4 0.0 copy-start.4
  79.4 0.0 all-to-all-done.mine
  79.4 12.0 %all-to-all-start.1 = ((bf16[32,40,384]{2,1,0:T(8,128)(2,1)}), bf16[32,40,384]{2,1,0:T(8,128)(2,1)S(1)}, u32[]{:S(2)}, u32[]{:S(2)}) async-start(bf16[32,40,384]{2,1,0:T(8,128)(2,1)} %bitcast.9), calls=%async_computation.1 | async-start | bytes 1966080 | tf_op jit(solution)/shard_map/all_to_all | solution.py:333
  91.4 1.9 %collective-permute-start.3 = (bf16[8,144,384]{2,1,0:T(8,128)(2,1)S(1)}, bf16[8,144,384]{2,1,0:T(8,128)(2,1)S(1)}, u32[]{:S(2)}, u32[]{:S(2)}) collective-permute-start(bf16[8,144,384]{2,1,0:T(8,128)(2,1)S(1)} %all-to-all-done.mine), channel_id=1, source_target_pairs={{0,1},{1,0},{2,3},{3,2},{4,5},{5,4},{6,7},{7,6},{8,9},{9,8},{10,11... | collective-permute-start | bytes 2654216 | tf_op jit(solution)/shard_map/ppermute | solution.py:269
  93.3 2.8 %collective-permute-start.7 = (bf16[144,1008]{1,0:T(8,128)(2,1)S(1)}, bf16[144,1008]{1,0:T(8,128)(2,1)S(1)}, u32[]{:S(2)}, u32[]{:S(2)}) collective-permute-start(bf16[144,1008]{1,0:T(8,128)(2,1)S(1)} %collective-permute-done.5.refs_1_), channel_id=1, source_target_pairs={{0,64},{64,128},{128,192},{192,256},{256,320},{320,384},{384,448},... | collective-permute-start | bytes 870920 | tf_op jit(solution)/shard_map/ppermute | solution.py:257
  96.1 4.3 %collective-permute-start.8 = (bf16[144,1008]{1,0:T(8,128)(2,1)S(1)}, bf16[144,1008]{1,0:T(8,128)(2,1)S(1)}, u32[]{:S(2)}, u32[]{:S(2)}) collective-permute-start(bf16[144,1008]{1,0:T(8,128)(2,1)S(1)} %collective-permute-done.6.refs_2_), channel_id=1, source_target_pairs={{0,448},{64,0},{128,64},{192,128},{256,192},{320,256},{384,320},{4... | collective-permute-start | bytes 870920 | tf_op jit(solution)/shard_map/ppermute | solution.py:257
  100.4 5.4 %collective-permute-done.7.refs_3_ = bf16[144,1008]{1,0:T(8,128)(2,1)S(1)} collective-permute-done((bf16[144,1008]{1,0:T(8,128)(2,1)S(1)}, bf16[144,1008]{1,0:T(8,128)(2,1)S(1)}, u32[]{:S(2)}, u32[]{:S(2)}) %collective-permute-start.7) | collective-permute-done | bytes 290336 | tf_op jit(solution)/shard_map/ppermute | solution.py:257
  105.9 0.0 copy-start.5
  105.9 1.9 %collective-permute-start.9 = (bf16[144,1008]{1,0:T(8,128)(2,1)S(1)}, bf16[144,1008]{1,0:T(8,128)(2,1)S(1)}, u32[]{:S(2)}, u32[]{:S(2)}) collective-permute-start(bf16[144,1008]{1,0:T(8,128)(2,1)S(1)} %collective-permute-done.7.refs_3_), channel_id=1, source_target_pairs={{0,64},{64,128},{128,192},{192,256},{256,320},{320,384},{384,448},... | collective-permute-start | bytes 870920 | tf_op jit(solution)/shard_map/ppermute | solution.py:257
  107.8 0.0 collective-permute-done.8.refs_4_
  107.8 0.0 copy-start.6
  107.8 5.1 %collective-permute-start.10 = (bf16[144,1008]{1,0:T(8,128)(2,1)S(1)}, bf16[144,1008]{1,0:T(8,128)(2,1)S(1)}, u32[]{:S(2)}, u32[]{:S(2)}) collective-permute-start(bf16[144,1008]{1,0:T(8,128)(2,1)S(1)} %collective-permute-done.8.refs_4_), channel_id=1, source_target_pairs={{0,448},{64,0},{128,64},{192,128},{256,192},{320,256},{384,320},{4... | collective-permute-start | bytes 870920 | tf_op jit(solution)/shard_map/ppermute | solution.py:257
  112.9 4.6 %collective-permute-done.9.refs_5_ = bf16[144,1008]{1,0:T(8,128)(2,1)S(1)} collective-permute-done((bf16[144,1008]{1,0:T(8,128)(2,1)S(1)}, bf16[144,1008]{1,0:T(8,128)(2,1)S(1)}, u32[]{:S(2)}, u32[]{:S(2)}) %collective-permute-start.9) | collective-permute-done | bytes 290336 | tf_op jit(solution)/shard_map/ppermute | solution.py:257
  117.6 0.0 copy-start.7
  117.6 1.9 %collective-permute-start.11 = (bf16[144,1008]{1,0:T(8,128)(2,1)S(1)}, bf16[144,1008]{1,0:T(8,128)(2,1)S(1)}, u32[]{:S(2)}, u32[]{:S(2)}) collective-permute-start(bf16[144,1008]{1,0:T(8,128)(2,1)S(1)} %collective-permute-done.9.refs_5_), channel_id=1, source_target_pairs={{0,64},{64,128},{128,192},{192,256},{256,320},{320,384},{384,448},... | collective-permute-start | bytes 870920 | tf_op jit(solution)/shard_map/ppermute | solution.py:257
  119.5 0.0 collective-permute-done.3.other
  119.5 0.0 copy-done.3
  119.5 0.0 copy-done.4
  119.5 0.0 copy-done.5
  119.5 0.0 copy-done.6
  119.6 0.0 copy-done.7
  119.6 3.5 %weight_grads.1.total = f32[384,1008]{1,0:T(8,128)S(1)} custom-call(s32[5]{0:T(128)S(1)} %stack.23.flags, bf16[8,144,384]{2,1,0:T(8,128)(2,1)S(1)} %all-to-all-done.mine, bf16[8,144,384]{2,1,0:T(8,128)(2,1)S(1)} %collective-permute-done.3.other, bf16[144,1008]{1,0:T(8,128)(2,1)} %copy-done, bf16[144,1008]{1,0:T(8,128)(2,1)} %copy-done.3, ...), custom_call_target="tpu_custom_call" | custom-call | flops 668860416 | bytes 3511296 | tf_op jit(solution)/shard_map/weight_grads/pallas_call | solution.py:239
  123.1 0.0 copy-start.1
  123.1 0.0 copy-start.2
  123.1 0.0 collective-permute-done.10.refs_0_
  123.1 5.3 %collective-permute-done.11.refs_1_ = bf16[144,1008]{1,0:T(8,128)(2,1)S(1)} collective-permute-done((bf16[144,1008]{1,0:T(8,128)(2,1)S(1)}, bf16[144,1008]{1,0:T(8,128)(2,1)S(1)}, u32[]{:S(2)}, u32[]{:S(2)}) %collective-permute-start.11) | collective-permute-done | bytes 290336 | tf_op jit(solution)/shard_map/ppermute | solution.py:257
  128.4 1.5 weight_grads_last.1
  129.9 3.3 %collective-permute-start.12 = (bf16[192,1008]{1,0:T(8,128)(2,1)S(1)}, bf16[192,1008]{1,0:T(8,128)(2,1)S(1)}, u32[]{:S(2)}, u32[]{:S(2)}) collective-permute-start(bf16[192,1008]{1,0:T(8,128)(2,1)S(1)} %get-tuple-element.30), channel_id=1, source_target_pairs={{0,512},{512,0},{1,513},{513,1},{2,514},{514,2},{3,515},{515,3},{4... | collective-permute-start | bytes 1161224 | tf_op jit(solution)/shard_map/ppermute | solution.py:269
  133.2 0.0 all-to-all-done.1.blocks
  133.2 0.0 copy-done.1
  133.2 0.0 copy-done.2
  133.2 1.1 combine.1
  134.3 17.8 %collective-permute-done.12.got = bf16[192,1008]{1,0:T(8,128)(2,1)S(1)} collective-permute-done((bf16[192,1008]{1,0:T(8,128)(2,1)S(1)}, bf16[192,1008]{1,0:T(8,128)(2,1)S(1)}, u32[]{:S(2)}, u32[]{:S(2)}) %collective-permute-start.12) | collective-permute-done | bytes 387104 | tf_op jit(solution)/shard_map/ppermute | solution.py:269
  152.1 1.1 finish.1
Async XLA Ops:
  2.7 11.7 %collective-permute-start = (bf16[40,3072]{1,0:T(8,128)(2,1)S(1)}, bf16[40,3072]{1,0:T(8,128)(2,1)S(1)}, u32[]{:S(2)}, u32[]{:S(2)}) collective-permute-start(bf16[40,3072]{1,0:T(8,128)(2,1)S(1)} %get-tuple-element.25), channel_id=1, source_target_pairs={{0,16},{16,32},{32,48},{48,0},{1,17},{17,33},{33,49},{49,1},{2,18}... | collective-permute-start | bytes 737288 | tf_op jit(solution)/shard_map/ppermute | solution.py:263
  7.8 21.2 %collective-permute-start.1 = (bf16[40,3072]{1,0:T(8,128)(2,1)S(1)}, bf16[40,3072]{1,0:T(8,128)(2,1)S(1)}, u32[]{:S(2)}, u32[]{:S(2)}) collective-permute-start(bf16[40,3072]{1,0:T(8,128)(2,1)S(1)} %get-tuple-element.26), channel_id=1, source_target_pairs={{0,32},{16,48},{32,0},{48,16},{1,33},{17,49},{33,1},{49,17},{2,34}... | collective-permute-start | bytes 737288 | tf_op jit(solution)/shard_map/ppermute | solution.py:263
  9.7 19.2 %collective-permute-start.2 = (bf16[40,3072]{1,0:T(8,128)(2,1)S(1)}, bf16[40,3072]{1,0:T(8,128)(2,1)S(1)}, u32[]{:S(2)}, u32[]{:S(2)}) collective-permute-start(bf16[40,3072]{1,0:T(8,128)(2,1)S(1)} %get-tuple-element.27), channel_id=1, source_target_pairs={{0,48},{16,0},{32,16},{48,32},{1,49},{17,1},{33,17},{49,33},{2,50}... | collective-permute-start | bytes 737288 | tf_op jit(solution)/shard_map/ppermute | solution.py:263
  31.1 18.6 %collective-permute-start.4 = (bf16[144,3072]{1,0:T(8,128)(2,1)S(1)}, bf16[144,3072]{1,0:T(8,128)(2,1)S(1)}, u32[]{:S(2)}, u32[]{:S(2)}) collective-permute-start(bf16[144,3072]{1,0:T(8,128)(2,1)S(1)} %get-tuple-element.29.mine), channel_id=1, source_target_pairs={{0,1},{1,0},{2,3},{3,2},{4,5},{5,4},{6,7},{7,6},{8,9},{9,8},{10,11... | collective-permute-start | bytes 2654216 | tf_op jit(solution)/shard_map/ppermute | solution.py:269
  33.1 46.4 %all-to-all-start = ((bf16[8,144,384]{2,1,0:T(8,128)(2,1)}), bf16[8,144,384]{2,1,0:T(8,128)(2,1)S(1)}, u32[]{:S(2)}, u32[]{:S(2)}) async-start(bf16[8,144,384]{2,1,0:T(8,128)(2,1)} %get-tuple-element.28), calls=%async_computation | async-start | bytes 1769472 | tf_op jit(solution)/shard_map/all_to_all | solution.py:310
  54.9 10.9 %copy-start = (bf16[144,1008]{1,0:T(8,128)(2,1)}, bf16[144,1008]{1,0:T(8,128)(2,1)S(1)}, u32[]{:S(2)}) copy-start(bf16[144,1008]{1,0:T(8,128)(2,1)S(1)} %expert_front.1.refs_0_.pieces) | copy-start | bytes 870916
  60.0 9.2 %collective-permute-start.13 = (bf16[4,8,40,384]{3,2,1,0:T(8,128)(2,1)S(1)}, bf16[4,8,40,384]{3,2,1,0:T(8,128)(2,1)S(1)}, u32[]{:S(2)}, u32[]{:S(2)}) collective-permute-start(bf16[4,8,40,384]{3,2,1,0:T(8,128)(2,1)S(1)} %get-tuple-element.32), channel_id=1, source_target_pairs={{0,1},{1,0},{2,3},{3,2},{4,5},{5,4},{6,7},{7,6},{8,9},{9,8},{10,11... | collective-permute-start | bytes 2949128 | tf_op jit(solution)/shard_map/ppermute | solution.py:269
  62.1 17.3 %collective-permute-start.5 = (bf16[144,1008]{1,0:T(8,128)(2,1)S(1)}, bf16[144,1008]{1,0:T(8,128)(2,1)S(1)}, u32[]{:S(2)}, u32[]{:S(2)}) collective-permute-start(bf16[144,1008]{1,0:T(8,128)(2,1)S(1)} %expert_front.1.refs_0_.pieces), channel_id=1, source_target_pairs={{0,64},{64,128},{128,192},{192,256},{256,320},{320,384},{384,448},... | collective-permute-start | bytes 870920 | tf_op jit(solution)/shard_map/ppermute | solution.py:257
  65.8 13.6 %collective-permute-start.6 = (bf16[144,1008]{1,0:T(8,128)(2,1)S(1)}, bf16[144,1008]{1,0:T(8,128)(2,1)S(1)}, u32[]{:S(2)}, u32[]{:S(2)}) collective-permute-start(bf16[144,1008]{1,0:T(8,128)(2,1)S(1)} %expert_front.1.refs_0_.pieces), channel_id=1, source_target_pairs={{0,448},{64,0},{128,64},{192,128},{256,192},{320,256},{384,320},{4... | collective-permute-start | bytes 870920 | tf_op jit(solution)/shard_map/ppermute | solution.py:257
  79.4 40.1 %copy-start.3 = (bf16[144,1008]{1,0:T(8,128)(2,1)}, bf16[144,1008]{1,0:T(8,128)(2,1)S(1)}, u32[]{:S(2)}) copy-start(bf16[144,1008]{1,0:T(8,128)(2,1)S(1)} %collective-permute-done.5.refs_1_) | copy-start | bytes 870916
  79.4 40.1 %copy-start.4 = (bf16[144,1008]{1,0:T(8,128)(2,1)}, bf16[144,1008]{1,0:T(8,128)(2,1)S(1)}, u32[]{:S(2)}) copy-start(bf16[144,1008]{1,0:T(8,128)(2,1)S(1)} %collective-permute-done.6.refs_2_) | copy-start | bytes 870916
  79.4 53.8 %all-to-all-start.1 = ((bf16[32,40,384]{2,1,0:T(8,128)(2,1)}), bf16[32,40,384]{2,1,0:T(8,128)(2,1)S(1)}, u32[]{:S(2)}, u32[]{:S(2)}) async-start(bf16[32,40,384]{2,1,0:T(8,128)(2,1)} %bitcast.9), calls=%async_computation.1 | async-start | bytes 1966080 | tf_op jit(solution)/shard_map/all_to_all | solution.py:333
  91.4 28.1 %collective-permute-start.3 = (bf16[8,144,384]{2,1,0:T(8,128)(2,1)S(1)}, bf16[8,144,384]{2,1,0:T(8,128)(2,1)S(1)}, u32[]{:S(2)}, u32[]{:S(2)}) collective-permute-start(bf16[8,144,384]{2,1,0:T(8,128)(2,1)S(1)} %all-to-all-done.mine), channel_id=1, source_target_pairs={{0,1},{1,0},{2,3},{3,2},{4,5},{5,4},{6,7},{7,6},{8,9},{9,8},{10,11... | collective-permute-start | bytes 2654216 | tf_op jit(solution)/shard_map/ppermute | solution.py:269
  93.3 12.5 %collective-permute-start.7 = (bf16[144,1008]{1,0:T(8,128)(2,1)S(1)}, bf16[144,1008]{1,0:T(8,128)(2,1)S(1)}, u32[]{:S(2)}, u32[]{:S(2)}) collective-permute-start(bf16[144,1008]{1,0:T(8,128)(2,1)S(1)} %collective-permute-done.5.refs_1_), channel_id=1, source_target_pairs={{0,64},{64,128},{128,192},{192,256},{256,320},{320,384},{384,448},... | collective-permute-start | bytes 870920 | tf_op jit(solution)/shard_map/ppermute | solution.py:257
  96.1 11.6 %collective-permute-start.8 = (bf16[144,1008]{1,0:T(8,128)(2,1)S(1)}, bf16[144,1008]{1,0:T(8,128)(2,1)S(1)}, u32[]{:S(2)}, u32[]{:S(2)}) collective-permute-start(bf16[144,1008]{1,0:T(8,128)(2,1)S(1)} %collective-permute-done.6.refs_2_), channel_id=1, source_target_pairs={{0,448},{64,0},{128,64},{192,128},{256,192},{320,256},{384,320},{4... | collective-permute-start | bytes 870920 | tf_op jit(solution)/shard_map/ppermute | solution.py:257
  105.9 13.7 %copy-start.5 = (bf16[144,1008]{1,0:T(8,128)(2,1)}, bf16[144,1008]{1,0:T(8,128)(2,1)S(1)}, u32[]{:S(2)}) copy-start(bf16[144,1008]{1,0:T(8,128)(2,1)S(1)} %collective-permute-done.7.refs_3_) | copy-start | bytes 870916
  105.9 11.7 %collective-permute-start.9 = (bf16[144,1008]{1,0:T(8,128)(2,1)S(1)}, bf16[144,1008]{1,0:T(8,128)(2,1)S(1)}, u32[]{:S(2)}, u32[]{:S(2)}) collective-permute-start(bf16[144,1008]{1,0:T(8,128)(2,1)S(1)} %collective-permute-done.7.refs_3_), channel_id=1, source_target_pairs={{0,64},{64,128},{128,192},{192,256},{256,320},{320,384},{384,448},... | collective-permute-start | bytes 870920 | tf_op jit(solution)/shard_map/ppermute | solution.py:257
  107.8 11.8 %copy-start.6 = (bf16[144,1008]{1,0:T(8,128)(2,1)}, bf16[144,1008]{1,0:T(8,128)(2,1)S(1)}, u32[]{:S(2)}) copy-start(bf16[144,1008]{1,0:T(8,128)(2,1)S(1)} %collective-permute-done.8.refs_4_) | copy-start | bytes 870916
  107.8 15.3 %collective-permute-start.10 = (bf16[144,1008]{1,0:T(8,128)(2,1)S(1)}, bf16[144,1008]{1,0:T(8,128)(2,1)S(1)}, u32[]{:S(2)}, u32[]{:S(2)}) collective-permute-start(bf16[144,1008]{1,0:T(8,128)(2,1)S(1)} %collective-permute-done.8.refs_4_), channel_id=1, source_target_pairs={{0,448},{64,0},{128,64},{192,128},{256,192},{320,256},{384,320},{4... | collective-permute-start | bytes 870920 | tf_op jit(solution)/shard_map/ppermute | solution.py:257
  117.6 2.0 %copy-start.7 = (bf16[144,1008]{1,0:T(8,128)(2,1)}, bf16[144,1008]{1,0:T(8,128)(2,1)S(1)}, u32[]{:S(2)}) copy-start(bf16[144,1008]{1,0:T(8,128)(2,1)S(1)} %collective-permute-done.9.refs_5_) | copy-start | bytes 870916
  117.6 10.8 %collective-permute-start.11 = (bf16[144,1008]{1,0:T(8,128)(2,1)S(1)}, bf16[144,1008]{1,0:T(8,128)(2,1)S(1)}, u32[]{:S(2)}, u32[]{:S(2)}) collective-permute-start(bf16[144,1008]{1,0:T(8,128)(2,1)S(1)} %collective-permute-done.9.refs_5_), channel_id=1, source_target_pairs={{0,64},{64,128},{128,192},{192,256},{256,320},{320,384},{384,448},... | collective-permute-start | bytes 870920 | tf_op jit(solution)/shard_map/ppermute | solution.py:257
  123.1 10.2 %copy-start.1 = (s32[64,2]{0,1:T(2,128)S(1)}, s32[64,2]{0,1:T(2,128)}, u32[]{:S(2)}) copy-start(s32[64,2]{0,1:T(2,128)} %param.9) | copy-start | bytes 1540
  123.1 10.2 %copy-start.2 = (f32[64,2]{0,1:T(2,128)S(1)}, f32[64,2]{0,1:T(2,128)}, u32[]{:S(2)}) copy-start(f32[64,2]{0,1:T(2,128)} %param.10) | copy-start | bytes 1540
  129.9 22.2 %collective-permute-start.12 = (bf16[192,1008]{1,0:T(8,128)(2,1)S(1)}, bf16[192,1008]{1,0:T(8,128)(2,1)S(1)}, u32[]{:S(2)}, u32[]{:S(2)}) collective-permute-start(bf16[192,1008]{1,0:T(8,128)(2,1)S(1)} %get-tuple-element.30), channel_id=1, source_target_pairs={{0,512},{512,0},{1,513},{513,1},{2,514},{514,2},{3,515},{515,3},{4... | collective-permute-start | bytes 1161224 | tf_op jit(solution)/shard_map/ppermute | solution.py:269

commit v5 on v2

--- a/solution.py
+++ b/solution.py
@@ -7,7 +7,8 @@
 
 CAP = 36
 SLOT = 40
-SOON = (0, 1, 7, 2, 6, 3, 5)
+SOON = (0, 1, 7, 2, 6, 3)
+LAST = (5, 4)
 CUTS = 3
 N_Z = 8
 N_Y = 8
@@ -211,8 +212,10 @@
     total_out[...] = grads_of(flags, mine, other, SOON, held[...])
 
 
-def weight_grads_last(flags, mine, other, piece, total, keep_out, send_out):
-    both = total[...] + grads_of(flags, mine, other, (N_Z // 2,), piece[...])
+def weight_grads_last(flags, mine, other, total, *refs):
+    *pieces, keep_out, send_out = refs
+    rows = jnp.concatenate([piece[...] for piece in pieces], axis=0)
+    both = total[...] + grads_of(flags, mine, other, LAST, rows)
     part = keep_out.shape[0]
     keep_out[...] = both[:part]
     send_out[...] = both[part:].astype(BF16)
@@ -322,11 +325,13 @@
     for k in range(1, N_Z // 2):
         found[k] = shift(found[k - 1], 1)
         found[N_Z - k] = shift(found[(N_Z - k + 1) % N_Z], -1)
-    found[N_Z // 2] = shift(found[N_Z // 2 - 1], 1)
     cols_other = swap(cols, "c")
 
+    summed, _ = lax.optimization_barrier((summed, (found[1], found[7])))
     blocks = lax.all_to_all(summed, "y", split_axis=0, concat_axis=0, tiled=True)
     (back,) = call(add_up, [((N_XL, SLOT, 2 * part), BF16)], [flags], blocks)
+    found[3], _ = lax.optimization_barrier((found[3], back))
+    found[4] = shift(found[3], 1)
     back = lax.all_to_all(back, "xl", split_axis=0, concat_axis=0, tiled=True)
     layer_out, token_grad = call(
         combine,
@@ -350,17 +355,21 @@
         ),
         flops=2 * len(SOON) * rows * 2 * part * 3 * ff,
     )
+    total, _ = lax.optimization_barrier((total, back))
     kept, given = call(
         weight_grads_last,
         [((part, 3 * ff), F32), ((part, 3 * ff), BF16)],
         [flags],
         cols,
         cols_other,
-        found[N_Z // 2],
         total,
+        *[found[k] for k in LAST],
+    )
+    received, layer_out, token_grad = lax.optimization_barrier(
+        (swap(given, "xh"), layer_out, token_grad)
     )
     grad_gate, grad_up, grad_down = call(
-        finish, [((1, part, ff), F32)] * 3, [], kept, swap(given, "xh")
+        finish, [((1, part, ff), F32)] * 3, [], kept, received
     )
     return layer_out, token_grad, grad_gate, grad_up, jnp.swapaxes(grad_down, 1, 2)
 

time: 156 us -> 154 us (0.987)
  the two profiles are of different devices: /device:TPU:16 before, /device:TPU:10 now
where the time goes in v5:
time: 154 us; the launch traced here: 153 us
  starting transfers between devices  68.8 us (45%)
  waiting for transfers between devices  59.3 us (39%)
  Pallas kernels  23.2 us (15%)
    ppermute x7, starting transfers between devices, shift(): return lax.ppermute(value, 'z', [(i, (i + by) % N_Z) for i in range(N_Z)])  23.6 us
    pallas_call x9, Pallas kernels, call(): pl.pallas_call(body, out_shape=[jax.ShapeDtypeStruct(s, t) if i < len(out...  23.2 us
    ppermute x4, waiting for transfers between devices, swap(): return lax.ppermute(value, axis, [(0, 1), (1, 0)])  20.2 us
    ppermute x3, waiting for transfers between devices, spread(): lax.ppermute(parts[k], axis, [(i, (i + forward * k) % count) for i in ran...  17.9 us
    all_to_all x1, starting transfers between devices, on_device(): cols = lax.all_to_all(cols, 'z', split_axis=0, concat_axis=0, tiled=True)  16.5 us
    ppermute x7, waiting for transfers between devices, shift(): return lax.ppermute(value, 'z', [(i, (i + by) % N_Z) for i in range(N_Z)])  16 us
    ppermute x3, starting transfers between devices, spread(): lax.ppermute(parts[k], axis, [(i, (i + forward * k) % count) for i in ran...  9.52 us
    ppermute x4, starting transfers between devices, swap(): return lax.ppermute(value, axis, [(0, 1), (1, 0)])  8.26 us
  transfers between devices with their start and end apart: 17, of which 9 were waited for; matrix products, arithmetic and copies ran while one was open for 1% of the time, Pallas kernels for 10%

profile of v5, /device:TPU:10, one launch (start us, length us, event | category | flops | bytes accessed | tf_op | source)
XLA Modules:
  0.0 153.5 jit_solution(5090140008526117948)
XLA Ops:
  0.6 0.1 stack.23.flags
  0.7 2.0 %dispatch.1 = (bf16[40,3072]{1,0:T(8,128)(2,1)S(1)}, bf16[40,3072]{1,0:T(8,128)(2,1)S(1)}, bf16[40,3072]{1,0:T(8,128)(2,1)S(1)}, bf16[40,3072]{1,0:T(8,128)(2,1)S(1)}) custom-call(s32[5]{0:T(128)S(1)} %stack.23.flags, s32[2,64]{1,0:T(2,128)} %bitcast.12, f32[2,64]{1,0:T(2,128)} %bitcast.14, bf16[64,3072]{1,0:T(8,128)(2,1)} %tokens.1, bf16[64,3072]{1,0:T(8,128)(2,1)} %cotangent.1), custom_call_target="tpu_custom_call" | custom-call | tf_op jit(solution)/shard_map/dispatch/pallas_call | solution.py:238
  2.7 2.5 %collective-permute-start = (bf16[40,3072]{1,0:T(8,128)(2,1)S(1)}, bf16[40,3072]{1,0:T(8,128)(2,1)S(1)}, u32[]{:S(2)}, u32[]{:S(2)}) collective-permute-start(bf16[40,3072]{1,0:T(8,128)(2,1)S(1)} %get-tuple-element.27), channel_id=1, source_target_pairs={{0,16},{16,32},{32,48},{48,0},{1,17},{17,33},{33,49},{49,1},{2,18}... | collective-permute-start | bytes 737288 | tf_op jit(solution)/shard_map/ppermute | solution.py:262
  5.2 5.1 %collective-permute-start.1 = (bf16[40,3072]{1,0:T(8,128)(2,1)S(1)}, bf16[40,3072]{1,0:T(8,128)(2,1)S(1)}, u32[]{:S(2)}, u32[]{:S(2)}) collective-permute-start(bf16[40,3072]{1,0:T(8,128)(2,1)S(1)} %get-tuple-element.28), channel_id=1, source_target_pairs={{0,32},{16,48},{32,0},{48,16},{1,33},{17,49},{33,1},{49,17},{2,34}... | collective-permute-start | bytes 737288 | tf_op jit(solution)/shard_map/ppermute | solution.py:262
  10.3 1.9 %collective-permute-start.2 = (bf16[40,3072]{1,0:T(8,128)(2,1)S(1)}, bf16[40,3072]{1,0:T(8,128)(2,1)S(1)}, u32[]{:S(2)}, u32[]{:S(2)}) collective-permute-start(bf16[40,3072]{1,0:T(8,128)(2,1)S(1)} %get-tuple-element.29), channel_id=1, source_target_pairs={{0,48},{16,0},{32,16},{48,32},{1,49},{17,1},{33,17},{49,33},{2,50}... | collective-permute-start | bytes 737288 | tf_op jit(solution)/shard_map/ppermute | solution.py:262
  12.3 1.2 collective-permute-done.refs_1_
  13.5 12.8 %collective-permute-done.1.refs_2_ = bf16[40,3072]{1,0:T(8,128)(2,1)S(1)} collective-permute-done((bf16[40,3072]{1,0:T(8,128)(2,1)S(1)}, bf16[40,3072]{1,0:T(8,128)(2,1)S(1)}, u32[]{:S(2)}, u32[]{:S(2)}) %collective-permute-start.1) | collective-permute-done | bytes 245792 | tf_op jit(solution)/shard_map/ppermute | solution.py:262
  26.2 3.9 %collective-permute-done.2.refs_3_ = bf16[40,3072]{1,0:T(8,128)(2,1)S(1)} collective-permute-done((bf16[40,3072]{1,0:T(8,128)(2,1)S(1)}, bf16[40,3072]{1,0:T(8,128)(2,1)S(1)}, u32[]{:S(2)}, u32[]{:S(2)}) %collective-permute-start.2) | collective-permute-done | bytes 245792 | tf_op jit(solution)/shard_map/ppermute | solution.py:262
  30.2 2.1 %squeeze.1 = (bf16[144,3072]{1,0:T(8,128)(2,1)S(1)}, bf16[8,144,384]{2,1,0:T(8,128)(2,1)}) custom-call(s32[5]{0:T(128)S(1)} %stack.23.flags, bf16[40,3072]{1,0:T(8,128)(2,1)S(1)} %get-tuple-element.26.refs_0_, bf16[40,3072]{1,0:T(8,128)(2,1)S(1)} %collective-permute-done.refs_1_, bf16[40,3072]{1,0:T(8,128)(2,1)S(1)} %collective-permute-done.1.refs_2_, ...), custom_call_target="tpu_custom_call" | custom-call | tf_op jit(solution)/shard_map/squeeze/pallas_call | solution.py:238
  32.3 1.9 %collective-permute-start.4 = (bf16[144,3072]{1,0:T(8,128)(2,1)S(1)}, bf16[144,3072]{1,0:T(8,128)(2,1)S(1)}, u32[]{:S(2)}, u32[]{:S(2)}) collective-permute-start(bf16[144,3072]{1,0:T(8,128)(2,1)S(1)} %get-tuple-element.31.mine), channel_id=1, source_target_pairs={{0,1},{1,0},{2,3},{3,2},{4,5},{5,4},{6,7},{7,6},{8,9},{9,8},{10,11... | collective-permute-start | bytes 2654216 | tf_op jit(solution)/shard_map/ppermute | solution.py:268
  34.2 16.5 %all-to-all-start = ((bf16[8,144,384]{2,1,0:T(8,128)(2,1)}), bf16[8,144,384]{2,1,0:T(8,128)(2,1)S(1)}, u32[]{:S(2)}, u32[]{:S(2)}) async-start(bf16[8,144,384]{2,1,0:T(8,128)(2,1)} %get-tuple-element.30), calls=%async_computation | async-start | bytes 1769472 | tf_op jit(solution)/shard_map/all_to_all | solution.py:309
  50.7 0.0 collective-permute-done.4.other
  50.7 5.1 %expert_front.1.pieces.refs_0_ = bf16[144,1008]{1,0:T(8,128)(2,1)S(1)} custom-call(s32[5]{0:T(128)S(1)} %stack.23.flags, bf16[144,3072]{1,0:T(8,128)(2,1)S(1)} %get-tuple-element.31.mine, bf16[144,3072]{1,0:T(8,128)(2,1)S(1)} %collective-permute-done.4.other, bf16[1,336,3072]{2,1,0:T(8,128)(2,1)} %bitcast.16, bf16[1,336,3072]{2,1,0:T(8,128)(2,1)} %bitcast.18, ...), custom_call_target="tpu_custom_call" | custom-call | tf_op jit(solution)/shard_map/expert_front/pallas_call | solution.py:238
  55.8 0.0 copy-start
  55.9 4.9 %expert_back.1 = (bf16[8,144,384]{2,1,0:T(8,128)(2,1)S(1)}, bf16[8,144,384]{2,1,0:T(8,128)(2,1)S(1)}) custom-call(s32[5]{0:T(128)S(1)} %stack.23.flags, bf16[144,1008]{1,0:T(8,128)(2,1)S(1)} %expert_front.1.pieces.refs_0_, bf16[1,336,3072]{2,1,0:T(8,128)(2,1)} %bitcast.17, bf16[1,336,3072]{2,1,0:T(8,128)(2,1)} %bitcast.19, bf16[1,336,3072]{2,1,0:T(8,128)(2,1)} %down_w.3), custom_call_target="tpu_custom_call" | custom-call | flops 891813888 | bytes 6483456 | tf_op jit(solution)/shard_map/expert_back/pallas_call | solution.py:238
  60.7 2.1 %collective-permute-start.10 = (bf16[8,144,384]{2,1,0:T(8,128)(2,1)S(1)}, bf16[8,144,384]{2,1,0:T(8,128)(2,1)S(1)}, u32[]{:S(2)}, u32[]{:S(2)}) collective-permute-start(bf16[8,144,384]{2,1,0:T(8,128)(2,1)S(1)} %get-tuple-element.33), channel_id=1, source_target_pairs={{0,1},{1,0},{2,3},{3,2},{4,5},{5,4},{6,7},{7,6},{8,9},{9,8},{10,11... | collective-permute-start | bytes 2654216 | tf_op jit(solution)/shard_map/ppermute | solution.py:268
  62.9 3.7 %collective-permute-start.5 = (bf16[144,1008]{1,0:T(8,128)(2,1)S(1)}, bf16[144,1008]{1,0:T(8,128)(2,1)S(1)}, u32[]{:S(2)}, u32[]{:S(2)}) collective-permute-start(bf16[144,1008]{1,0:T(8,128)(2,1)S(1)} %expert_front.1.pieces.refs_0_), channel_id=1, source_target_pairs={{0,64},{64,128},{128,192},{192,256},{256,320},{320,384},{384,448},... | collective-permute-start | bytes 870920 | tf_op jit(solution)/shard_map/ppermute | solution.py:256
  66.6 0.0 copy-done
  66.6 3.3 %collective-permute-start.6 = (bf16[144,1008]{1,0:T(8,128)(2,1)S(1)}, bf16[144,1008]{1,0:T(8,128)(2,1)S(1)}, u32[]{:S(2)}, u32[]{:S(2)}) collective-permute-start(bf16[144,1008]{1,0:T(8,128)(2,1)S(1)} %expert_front.1.pieces.refs_0_), channel_id=1, source_target_pairs={{0,448},{64,0},{128,64},{192,128},{256,192},{320,256},{384,320},{4... | collective-permute-start | bytes 870920 | tf_op jit(solution)/shard_map/ppermute | solution.py:256
  69.9 0.0 collective-permute-done.10
  70.0 1.2 add_convert_fusion
  71.1 9.1 %collective-permute-done.5.refs_1_ = bf16[144,1008]{1,0:T(8,128)(2,1)S(1)} collective-permute-done((bf16[144,1008]{1,0:T(8,128)(2,1)S(1)}, bf16[144,1008]{1,0:T(8,128)(2,1)S(1)}, u32[]{:S(2)}, u32[]{:S(2)}) %collective-permute-start.5) | collective-permute-done | bytes 290336 | tf_op jit(solution)/shard_map/ppermute | solution.py:256
  80.2 0.0 copy-start.3
  80.2 0.0 collective-permute-done.6.refs_2_
  80.2 0.0 copy-start.4
  80.2 0.0 all-to-all-done.mine
  80.2 7.6 %all-to-all-start.1 = ((bf16[8,144,384]{2,1,0:T(8,128)(2,1)}), bf16[8,144,384]{2,1,0:T(8,128)(2,1)S(1)}, u32[]{:S(2)}, u32[]{:S(2)}) async-start(bf16[8,144,384]{2,1,0:T(8,128)(2,1)} %add_convert_fusion), calls=%async_computation.1 | async-start | bytes 1769472 | tf_op jit(solution)/shard_map/all_to_all | solution.py:331
  87.8 1.9 %collective-permute-start.3 = (bf16[8,144,384]{2,1,0:T(8,128)(2,1)S(1)}, bf16[8,144,384]{2,1,0:T(8,128)(2,1)S(1)}, u32[]{:S(2)}, u32[]{:S(2)}) collective-permute-start(bf16[8,144,384]{2,1,0:T(8,128)(2,1)S(1)} %all-to-all-done.mine), channel_id=1, source_target_pairs={{0,1},{1,0},{2,3},{3,2},{4,5},{5,4},{6,7},{7,6},{8,9},{9,8},{10,11... | collective-permute-start | bytes 2654216 | tf_op jit(solution)/shard_map/ppermute | solution.py:268
  89.8 2.8 %collective-permute-start.7 = (bf16[144,1008]{1,0:T(8,128)(2,1)S(1)}, bf16[144,1008]{1,0:T(8,128)(2,1)S(1)}, u32[]{:S(2)}, u32[]{:S(2)}) collective-permute-start(bf16[144,1008]{1,0:T(8,128)(2,1)S(1)} %collective-permute-done.5.refs_1_), channel_id=1, source_target_pairs={{0,64},{64,128},{128,192},{192,256},{256,320},{320,384},{384,448},... | collective-permute-start | bytes 870920 | tf_op jit(solution)/shard_map/ppermute | solution.py:256
  92.6 4.3 %collective-permute-start.8 = (bf16[144,1008]{1,0:T(8,128)(2,1)S(1)}, bf16[144,1008]{1,0:T(8,128)(2,1)}, u32[]{:S(2)}, u32[]{:S(2)}) collective-permute-start(bf16[144,1008]{1,0:T(8,128)(2,1)S(1)} %collective-permute-done.6.refs_2_), channel_id=1, source_target_pairs={{0,448},{64,0},{128,64},{192,128},{256,192},{320,256},{384,320},{4... | collective-permute-start | bytes 870920 | tf_op jit(solution)/shard_map/ppermute | solution.py:256
  96.8 5.4 %collective-permute-done.7.refs_3_ = bf16[144,1008]{1,0:T(8,128)(2,1)S(1)} collective-permute-done((bf16[144,1008]{1,0:T(8,128)(2,1)S(1)}, bf16[144,1008]{1,0:T(8,128)(2,1)S(1)}, u32[]{:S(2)}, u32[]{:S(2)}) %collective-permute-start.7) | collective-permute-done | bytes 290336 | tf_op jit(solution)/shard_map/ppermute | solution.py:256
  102.3 0.0 copy-start.5
  102.3 1.9 %collective-permute-start.9 = (bf16[144,1008]{1,0:T(8,128)(2,1)S(1)}, bf16[144,1008]{1,0:T(8,128)(2,1)}, u32[]{:S(2)}, u32[]{:S(2)}) collective-permute-start(bf16[144,1008]{1,0:T(8,128)(2,1)S(1)} %collective-permute-done.7.refs_3_), channel_id=1, source_target_pairs={{0,64},{64,128},{128,192},{192,256},{256,320},{320,384},{384,448},... | collective-permute-start | bytes 870920 | tf_op jit(solution)/shard_map/ppermute | solution.py:256
  104.2 0.0 collective-permute-done.8.refs_4_
  104.2 5.1 %collective-permute-start.11 = (bf16[144,1008]{1,0:T(8,128)(2,1)}, bf16[144,1008]{1,0:T(8,128)(2,1)}, u32[]{:S(2)}, u32[]{:S(2)}) collective-permute-start(bf16[144,1008]{1,0:T(8,128)(2,1)} %collective-permute-done.8.refs_4_), channel_id=1, source_target_pairs={{0,448},{64,0},{128,64},{192,128},{256,192},{320,256},{384,320},{4... | collective-permute-start | bytes 870920 | tf_op jit(solution)/shard_map/ppermute | solution.py:256
  109.3 3.7 %all-to-all-done.1.blocks = bf16[8,144,384]{2,1,0:T(8,128)(2,1)S(1)} async-done(((bf16[8,144,384]{2,1,0:T(8,128)(2,1)}), bf16[8,144,384]{2,1,0:T(8,128)(2,1)S(1)}, u32[]{:S(2)}, u32[]{:S(2)}) %all-to-all-start.1) | async-done | bytes 884768 | tf_op jit(solution)/shard_map/all_to_all | solution.py:331
  113.0 1.5 add_up.1
  114.5 0.0 collective-permute-done.9.refs_5_
  114.5 2.4 %collective-permute-start.12 = (bf16[144,1008]{1,0:T(8,128)(2,1)}, bf16[144,1008]{1,0:T(8,128)(2,1)}, u32[]{:S(2)}, u32[]{:S(2)}) collective-permute-start(bf16[144,1008]{1,0:T(8,128)(2,1)} %collective-permute-done.9.refs_5_), channel_id=1, source_target_pairs={{0,64},{64,128},{128,192},{192,256},{256,320},{320,384},{384,448},... | collective-permute-start | bytes 870920 | tf_op jit(solution)/shard_map/ppermute | solution.py:256
  117.0 3.3 %all-to-all-start.2 = ((bf16[4,40,384]{2,1,0:T(8,128)(2,1)}), bf16[4,40,384]{2,1,0:T(8,128)(2,1)S(1)}, u32[]{:S(2)}, u32[]{:S(2)}) async-start(bf16[4,40,384]{2,1,0:T(8,128)(2,1)} %add_up.1), calls=%async_computation.2 | async-start | bytes 245760 | tf_op jit(solution)/shard_map/all_to_all | solution.py:335
  120.3 0.0 copy-done.3
  120.3 0.0 copy-done.4
  120.3 0.0 copy-done.5
  120.3 0.0 collective-permute-done.3.other
  120.3 3.5 %weight_grads.1.total = f32[384,1008]{1,0:T(8,128)S(1)} custom-call(s32[5]{0:T(128)S(1)} %stack.23.flags, bf16[8,144,384]{2,1,0:T(8,128)(2,1)S(1)} %all-to-all-done.mine, bf16[8,144,384]{2,1,0:T(8,128)(2,1)S(1)} %collective-permute-done.3.other, bf16[144,1008]{1,0:T(8,128)(2,1)} %copy-done, bf16[144,1008]{1,0:T(8,128)(2,1)} %copy-done.3, ...), custom_call_target="tpu_custom_call" | custom-call | flops 668860416 | bytes 3511296 | tf_op jit(solution)/shard_map/weight_grads/pallas_call | solution.py:238
  123.8 0.0 copy-start.1
  123.8 0.0 copy-start.2
  123.9 1.5 all-to-all-done.2
  125.4 0.0 collective-permute-done.11.refs_0_
  125.4 1.5 collective-permute-done.12.refs_1_
  126.8 2.0 %weight_grads_last.1 = (f32[192,1008]{1,0:T(8,128)S(1)}, bf16[192,1008]{1,0:T(8,128)(2,1)S(1)}) custom-call(s32[5]{0:T(128)S(1)} %stack.23.flags, bf16[8,144,384]{2,1,0:T(8,128)(2,1)S(1)} %all-to-all-done.mine, bf16[8,144,384]{2,1,0:T(8,128)(2,1)S(1)} %collective-permute-done.3.other, f32[384,1008]{1,0:T(8,128)S(1)} %weight_grads.1.total, ...), custom_call_target="tpu_custom_call" | custom-call | tf_op jit(solution)/shard_map/weight_grads_last/pallas_call | solution.py:238
  128.9 2.3 %collective-permute-start.13 = (bf16[192,1008]{1,0:T(8,128)(2,1)S(1)}, bf16[192,1008]{1,0:T(8,128)(2,1)S(1)}, u32[]{:S(2)}, u32[]{:S(2)}) collective-permute-start(bf16[192,1008]{1,0:T(8,128)(2,1)S(1)} %get-tuple-element.37), channel_id=1, source_target_pairs={{0,512},{512,0},{1,513},{513,1},{2,514},{514,2},{3,515},{515,3},{4... | collective-permute-start | bytes 1161224 | tf_op jit(solution)/shard_map/ppermute | solution.py:268
  131.2 0.0 copy-done.1
  131.2 0.0 copy-done.2
  131.2 1.1 combine.1
  132.2 20.2 %collective-permute-done.13.got = bf16[192,1008]{1,0:T(8,128)(2,1)S(1)} collective-permute-done((bf16[192,1008]{1,0:T(8,128)(2,1)S(1)}, bf16[192,1008]{1,0:T(8,128)(2,1)S(1)}, u32[]{:S(2)}, u32[]{:S(2)}) %collective-permute-start.13) | collective-permute-done | bytes 387104 | tf_op jit(solution)/shard_map/ppermute | solution.py:268
  152.4 1.1 finish.1
Async XLA Ops:
  2.7 10.7 %collective-permute-start = (bf16[40,3072]{1,0:T(8,128)(2,1)S(1)}, bf16[40,3072]{1,0:T(8,128)(2,1)S(1)}, u32[]{:S(2)}, u32[]{:S(2)}) collective-permute-start(bf16[40,3072]{1,0:T(8,128)(2,1)S(1)} %get-tuple-element.27), channel_id=1, source_target_pairs={{0,16},{16,32},{32,48},{48,0},{1,17},{17,33},{33,49},{49,1},{2,18}... | collective-permute-start | bytes 737288 | tf_op jit(solution)/shard_map/ppermute | solution.py:262
  5.2 21.0 %collective-permute-start.1 = (bf16[40,3072]{1,0:T(8,128)(2,1)S(1)}, bf16[40,3072]{1,0:T(8,128)(2,1)S(1)}, u32[]{:S(2)}, u32[]{:S(2)}) collective-permute-start(bf16[40,3072]{1,0:T(8,128)(2,1)S(1)} %get-tuple-element.28), channel_id=1, source_target_pairs={{0,32},{16,48},{32,0},{48,16},{1,33},{17,49},{33,1},{49,17},{2,34}... | collective-permute-start | bytes 737288 | tf_op jit(solution)/shard_map/ppermute | solution.py:262
  10.3 19.8 %collective-permute-start.2 = (bf16[40,3072]{1,0:T(8,128)(2,1)S(1)}, bf16[40,3072]{1,0:T(8,128)(2,1)S(1)}, u32[]{:S(2)}, u32[]{:S(2)}) collective-permute-start(bf16[40,3072]{1,0:T(8,128)(2,1)S(1)} %get-tuple-element.29), channel_id=1, source_target_pairs={{0,48},{16,0},{32,16},{48,32},{1,49},{17,1},{33,17},{49,33},{2,50}... | collective-permute-start | bytes 737288 | tf_op jit(solution)/shard_map/ppermute | solution.py:262
  32.3 18.4 %collective-permute-start.4 = (bf16[144,3072]{1,0:T(8,128)(2,1)S(1)}, bf16[144,3072]{1,0:T(8,128)(2,1)S(1)}, u32[]{:S(2)}, u32[]{:S(2)}) collective-permute-start(bf16[144,3072]{1,0:T(8,128)(2,1)S(1)} %get-tuple-element.31.mine), channel_id=1, source_target_pairs={{0,1},{1,0},{2,3},{3,2},{4,5},{5,4},{6,7},{7,6},{8,9},{9,8},{10,11... | collective-permute-start | bytes 2654216 | tf_op jit(solution)/shard_map/ppermute | solution.py:268
  34.2 46.0 %all-to-all-start = ((bf16[8,144,384]{2,1,0:T(8,128)(2,1)}), bf16[8,144,384]{2,1,0:T(8,128)(2,1)S(1)}, u32[]{:S(2)}, u32[]{:S(2)}) async-start(bf16[8,144,384]{2,1,0:T(8,128)(2,1)} %get-tuple-element.30), calls=%async_computation | async-start | bytes 1769472 | tf_op jit(solution)/shard_map/all_to_all | solution.py:309
  55.8 10.8 %copy-start = (bf16[144,1008]{1,0:T(8,128)(2,1)}, bf16[144,1008]{1,0:T(8,128)(2,1)S(1)}, u32[]{:S(2)}) copy-start(bf16[144,1008]{1,0:T(8,128)(2,1)S(1)} %expert_front.1.pieces.refs_0_) | copy-start | bytes 870916
  60.7 9.2 %collective-permute-start.10 = (bf16[8,144,384]{2,1,0:T(8,128)(2,1)S(1)}, bf16[8,144,384]{2,1,0:T(8,128)(2,1)S(1)}, u32[]{:S(2)}, u32[]{:S(2)}) collective-permute-start(bf16[8,144,384]{2,1,0:T(8,128)(2,1)S(1)} %get-tuple-element.33), channel_id=1, source_target_pairs={{0,1},{1,0},{2,3},{3,2},{4,5},{5,4},{6,7},{7,6},{8,9},{9,8},{10,11... | collective-permute-start | bytes 2654216 | tf_op jit(solution)/shard_map/ppermute | solution.py:268
  62.9 17.3 %collective-permute-start.5 = (bf16[144,1008]{1,0:T(8,128)(2,1)S(1)}, bf16[144,1008]{1,0:T(8,128)(2,1)S(1)}, u32[]{:S(2)}, u32[]{:S(2)}) collective-permute-start(bf16[144,1008]{1,0:T(8,128)(2,1)S(1)} %expert_front.1.pieces.refs_0_), channel_id=1, source_target_pairs={{0,64},{64,128},{128,192},{192,256},{256,320},{320,384},{384,448},... | collective-permute-start | bytes 870920 | tf_op jit(solution)/shard_map/ppermute | solution.py:256
  66.6 13.6 %collective-permute-start.6 = (bf16[144,1008]{1,0:T(8,128)(2,1)S(1)}, bf16[144,1008]{1,0:T(8,128)(2,1)S(1)}, u32[]{:S(2)}, u32[]{:S(2)}) collective-permute-start(bf16[144,1008]{1,0:T(8,128)(2,1)S(1)} %expert_front.1.pieces.refs_0_), channel_id=1, source_target_pairs={{0,448},{64,0},{128,64},{192,128},{256,192},{320,256},{384,320},{4... | collective-permute-start | bytes 870920 | tf_op jit(solution)/shard_map/ppermute | solution.py:256
  80.2 40.1 %copy-start.3 = (bf16[144,1008]{1,0:T(8,128)(2,1)}, bf16[144,1008]{1,0:T(8,128)(2,1)S(1)}, u32[]{:S(2)}) copy-start(bf16[144,1008]{1,0:T(8,128)(2,1)S(1)} %collective-permute-done.5.refs_1_) | copy-start | bytes 870916
  80.2 40.1 %copy-start.4 = (bf16[144,1008]{1,0:T(8,128)(2,1)}, bf16[144,1008]{1,0:T(8,128)(2,1)S(1)}, u32[]{:S(2)}) copy-start(bf16[144,1008]{1,0:T(8,128)(2,1)S(1)} %collective-permute-done.6.refs_2_) | copy-start | bytes 870916
  80.2 32.8 %all-to-all-start.1 = ((bf16[8,144,384]{2,1,0:T(8,128)(2,1)}), bf16[8,144,384]{2,1,0:T(8,128)(2,1)S(1)}, u32[]{:S(2)}, u32[]{:S(2)}) async-start(bf16[8,144,384]{2,1,0:T(8,128)(2,1)} %add_convert_fusion), calls=%async_computation.1 | async-start | bytes 1769472 | tf_op jit(solution)/shard_map/all_to_all | solution.py:331
  87.8 32.5 %collective-permute-start.3 = (bf16[8,144,384]{2,1,0:T(8,128)(2,1)S(1)}, bf16[8,144,384]{2,1,0:T(8,128)(2,1)S(1)}, u32[]{:S(2)}, u32[]{:S(2)}) collective-permute-start(bf16[8,144,384]{2,1,0:T(8,128)(2,1)S(1)} %all-to-all-done.mine), channel_id=1, source_target_pairs={{0,1},{1,0},{2,3},{3,2},{4,5},{5,4},{6,7},{7,6},{8,9},{9,8},{10,11... | collective-permute-start | bytes 2654216 | tf_op jit(solution)/shard_map/ppermute | solution.py:268
  89.8 12.5 %collective-permute-start.7 = (bf16[144,1008]{1,0:T(8,128)(2,1)S(1)}, bf16[144,1008]{1,0:T(8,128)(2,1)S(1)}, u32[]{:S(2)}, u32[]{:S(2)}) collective-permute-start(bf16[144,1008]{1,0:T(8,128)(2,1)S(1)} %collective-permute-done.5.refs_1_), channel_id=1, source_target_pairs={{0,64},{64,128},{128,192},{192,256},{256,320},{320,384},{384,448},... | collective-permute-start | bytes 870920 | tf_op jit(solution)/shard_map/ppermute | solution.py:256
  92.6 11.6 %collective-permute-start.8 = (bf16[144,1008]{1,0:T(8,128)(2,1)S(1)}, bf16[144,1008]{1,0:T(8,128)(2,1)}, u32[]{:S(2)}, u32[]{:S(2)}) collective-permute-start(bf16[144,1008]{1,0:T(8,128)(2,1)S(1)} %collective-permute-done.6.refs_2_), channel_id=1, source_target_pairs={{0,448},{64,0},{128,64},{192,128},{256,192},{320,256},{384,320},{4... | collective-permute-start | bytes 870920 | tf_op jit(solution)/shard_map/ppermute | solution.py:256
  102.3 18.0 %copy-start.5 = (bf16[144,1008]{1,0:T(8,128)(2,1)}, bf16[144,1008]{1,0:T(8,128)(2,1)S(1)}, u32[]{:S(2)}) copy-start(bf16[144,1008]{1,0:T(8,128)(2,1)S(1)} %collective-permute-done.7.refs_3_) | copy-start | bytes 870916
  102.3 12.2 %collective-permute-start.9 = (bf16[144,1008]{1,0:T(8,128)(2,1)S(1)}, bf16[144,1008]{1,0:T(8,128)(2,1)}, u32[]{:S(2)}, u32[]{:S(2)}) collective-permute-start(bf16[144,1008]{1,0:T(8,128)(2,1)S(1)} %collective-permute-done.7.refs_3_), channel_id=1, source_target_pairs={{0,64},{64,128},{128,192},{192,256},{256,320},{320,384},{384,448},... | collective-permute-start | bytes 870920 | tf_op jit(solution)/shard_map/ppermute | solution.py:256
  104.2 21.2 %collective-permute-start.11 = (bf16[144,1008]{1,0:T(8,128)(2,1)}, bf16[144,1008]{1,0:T(8,128)(2,1)}, u32[]{:S(2)}, u32[]{:S(2)}) collective-permute-start(bf16[144,1008]{1,0:T(8,128)(2,1)} %collective-permute-done.8.refs_4_), channel_id=1, source_target_pairs={{0,448},{64,0},{128,64},{192,128},{256,192},{320,256},{384,320},{4... | collective-permute-start | bytes 870920 | tf_op jit(solution)/shard_map/ppermute | solution.py:256
  114.5 12.3 %collective-permute-start.12 = (bf16[144,1008]{1,0:T(8,128)(2,1)}, bf16[144,1008]{1,0:T(8,128)(2,1)}, u32[]{:S(2)}, u32[]{:S(2)}) collective-permute-start(bf16[144,1008]{1,0:T(8,128)(2,1)} %collective-permute-done.9.refs_5_), channel_id=1, source_target_pairs={{0,64},{64,128},{128,192},{192,256},{256,320},{320,384},{384,448},... | collective-permute-start | bytes 870920 | tf_op jit(solution)/shard_map/ppermute | solution.py:256
  117.0 8.4 %all-to-all-start.2 = ((bf16[4,40,384]{2,1,0:T(8,128)(2,1)}), bf16[4,40,384]{2,1,0:T(8,128)(2,1)S(1)}, u32[]{:S(2)}, u32[]{:S(2)}) async-start(bf16[4,40,384]{2,1,0:T(8,128)(2,1)} %add_up.1), calls=%async_computation.2 | async-start | bytes 245760 | tf_op jit(solution)/shard_map/all_to_all | solution.py:335
  123.8 7.3 %copy-start.1 = (s32[64,2]{0,1:T(2,128)S(1)}, s32[64,2]{0,1:T(2,128)}, u32[]{:S(2)}) copy-start(s32[64,2]{0,1:T(2,128)} %param.9) | copy-start | bytes 1540
  123.8 7.3 %copy-start.2 = (f32[64,2]{0,1:T(2,128)S(1)}, f32[64,2]{0,1:T(2,128)}, u32[]{:S(2)}) copy-start(f32[64,2]{0,1:T(2,128)} %param.10) | copy-start | bytes 1540
  128.9 23.6 %collective-permute-start.13 = (bf16[192,1008]{1,0:T(8,128)(2,1)S(1)}, bf16[192,1008]{1,0:T(8,128)(2,1)S(1)}, u32[]{:S(2)}, u32[]{:S(2)}) collective-permute-start(bf16[192,1008]{1,0:T(8,128)(2,1)S(1)} %get-tuple-element.37), channel_id=1, source_target_pairs={{0,512},{512,0},{1,513},{513,1},{2,514},{514,2},{3,515},{515,3},{4... | collective-permute-start | bytes 1161224 | tf_op jit(solution)/shard_map/ppermute | solution.py:268

commit v6 on v5

--- a/solution.py
+++ b/solution.py
@@ -355,7 +355,6 @@
         ),
         flops=2 * len(SOON) * rows * 2 * part * 3 * ff,
     )
-    total, _ = lax.optimization_barrier((total, back))
     kept, given = call(
         weight_grads_last,
         [((part, 3 * ff), F32), ((part, 3 * ff), BF16)],
@@ -365,6 +364,7 @@
         total,
         *[found[k] for k in LAST],
     )
+    given, _ = lax.optimization_barrier((given, back))
     received, layer_out, token_grad = lax.optimization_barrier(
         (swap(given, "xh"), layer_out, token_grad)
     )

time: 154 us -> 155 us (level)
  transfers between devices with their start and end apart: 17 -> 17, of which waited for: 9 -> 8; matrix products, arithmetic and copies ran while one was open for 1% -> 1% of each run, Pallas kernels for 10% -> 11%
where the time goes in v6:
time: 155 us; the launch traced here: 154 us
  starting transfers between devices  68.8 us (44%)
  waiting for transfers between devices  59.4 us (38%)
  Pallas kernels  22.7 us (15%)
    ppermute x7, starting transfers between devices, shift(): return lax.ppermute(value, 'z', [(i, (i + by) % N_Z) for i in range(N_Z)])  23.6 us
    pallas_call x9, Pallas kernels, call(): pl.pallas_call(body, out_shape=[jax.ShapeDtypeStruct(s, t) if i < len(out...  22.7 us
    ppermute x4, waiting for transfers between devices, swap(): return lax.ppermute(value, axis, [(0, 1), (1, 0)])  20.4 us
    ppermute x3, waiting for transfers between devices, spread(): lax.ppermute(parts[k], axis, [(i, (i + forward * k) % count) for i in ran...  17.9 us
    ppermute x7, waiting for transfers between devices, shift(): return lax.ppermute(value, 'z', [(i, (i + by) % N_Z) for i in range(N_Z)])  17.4 us
    all_to_all x1, starting transfers between devices, on_device(): cols = lax.all_to_all(cols, 'z', split_axis=0, concat_axis=0, tiled=True)  16.5 us
    ppermute x3, starting transfers between devices, spread(): lax.ppermute(parts[k], axis, [(i, (i + forward * k) % count) for i in ran...  9.52 us
    ppermute x4, starting transfers between devices, swap(): return lax.ppermute(value, axis, [(0, 1), (1, 0)])  8.25 us
  transfers between devices with their start and end apart: 17, of which 8 were waited for; matrix products, arithmetic and copies ran while one was open for 1% of the time, Pallas kernels for 11%

profile of v6, /device:TPU:10, one launch (start us, length us, event | category | flops | bytes accessed | tf_op | source)
XLA Modules:
  0.0 153.8 jit_solution(9967764243134999379)
XLA Ops:
  0.6 0.1 stack.23.flags
  0.7 2.0 %dispatch.1 = (bf16[40,3072]{1,0:T(8,128)(2,1)S(1)}, bf16[40,3072]{1,0:T(8,128)(2,1)S(1)}, bf16[40,3072]{1,0:T(8,128)(2,1)S(1)}, bf16[40,3072]{1,0:T(8,128)(2,1)S(1)}) custom-call(s32[5]{0:T(128)S(1)} %stack.23.flags, s32[2,64]{1,0:T(2,128)} %bitcast.12, f32[2,64]{1,0:T(2,128)} %bitcast.14, bf16[64,3072]{1,0:T(8,128)(2,1)} %tokens.1, bf16[64,3072]{1,0:T(8,128)(2,1)} %cotangent.1), custom_call_target="tpu_custom_call" | custom-call | tf_op jit(solution)/shard_map/dispatch/pallas_call | solution.py:238
  2.7 2.5 %collective-permute-start = (bf16[40,3072]{1,0:T(8,128)(2,1)S(1)}, bf16[40,3072]{1,0:T(8,128)(2,1)S(1)}, u32[]{:S(2)}, u32[]{:S(2)}) collective-permute-start(bf16[40,3072]{1,0:T(8,128)(2,1)S(1)} %get-tuple-element.27), channel_id=1, source_target_pairs={{0,16},{16,32},{32,48},{48,0},{1,17},{17,33},{33,49},{49,1},{2,18}... | collective-permute-start | bytes 737288 | tf_op jit(solution)/shard_map/ppermute | solution.py:262
  5.2 5.1 %collective-permute-start.1 = (bf16[40,3072]{1,0:T(8,128)(2,1)S(1)}, bf16[40,3072]{1,0:T(8,128)(2,1)S(1)}, u32[]{:S(2)}, u32[]{:S(2)}) collective-permute-start(bf16[40,3072]{1,0:T(8,128)(2,1)S(1)} %get-tuple-element.28), channel_id=1, source_target_pairs={{0,32},{16,48},{32,0},{48,16},{1,33},{17,49},{33,1},{49,17},{2,34}... | collective-permute-start | bytes 737288 | tf_op jit(solution)/shard_map/ppermute | solution.py:262
  10.3 1.9 %collective-permute-start.2 = (bf16[40,3072]{1,0:T(8,128)(2,1)S(1)}, bf16[40,3072]{1,0:T(8,128)(2,1)S(1)}, u32[]{:S(2)}, u32[]{:S(2)}) collective-permute-start(bf16[40,3072]{1,0:T(8,128)(2,1)S(1)} %get-tuple-element.29), channel_id=1, source_target_pairs={{0,48},{16,0},{32,16},{48,32},{1,49},{17,1},{33,17},{49,33},{2,50}... | collective-permute-start | bytes 737288 | tf_op jit(solution)/shard_map/ppermute | solution.py:262
  12.3 1.2 collective-permute-done.refs_1_
  13.5 12.8 %collective-permute-done.1.refs_2_ = bf16[40,3072]{1,0:T(8,128)(2,1)S(1)} collective-permute-done((bf16[40,3072]{1,0:T(8,128)(2,1)S(1)}, bf16[40,3072]{1,0:T(8,128)(2,1)S(1)}, u32[]{:S(2)}, u32[]{:S(2)}) %collective-permute-start.1) | collective-permute-done | bytes 245792 | tf_op jit(solution)/shard_map/ppermute | solution.py:262
  26.2 3.9 %collective-permute-done.2.refs_3_ = bf16[40,3072]{1,0:T(8,128)(2,1)S(1)} collective-permute-done((bf16[40,3072]{1,0:T(8,128)(2,1)S(1)}, bf16[40,3072]{1,0:T(8,128)(2,1)S(1)}, u32[]{:S(2)}, u32[]{:S(2)}) %collective-permute-start.2) | collective-permute-done | bytes 245792 | tf_op jit(solution)/shard_map/ppermute | solution.py:262
  30.2 2.1 %squeeze.1 = (bf16[144,3072]{1,0:T(8,128)(2,1)S(1)}, bf16[8,144,384]{2,1,0:T(8,128)(2,1)}) custom-call(s32[5]{0:T(128)S(1)} %stack.23.flags, bf16[40,3072]{1,0:T(8,128)(2,1)S(1)} %get-tuple-element.26.refs_0_, bf16[40,3072]{1,0:T(8,128)(2,1)S(1)} %collective-permute-done.refs_1_, bf16[40,3072]{1,0:T(8,128)(2,1)S(1)} %collective-permute-done.1.refs_2_, ...), custom_call_target="tpu_custom_call" | custom-call | tf_op jit(solution)/shard_map/squeeze/pallas_call | solution.py:238
  32.3 1.9 %collective-permute-start.4 = (bf16[144,3072]{1,0:T(8,128)(2,1)S(1)}, bf16[144,3072]{1,0:T(8,128)(2,1)S(1)}, u32[]{:S(2)}, u32[]{:S(2)}) collective-permute-start(bf16[144,3072]{1,0:T(8,128)(2,1)S(1)} %get-tuple-element.31.mine), channel_id=1, source_target_pairs={{0,1},{1,0},{2,3},{3,2},{4,5},{5,4},{6,7},{7,6},{8,9},{9,8},{10,11... | collective-permute-start | bytes 2654216 | tf_op jit(solution)/shard_map/ppermute | solution.py:268
  34.2 16.5 %all-to-all-start = ((bf16[8,144,384]{2,1,0:T(8,128)(2,1)}), bf16[8,144,384]{2,1,0:T(8,128)(2,1)S(1)}, u32[]{:S(2)}, u32[]{:S(2)}) async-start(bf16[8,144,384]{2,1,0:T(8,128)(2,1)} %get-tuple-element.30), calls=%async_computation | async-start | bytes 1769472 | tf_op jit(solution)/shard_map/all_to_all | solution.py:309
  50.7 0.0 collective-permute-done.4.other
  50.7 5.1 %expert_front.1.pieces.refs_0_ = bf16[144,1008]{1,0:T(8,128)(2,1)S(1)} custom-call(s32[5]{0:T(128)S(1)} %stack.23.flags, bf16[144,3072]{1,0:T(8,128)(2,1)S(1)} %get-tuple-element.31.mine, bf16[144,3072]{1,0:T(8,128)(2,1)S(1)} %collective-permute-done.4.other, bf16[1,336,3072]{2,1,0:T(8,128)(2,1)} %bitcast.16, bf16[1,336,3072]{2,1,0:T(8,128)(2,1)} %bitcast.18, ...), custom_call_target="tpu_custom_call" | custom-call | tf_op jit(solution)/shard_map/expert_front/pallas_call | solution.py:238
  55.8 0.0 copy-start
  55.9 4.9 %expert_back.1 = (bf16[8,144,384]{2,1,0:T(8,128)(2,1)S(1)}, bf16[8,144,384]{2,1,0:T(8,128)(2,1)S(1)}) custom-call(s32[5]{0:T(128)S(1)} %stack.23.flags, bf16[144,1008]{1,0:T(8,128)(2,1)S(1)} %expert_front.1.pieces.refs_0_, bf16[1,336,3072]{2,1,0:T(8,128)(2,1)} %bitcast.17, bf16[1,336,3072]{2,1,0:T(8,128)(2,1)} %bitcast.19, bf16[1,336,3072]{2,1,0:T(8,128)(2,1)} %down_w.3), custom_call_target="tpu_custom_call" | custom-call | flops 891813888 | bytes 6483456 | tf_op jit(solution)/shard_map/expert_back/pallas_call | solution.py:238
  60.7 2.1 %collective-permute-start.10 = (bf16[8,144,384]{2,1,0:T(8,128)(2,1)S(1)}, bf16[8,144,384]{2,1,0:T(8,128)(2,1)S(1)}, u32[]{:S(2)}, u32[]{:S(2)}) collective-permute-start(bf16[8,144,384]{2,1,0:T(8,128)(2,1)S(1)} %get-tuple-element.33), channel_id=1, source_target_pairs={{0,1},{1,0},{2,3},{3,2},{4,5},{5,4},{6,7},{7,6},{8,9},{9,8},{10,11... | collective-permute-start | bytes 2654216 | tf_op jit(solution)/shard_map/ppermute | solution.py:268
  62.9 3.7 %collective-permute-start.5 = (bf16[144,1008]{1,0:T(8,128)(2,1)S(1)}, bf16[144,1008]{1,0:T(8,128)(2,1)S(1)}, u32[]{:S(2)}, u32[]{:S(2)}) collective-permute-start(bf16[144,1008]{1,0:T(8,128)(2,1)S(1)} %expert_front.1.pieces.refs_0_), channel_id=1, source_target_pairs={{0,64},{64,128},{128,192},{192,256},{256,320},{320,384},{384,448},... | collective-permute-start | bytes 870920 | tf_op jit(solution)/shard_map/ppermute | solution.py:256
  66.6 0.0 copy-done
  66.6 3.3 %collective-permute-start.6 = (bf16[144,1008]{1,0:T(8,128)(2,1)S(1)}, bf16[144,1008]{1,0:T(8,128)(2,1)S(1)}, u32[]{:S(2)}, u32[]{:S(2)}) collective-permute-start(bf16[144,1008]{1,0:T(8,128)(2,1)S(1)} %expert_front.1.pieces.refs_0_), channel_id=1, source_target_pairs={{0,448},{64,0},{128,64},{192,128},{256,192},{320,256},{384,320},{4... | collective-permute-start | bytes 870920 | tf_op jit(solution)/shard_map/ppermute | solution.py:256
  69.9 0.0 collective-permute-done.10
  69.9 1.2 add_convert_fusion
  71.1 9.1 %collective-permute-done.5.refs_1_ = bf16[144,1008]{1,0:T(8,128)(2,1)S(1)} collective-permute-done((bf16[144,1008]{1,0:T(8,128)(2,1)S(1)}, bf16[144,1008]{1,0:T(8,128)(2,1)S(1)}, u32[]{:S(2)}, u32[]{:S(2)}) %collective-permute-start.5) | collective-permute-done | bytes 290336 | tf_op jit(solution)/shard_map/ppermute | solution.py:256
  80.2 0.0 copy-start.4
  80.2 0.0 collective-permute-done.6.refs_2_
  80.2 0.0 copy-start.5
  80.2 0.0 all-to-all-done.mine
  80.2 7.6 %all-to-all-start.1 = ((bf16[8,144,384]{2,1,0:T(8,128)(2,1)}), bf16[8,144,384]{2,1,0:T(8,128)(2,1)S(1)}, u32[]{:S(2)}, u32[]{:S(2)}) async-start(bf16[8,144,384]{2,1,0:T(8,128)(2,1)} %add_convert_fusion), calls=%async_computation.1 | async-start | bytes 1769472 | tf_op jit(solution)/shard_map/all_to_all | solution.py:331
  87.8 1.9 %collective-permute-start.3 = (bf16[8,144,384]{2,1,0:T(8,128)(2,1)S(1)}, bf16[8,144,384]{2,1,0:T(8,128)(2,1)S(1)}, u32[]{:S(2)}, u32[]{:S(2)}) collective-permute-start(bf16[8,144,384]{2,1,0:T(8,128)(2,1)S(1)} %all-to-all-done.mine), channel_id=1, source_target_pairs={{0,1},{1,0},{2,3},{3,2},{4,5},{5,4},{6,7},{7,6},{8,9},{9,8},{10,11... | collective-permute-start | bytes 2654216 | tf_op jit(solution)/shard_map/ppermute | solution.py:268
  89.7 2.8 %collective-permute-start.7 = (bf16[144,1008]{1,0:T(8,128)(2,1)S(1)}, bf16[144,1008]{1,0:T(8,128)(2,1)S(1)}, u32[]{:S(2)}, u32[]{:S(2)}) collective-permute-start(bf16[144,1008]{1,0:T(8,128)(2,1)S(1)} %collective-permute-done.5.refs_1_), channel_id=1, source_target_pairs={{0,64},{64,128},{128,192},{192,256},{256,320},{320,384},{384,448},... | collective-permute-start | bytes 870920 | tf_op jit(solution)/shard_map/ppermute | solution.py:256
  92.5 4.3 %collective-permute-start.8 = (bf16[144,1008]{1,0:T(8,128)(2,1)S(1)}, bf16[144,1008]{1,0:T(8,128)(2,1)}, u32[]{:S(2)}, u32[]{:S(2)}) collective-permute-start(bf16[144,1008]{1,0:T(8,128)(2,1)S(1)} %collective-permute-done.6.refs_2_), channel_id=1, source_target_pairs={{0,448},{64,0},{128,64},{192,128},{256,192},{320,256},{384,320},{4... | collective-permute-start | bytes 870920 | tf_op jit(solution)/shard_map/ppermute | solution.py:256
  96.8 5.4 %collective-permute-done.7.refs_3_ = bf16[144,1008]{1,0:T(8,128)(2,1)S(1)} collective-permute-done((bf16[144,1008]{1,0:T(8,128)(2,1)S(1)}, bf16[144,1008]{1,0:T(8,128)(2,1)S(1)}, u32[]{:S(2)}, u32[]{:S(2)}) %collective-permute-start.7) | collective-permute-done | bytes 290336 | tf_op jit(solution)/shard_map/ppermute | solution.py:256
  102.3 0.0 copy-start.6
  102.3 1.9 %collective-permute-start.9 = (bf16[144,1008]{1,0:T(8,128)(2,1)S(1)}, bf16[144,1008]{1,0:T(8,128)(2,1)}, u32[]{:S(2)}, u32[]{:S(2)}) collective-permute-start(bf16[144,1008]{1,0:T(8,128)(2,1)S(1)} %collective-permute-done.7.refs_3_), channel_id=1, source_target_pairs={{0,64},{64,128},{128,192},{192,256},{256,320},{320,384},{384,448},... | collective-permute-start | bytes 870920 | tf_op jit(solution)/shard_map/ppermute | solution.py:256
  104.2 0.0 copy-done.4
  104.2 0.0 collective-permute-done.8.refs_4_
  104.2 5.1 %collective-permute-start.11 = (bf16[144,1008]{1,0:T(8,128)(2,1)}, bf16[144,1008]{1,0:T(8,128)(2,1)S(1)}, u32[]{:S(2)}, u32[]{:S(2)}) collective-permute-start(bf16[144,1008]{1,0:T(8,128)(2,1)} %collective-permute-done.8.refs_4_), channel_id=1, source_target_pairs={{0,448},{64,0},{128,64},{192,128},{256,192},{320,256},{384,320},{4... | collective-permute-start | bytes 870920 | tf_op jit(solution)/shard_map/ppermute | solution.py:256
  109.3 3.7 %all-to-all-done.1.blocks = bf16[8,144,384]{2,1,0:T(8,128)(2,1)S(1)} async-done(((bf16[8,144,384]{2,1,0:T(8,128)(2,1)}), bf16[8,144,384]{2,1,0:T(8,128)(2,1)S(1)}, u32[]{:S(2)}, u32[]{:S(2)}) %all-to-all-start.1) | async-done | bytes 884768 | tf_op jit(solution)/shard_map/all_to_all | solution.py:331
  113.0 1.5 add_up.1
  114.5 0.0 copy-done.5
  114.5 0.0 copy-done.6
  114.5 0.0 collective-permute-done.9.refs_5_
  114.5 2.4 %collective-permute-start.12 = (bf16[144,1008]{1,0:T(8,128)(2,1)}, bf16[144,1008]{1,0:T(8,128)(2,1)S(1)}, u32[]{:S(2)}, u32[]{:S(2)}) collective-permute-start(bf16[144,1008]{1,0:T(8,128)(2,1)} %collective-permute-done.9.refs_5_), channel_id=1, source_target_pairs={{0,64},{64,128},{128,192},{192,256},{256,320},{320,384},{384,448},... | collective-permute-start | bytes 870920 | tf_op jit(solution)/shard_map/ppermute | solution.py:256
  117.0 3.3 %all-to-all-start.2 = ((bf16[4,40,384]{2,1,0:T(8,128)(2,1)}), bf16[4,40,384]{2,1,0:T(8,128)(2,1)S(1)}, u32[]{:S(2)}, u32[]{:S(2)}) async-start(bf16[4,40,384]{2,1,0:T(8,128)(2,1)} %add_up.1), calls=%async_computation.2 | async-start | bytes 245760 | tf_op jit(solution)/shard_map/all_to_all | solution.py:335
  120.3 0.0 collective-permute-done.3.other
  120.3 3.5 %weight_grads.1.total = f32[384,1008]{1,0:T(8,128)S(1)} custom-call(s32[5]{0:T(128)S(1)} %stack.23.flags, bf16[8,144,384]{2,1,0:T(8,128)(2,1)S(1)} %all-to-all-done.mine, bf16[8,144,384]{2,1,0:T(8,128)(2,1)S(1)} %collective-permute-done.3.other, bf16[144,1008]{1,0:T(8,128)(2,1)} %copy-done, bf16[144,1008]{1,0:T(8,128)(2,1)} %copy-done.4, ...), custom_call_target="tpu_custom_call" | custom-call | flops 668860416 | bytes 3511296 | tf_op jit(solution)/shard_map/weight_grads/pallas_call | solution.py:238
  123.8 0.0 copy-start.1
  123.8 0.0 copy-start.2
  123.8 0.0 collective-permute-done.11.refs_0_
  123.8 2.9 %collective-permute-done.12.refs_1_ = bf16[144,1008]{1,0:T(8,128)(2,1)S(1)} collective-permute-done((bf16[144,1008]{1,0:T(8,128)(2,1)}, bf16[144,1008]{1,0:T(8,128)(2,1)S(1)}, u32[]{:S(2)}, u32[]{:S(2)}) %collective-permute-start.12) | collective-permute-done | bytes 290336 | tf_op jit(solution)/shard_map/ppermute | solution.py:256
  126.8 1.5 weight_grads_last.1
  128.2 0.0 copy-start.3
  128.3 0.7 copy-done.3
  129.0 0.0 all-to-all-done.2
  129.0 2.3 %collective-permute-start.13 = (bf16[192,1008]{1,0:T(8,128)(2,1)}, bf16[192,1008]{1,0:T(8,128)(2,1)S(1)}, u32[]{:S(2)}, u32[]{:S(2)}) collective-permute-start(bf16[192,1008]{1,0:T(8,128)(2,1)} %copy-done.3), channel_id=1, source_target_pairs={{0,512},{512,0},{1,513},{513,1},{2,514},{514,2},{3,515},{515,3},{4... | collective-permute-start | bytes 1161224 | tf_op jit(solution)/shard_map/ppermute | solution.py:268
  131.3 0.0 copy-done.1
  131.3 0.0 copy-done.2
  131.3 1.1 combine.1
  132.4 20.4 %collective-permute-done.13.got = bf16[192,1008]{1,0:T(8,128)(2,1)S(1)} collective-permute-done((bf16[192,1008]{1,0:T(8,128)(2,1)}, bf16[192,1008]{1,0:T(8,128)(2,1)S(1)}, u32[]{:S(2)}, u32[]{:S(2)}) %collective-permute-start.13) | collective-permute-done | bytes 387104 | tf_op jit(solution)/shard_map/ppermute | solution.py:268
  152.7 1.1 finish.1
Async XLA Ops:
  2.7 10.7 %collective-permute-start = (bf16[40,3072]{1,0:T(8,128)(2,1)S(1)}, bf16[40,3072]{1,0:T(8,128)(2,1)S(1)}, u32[]{:S(2)}, u32[]{:S(2)}) collective-permute-start(bf16[40,3072]{1,0:T(8,128)(2,1)S(1)} %get-tuple-element.27), channel_id=1, source_target_pairs={{0,16},{16,32},{32,48},{48,0},{1,17},{17,33},{33,49},{49,1},{2,18}... | collective-permute-start | bytes 737288 | tf_op jit(solution)/shard_map/ppermute | solution.py:262
  5.2 21.0 %collective-permute-start.1 = (bf16[40,3072]{1,0:T(8,128)(2,1)S(1)}, bf16[40,3072]{1,0:T(8,128)(2,1)S(1)}, u32[]{:S(2)}, u32[]{:S(2)}) collective-permute-start(bf16[40,3072]{1,0:T(8,128)(2,1)S(1)} %get-tuple-element.28), channel_id=1, source_target_pairs={{0,32},{16,48},{32,0},{48,16},{1,33},{17,49},{33,1},{49,17},{2,34}... | collective-permute-start | bytes 737288 | tf_op jit(solution)/shard_map/ppermute | solution.py:262
  10.3 19.8 %collective-permute-start.2 = (bf16[40,3072]{1,0:T(8,128)(2,1)S(1)}, bf16[40,3072]{1,0:T(8,128)(2,1)S(1)}, u32[]{:S(2)}, u32[]{:S(2)}) collective-permute-start(bf16[40,3072]{1,0:T(8,128)(2,1)S(1)} %get-tuple-element.29), channel_id=1, source_target_pairs={{0,48},{16,0},{32,16},{48,32},{1,49},{17,1},{33,17},{49,33},{2,50}... | collective-permute-start | bytes 737288 | tf_op jit(solution)/shard_map/ppermute | solution.py:262
  32.3 18.4 %collective-permute-start.4 = (bf16[144,3072]{1,0:T(8,128)(2,1)S(1)}, bf16[144,3072]{1,0:T(8,128)(2,1)S(1)}, u32[]{:S(2)}, u32[]{:S(2)}) collective-permute-start(bf16[144,3072]{1,0:T(8,128)(2,1)S(1)} %get-tuple-element.31.mine), channel_id=1, source_target_pairs={{0,1},{1,0},{2,3},{3,2},{4,5},{5,4},{6,7},{7,6},{8,9},{9,8},{10,11... | collective-permute-start | bytes 2654216 | tf_op jit(solution)/shard_map/ppermute | solution.py:268
  34.2 46.0 %all-to-all-start = ((bf16[8,144,384]{2,1,0:T(8,128)(2,1)}), bf16[8,144,384]{2,1,0:T(8,128)(2,1)S(1)}, u32[]{:S(2)}, u32[]{:S(2)}) async-start(bf16[8,144,384]{2,1,0:T(8,128)(2,1)} %get-tuple-element.30), calls=%async_computation | async-start | bytes 1769472 | tf_op jit(solution)/shard_map/all_to_all | solution.py:309
  55.8 10.8 %copy-start = (bf16[144,1008]{1,0:T(8,128)(2,1)}, bf16[144,1008]{1,0:T(8,128)(2,1)S(1)}, u32[]{:S(2)}) copy-start(bf16[144,1008]{1,0:T(8,128)(2,1)S(1)} %expert_front.1.pieces.refs_0_) | copy-start | bytes 870916
  60.7 9.2 %collective-permute-start.10 = (bf16[8,144,384]{2,1,0:T(8,128)(2,1)S(1)}, bf16[8,144,384]{2,1,0:T(8,128)(2,1)S(1)}, u32[]{:S(2)}, u32[]{:S(2)}) collective-permute-start(bf16[8,144,384]{2,1,0:T(8,128)(2,1)S(1)} %get-tuple-element.33), channel_id=1, source_target_pairs={{0,1},{1,0},{2,3},{3,2},{4,5},{5,4},{6,7},{7,6},{8,9},{9,8},{10,11... | collective-permute-start | bytes 2654216 | tf_op jit(solution)/shard_map/ppermute | solution.py:268
  62.9 17.3 %collective-permute-start.5 = (bf16[144,1008]{1,0:T(8,128)(2,1)S(1)}, bf16[144,1008]{1,0:T(8,128)(2,1)S(1)}, u32[]{:S(2)}, u32[]{:S(2)}) collective-permute-start(bf16[144,1008]{1,0:T(8,128)(2,1)S(1)} %expert_front.1.pieces.refs_0_), channel_id=1, source_target_pairs={{0,64},{64,128},{128,192},{192,256},{256,320},{320,384},{384,448},... | collective-permute-start | bytes 870920 | tf_op jit(solution)/shard_map/ppermute | solution.py:256
  66.6 13.6 %collective-permute-start.6 = (bf16[144,1008]{1,0:T(8,128)(2,1)S(1)}, bf16[144,1008]{1,0:T(8,128)(2,1)S(1)}, u32[]{:S(2)}, u32[]{:S(2)}) collective-permute-start(bf16[144,1008]{1,0:T(8,128)(2,1)S(1)} %expert_front.1.pieces.refs_0_), channel_id=1, source_target_pairs={{0,448},{64,0},{128,64},{192,128},{256,192},{320,256},{384,320},{4... | collective-permute-start | bytes 870920 | tf_op jit(solution)/shard_map/ppermute | solution.py:256
  80.2 24.0 %copy-start.4 = (bf16[144,1008]{1,0:T(8,128)(2,1)}, bf16[144,1008]{1,0:T(8,128)(2,1)S(1)}, u32[]{:S(2)}) copy-start(bf16[144,1008]{1,0:T(8,128)(2,1)S(1)} %collective-permute-done.5.refs_1_) | copy-start | bytes 870916
  80.2 34.3 %copy-start.5 = (bf16[144,1008]{1,0:T(8,128)(2,1)}, bf16[144,1008]{1,0:T(8,128)(2,1)S(1)}, u32[]{:S(2)}) copy-start(bf16[144,1008]{1,0:T(8,128)(2,1)S(1)} %collective-permute-done.6.refs_2_) | copy-start | bytes 870916
  80.2 32.8 %all-to-all-start.1 = ((bf16[8,144,384]{2,1,0:T(8,128)(2,1)}), bf16[8,144,384]{2,1,0:T(8,128)(2,1)S(1)}, u32[]{:S(2)}, u32[]{:S(2)}) async-start(bf16[8,144,384]{2,1,0:T(8,128)(2,1)} %add_convert_fusion), calls=%async_computation.1 | async-start | bytes 1769472 | tf_op jit(solution)/shard_map/all_to_all | solution.py:331
  87.8 32.5 %collective-permute-start.3 = (bf16[8,144,384]{2,1,0:T(8,128)(2,1)S(1)}, bf16[8,144,384]{2,1,0:T(8,128)(2,1)S(1)}, u32[]{:S(2)}, u32[]{:S(2)}) collective-permute-start(bf16[8,144,384]{2,1,0:T(8,128)(2,1)S(1)} %all-to-all-done.mine), channel_id=1, source_target_pairs={{0,1},{1,0},{2,3},{3,2},{4,5},{5,4},{6,7},{7,6},{8,9},{9,8},{10,11... | collective-permute-start | bytes 2654216 | tf_op jit(solution)/shard_map/ppermute | solution.py:268
  89.7 12.5 %collective-permute-start.7 = (bf16[144,1008]{1,0:T(8,128)(2,1)S(1)}, bf16[144,1008]{1,0:T(8,128)(2,1)S(1)}, u32[]{:S(2)}, u32[]{:S(2)}) collective-permute-start(bf16[144,1008]{1,0:T(8,128)(2,1)S(1)} %collective-permute-done.5.refs_1_), channel_id=1, source_target_pairs={{0,64},{64,128},{128,192},{192,256},{256,320},{320,384},{384,448},... | collective-permute-start | bytes 870920 | tf_op jit(solution)/shard_map/ppermute | solution.py:256
  92.5 11.7 %collective-permute-start.8 = (bf16[144,1008]{1,0:T(8,128)(2,1)S(1)}, bf16[144,1008]{1,0:T(8,128)(2,1)}, u32[]{:S(2)}, u32[]{:S(2)}) collective-permute-start(bf16[144,1008]{1,0:T(8,128)(2,1)S(1)} %collective-permute-done.6.refs_2_), channel_id=1, source_target_pairs={{0,448},{64,0},{128,64},{192,128},{256,192},{320,256},{384,320},{4... | collective-permute-start | bytes 870920 | tf_op jit(solution)/shard_map/ppermute | solution.py:256
  102.3 12.2 %copy-start.6 = (bf16[144,1008]{1,0:T(8,128)(2,1)}, bf16[144,1008]{1,0:T(8,128)(2,1)S(1)}, u32[]{:S(2)}) copy-start(bf16[144,1008]{1,0:T(8,128)(2,1)S(1)} %collective-permute-done.7.refs_3_) | copy-start | bytes 870916
  102.3 12.2 %collective-permute-start.9 = (bf16[144,1008]{1,0:T(8,128)(2,1)S(1)}, bf16[144,1008]{1,0:T(8,128)(2,1)}, u32[]{:S(2)}, u32[]{:S(2)}) collective-permute-start(bf16[144,1008]{1,0:T(8,128)(2,1)S(1)} %collective-permute-done.7.refs_3_), channel_id=1, source_target_pairs={{0,64},{64,128},{128,192},{192,256},{256,320},{320,384},{384,448},... | collective-permute-start | bytes 870920 | tf_op jit(solution)/shard_map/ppermute | solution.py:256
  104.2 19.6 %collective-permute-start.11 = (bf16[144,1008]{1,0:T(8,128)(2,1)}, bf16[144,1008]{1,0:T(8,128)(2,1)S(1)}, u32[]{:S(2)}, u32[]{:S(2)}) collective-permute-start(bf16[144,1008]{1,0:T(8,128)(2,1)} %collective-permute-done.8.refs_4_), channel_id=1, source_target_pairs={{0,448},{64,0},{128,64},{192,128},{256,192},{320,256},{384,320},{4... | collective-permute-start | bytes 870920 | tf_op jit(solution)/shard_map/ppermute | solution.py:256
  114.5 12.2 %collective-permute-start.12 = (bf16[144,1008]{1,0:T(8,128)(2,1)}, bf16[144,1008]{1,0:T(8,128)(2,1)S(1)}, u32[]{:S(2)}, u32[]{:S(2)}) collective-permute-start(bf16[144,1008]{1,0:T(8,128)(2,1)} %collective-permute-done.9.refs_5_), channel_id=1, source_target_pairs={{0,64},{64,128},{128,192},{192,256},{256,320},{320,384},{384,448},... | collective-permute-start | bytes 870920 | tf_op jit(solution)/shard_map/ppermute | solution.py:256
  117.0 12.0 %all-to-all-start.2 = ((bf16[4,40,384]{2,1,0:T(8,128)(2,1)}), bf16[4,40,384]{2,1,0:T(8,128)(2,1)S(1)}, u32[]{:S(2)}, u32[]{:S(2)}) async-start(bf16[4,40,384]{2,1,0:T(8,128)(2,1)} %add_up.1), calls=%async_computation.2 | async-start | bytes 245760 | tf_op jit(solution)/shard_map/all_to_all | solution.py:335
  123.8 7.5 %copy-start.1 = (s32[64,2]{0,1:T(2,128)S(1)}, s32[64,2]{0,1:T(2,128)}, u32[]{:S(2)}) copy-start(s32[64,2]{0,1:T(2,128)} %param.9) | copy-start | bytes 1540
  123.8 7.5 %copy-start.2 = (f32[64,2]{0,1:T(2,128)S(1)}, f32[64,2]{0,1:T(2,128)}, u32[]{:S(2)}) copy-start(f32[64,2]{0,1:T(2,128)} %param.10) | copy-start | bytes 1540
  128.2 0.8 copy-start.3
  129.0 23.7 %collective-permute-start.13 = (bf16[192,1008]{1,0:T(8,128)(2,1)}, bf16[192,1008]{1,0:T(8,128)(2,1)S(1)}, u32[]{:S(2)}, u32[]{:S(2)}) collective-permute-start(bf16[192,1008]{1,0:T(8,128)(2,1)} %copy-done.3), channel_id=1, source_target_pairs={{0,512},{512,0},{1,513},{513,1},{2,514},{514,2},{3,515},{515,3},{4... | collective-permute-start | bytes 1161224 | tf_op jit(solution)/shard_map/ppermute | solution.py:268
